TPU v7x, 32 devices: a whole 2x2x4 slice. The times are simulated.
32 devices in a mesh: parts: 1, wide: 8 (over z, y), narrow: 4 (over x, core), sub: 1.
Axes of the slice: x: 2, y: 2, z: 4, core: 2. Of those that a mesh axis runs over, the one named last changes fastest.
Arguments:
- pair: bfloat16 [128, 128, 128], P(('parts', 'wide', 'narrow'), 'sub'), may hold values from -6 to 6
- valid: int32 [128], P('parts'), may hold values from 0 to 1, as said below
- norm_gain: float32 [128], replicated, may hold values from 0.5 to 1.5
- norm_bias: float32 [128], replicated, may hold values from -3 to 3
- w_proj: bfloat16 [128, 640], replicated, may hold values from -0.5 to 0.5
- out_gain: float32 [128], replicated, may hold values from 0.5 to 1.5
- out_bias: float32 [128], replicated, may hold values from -3 to 3
- w_out: bfloat16 [128, 128], replicated, may hold values from -0.5 to 0.5
Outputs:
- update: bfloat16 [128, 128, 128], P(('parts', 'wide', 'narrow'), 'sub')
Inputs may be any that keep to these rules, and one draw needn't show every extreme that they name: valid is 1 on a prefix of at least 64 positions and 0 after it.
All inputs are finite; a program needn't handle non-finite values.
Results may differ from a plain program's by a relative error of at most 0.012.
Values may be sent and summed in bfloat16 or wider, within the bound.
No kernel may reach another device: no remote copies, remote signals or barrier semaphores. Data moves between devices by JAX's collectives and lax.ppermute only.
A program may use at most 64 MiB of HBM per device.

v0:
```python
import jax
import jax.numpy as jnp
from jax import lax
from jax.sharding import PartitionSpec as P

epsilon = 1e-05


def layer_norm(values, gain_vec, bias_vec, axis_dim):
    average = jnp.mean(values, axis=axis_dim, keepdims=True)
    centered = values - average
    variance = jnp.mean(centered * centered, axis=axis_dim, keepdims=True)
    return centered * lax.rsqrt(variance + epsilon) * gain_vec + bias_vec


def local(pair, valid, norm_gain, norm_bias, w_proj, out_gain, out_bias, w_out):
    row_count, col_count, chan_count = pair.shape
    row_start = lax.axis_index(("wide", "narrow")) * row_count
    col_start = lax.axis_index("sub") * col_count
    row_flags = lax.dynamic_slice_in_dim(valid, row_start, row_count, 0).astype(jnp.float32)
    col_flags = lax.dynamic_slice_in_dim(valid, col_start, col_count, 0).astype(jnp.float32)
    pair_flags = row_flags[:, None] * col_flags[None, :]
    normed = layer_norm(pair.astype(jnp.float32), norm_gain, norm_bias, 2).astype(jnp.bfloat16)
    projected = jnp.einsum(
        "rkc,cd->drk", normed, w_proj[:, : 4 * chan_count], preferred_element_type=jnp.float32
    )
    left_side = (
        jax.nn.sigmoid(projected[:chan_count]) * projected[chan_count : 2 * chan_count] * pair_flags
    ).astype(jnp.bfloat16)
    right_side = (
        jax.nn.sigmoid(projected[2 * chan_count : 3 * chan_count])
        * projected[3 * chan_count :]
        * pair_flags
    ).astype(jnp.bfloat16)
    gate_values = jax.nn.sigmoid(
        jnp.einsum(
            "rkc,cd->rkd", normed, w_proj[:, 4 * chan_count :], preferred_element_type=jnp.float32
        )
    ).astype(jnp.bfloat16)
    left_group, right_group = (
        lax.all_to_all(left_side, ("wide", "narrow"), split_axis=0, concat_axis=1, tiled=True),
        lax.all_to_all(right_side, ("wide", "narrow"), split_axis=0, concat_axis=1, tiled=True),
    )
    partial_sums = jnp.einsum(
        "cik,cjk->cij", left_group, right_group, preferred_element_type=jnp.float32
    )
    summed = lax.psum_scatter(partial_sums, "sub", scatter_dimension=2, tiled=True).astype(
        jnp.bfloat16
    )
    returned = lax.all_to_all(summed, ("wide", "narrow"), split_axis=1, concat_axis=0, tiled=True)
    normed_out = layer_norm(
        returned.astype(jnp.float32), out_gain[:, None, None], out_bias[:, None, None], 0
    ).astype(jnp.bfloat16)
    result_out = jnp.einsum("crj,cd->rjd", normed_out, w_out, preferred_element_type=jnp.float32)
    return (gate_values.astype(jnp.float32) * result_out).astype(jnp.bfloat16)


def solution(mesh):
    in_specs = (
        P(("parts", "wide", "narrow"), "sub", None),
        P("parts"),
        P(),
        P(),
        P(),
        P(),
        P(),
        P(),
    )
    out_specs = P(("parts", "wide", "narrow"), "sub", None)
    return jax.shard_map(local, mesh=mesh, in_specs=in_specs, out_specs=out_specs, check_vma=False)
```

profile of v0, /device:TPU:0, one launch (start us, length us, event | category | flops | bytes accessed | tf_op | source)
XLA Modules:
  0.0 44.9 jit_solution(7185394692754604785)
XLA Ops:
  0.0 0.7 %convert_element_type.56 = f32[128]{0:T(128)S(1)} convert(s32[128]{0:T(128)} %param.9) | non-fusion elementwise | flops 128 | bytes 1024 | tf_op jit(solution)/shard_map/convert_element_type | solution.py:21
  0.7 0.7 %dynamic-slice_convert_fusion = f32[4]{0:T(128)S(1)} fusion(s32[128]{0:T(128)} %param.9, s32[]{:T(128)S(6)} %select_n.4), kind=kLoop, calls=%fused_computation.51 | loop fusion | flops 4 | bytes 36 | tf_op jit(solution)/shard_map/convert_element_type | solution.py:20
  1.4 1.0 %convert_reduce_fusion = f32[4,128]{1,0:T(4,128)S(1)} fusion(bf16[4,128,128]{2,1,0:T(8,128)(2,1)} %param.8), kind=kLoop, calls=%fused_computation.11 | loop fusion | flops 130560 | bytes 133120 | tf_op jit(solution)/shard_map/reduce_sum | solution.py:10
  2.5 0.2 fusion.8
  2.8 0.1 broadcast_multiply_fusion
  2.8 0.6 %copy-done.3 = f32[128]{0:T(128)S(1)} copy-done((f32[128]{0:T(128)S(1)}, f32[128]{0:T(128)}, u32[]{:S(2)}) %copy-start.3) | copy-done | bytes 536
  3.4 0.4 convolution_bitcast_fusion
  3.8 0.2 fusion.13
  3.9 0.8 %copy.18 = bf16[128,4,128]{2,1,0:T(4,128)(2,1)} copy(bf16[128,4,128]{0,2,1:T(8,128)(2,1)S(1)} %get-tuple-element.6) | data formatting | bytes 262144 | tf_op jit(solution)/shard_map/convert_element_type | solution.py:29
  4.7 7.3 %all-to-all-start = ((bf16[128,4,128]{2,1,0:T(4,128)(2,1)}), bf16[128,4,128]{2,1,0:T(4,128)(2,1)S(1)}, u32[]{:S(2)}, u32[]{:S(2)}) async-start(bf16[128,4,128]{2,1,0:T(4,128)(2,1)} %copy.18), calls=%async_computation | async-start | bytes 262144 | tf_op jit(solution)/shard_map/all_to_all | solution.py:41
  12.1 0.8 %copy.21 = bf16[128,4,128]{2,1,0:T(4,128)(2,1)} copy(bf16[128,4,128]{0,2,1:T(8,128)(2,1)S(1)} %get-tuple-element.5) | data formatting | bytes 262144 | tf_op jit(solution)/shard_map/convert_element_type | solution.py:34
  12.8 7.4 %all-to-all-done = bf16[128,4,128]{2,1,0:T(4,128)(2,1)S(1)} async-done(((bf16[128,4,128]{2,1,0:T(4,128)(2,1)}), bf16[128,4,128]{2,1,0:T(4,128)(2,1)S(1)}, u32[]{:S(2)}, u32[]{:S(2)}) %all-to-all-start) | async-done | bytes 131104 | tf_op jit(solution)/shard_map/all_to_all | solution.py:41
  20.3 2.6 %all-to-all-start.1 = ((bf16[128,4,128]{2,1,0:T(4,128)(2,1)}), bf16[128,4,128]{2,1,0:T(4,128)(2,1)S(1)}, u32[]{:S(2)}, u32[]{:S(2)}) async-start(bf16[128,4,128]{2,1,0:T(4,128)(2,1)} %copy.21), calls=%async_computation.1 | async-start | bytes 262144 | tf_op jit(solution)/shard_map/all_to_all | solution.py:42
  22.9 0.1 copy.20
  23.0 8.1 %all-to-all-done.1 = bf16[128,4,128]{2,1,0:T(4,128)(2,1)S(1)} async-done(((bf16[128,4,128]{2,1,0:T(4,128)(2,1)}), bf16[128,4,128]{2,1,0:T(4,128)(2,1)S(1)}, u32[]{:S(2)}, u32[]{:S(2)}) %all-to-all-start.1) | async-done | bytes 131104 | tf_op jit(solution)/shard_map/all_to_all | solution.py:42
  31.1 0.1 copy.23
  31.2 0.2 convolution_convert_fusion
  31.4 0.8 %copy.24 = bf16[4,128,128]{2,0,1:T(4,128)(2,1)} copy(bf16[4,128,128]{2,1,0:T(8,128)(2,1)S(1)} %convolution_convert_fusion) | data formatting | bytes 262144 | tf_op jit(solution)/shard_map/convert_element_type | solution.py:47
  32.2 2.6 %all-to-all-start.2 = ((bf16[4,128,128]{2,0,1:T(4,128)(2,1)}), bf16[4,128,128]{2,0,1:T(4,128)(2,1)S(1)}, u32[]{:S(2)}, u32[]{:S(2)}) async-start(bf16[4,128,128]{2,0,1:T(4,128)(2,1)} %copy.24), calls=%async_computation.2 | async-start | bytes 262144 | tf_op jit(solution)/shard_map/all_to_all | solution.py:50
  34.8 0.3 fusion.4
  35.1 7.9 %all-to-all-done.2 = bf16[4,128,128]{2,0,1:T(4,128)(2,1)S(1)} async-done(((bf16[4,128,128]{2,0,1:T(4,128)(2,1)}), bf16[4,128,128]{2,0,1:T(4,128)(2,1)S(1)}, u32[]{:S(2)}, u32[]{:S(2)}) %all-to-all-start.2) | async-done | bytes 131104 | tf_op jit(solution)/shard_map/all_to_all | solution.py:50
  43.1 0.1 fusion.23
  43.3 0.6 %copy-done.5 = f32[128]{0:T(128)S(1)} copy-done((f32[128]{0:T(128)S(1)}, f32[128]{0:T(128)}, u32[]{:S(2)}) %copy-start.5) | copy-done | bytes 536
  43.9 1.0 %fusion.5 = bf16[4,128,128]{2,1,0:T(8,128)(2,1)} fusion(f32[4,128,128]{2,1,0:T(8,128)S(1)} %fusion.4, f32[128,4,128]{2,0,1:T(8,128)S(1)} %bitcast.34, f32[128]{0:T(128)S(1)} %copy-done.5, f32[128]{0:T(128)S(1)} %copy-done.6, f32[4,128]{1,0:T(4,128)S(1)} %add_rsqrt_fusion, f32[4,128]{1,0:T(4,128)S(1)} %broadcast_multiply_fusion.1, ...), kind=kOutput, calls=%fused_computation.8 | convolution fusion | flops 17235968 | bytes 693248 | tf_op jit(solution)/shard_map/crj,cd->rjd/dot_general | solution.py:54
  (21 shorter events, 0.2 us)
Async XLA Ops:
  0.0 43.3 %copy-start = (bf16[128,128]{1,0:T(8,128)(2,1)S(1)}, bf16[128,128]{1,0:T(8,128)(2,1)}, u32[]{:S(2)}) copy-start(bf16[128,128]{1,0:T(8,128)(2,1)} %param.15) | copy-start | bytes 98308
  0.0 2.5 %copy-start.1 = (bf16[4,128,128]{2,1,0:T(8,128)(2,1)S(1)}, bf16[4,128,128]{2,1,0:T(8,128)(2,1)}, u32[]{:S(2)}) copy-start(bf16[4,128,128]{2,1,0:T(8,128)(2,1)} %param.8) | copy-start | bytes 393220
  0.0 2.8 %copy-start.2 = (bf16[128,640]{1,0:T(8,128)(2,1)S(1)}, bf16[128,640]{1,0:T(8,128)(2,1)}, u32[]{:S(2)}) copy-start(bf16[128,640]{1,0:T(8,128)(2,1)} %param.12) | copy-start | bytes 491524
  2.7 0.7 %copy-start.3 = (f32[128]{0:T(128)S(1)}, f32[128]{0:T(128)}, u32[]{:S(2)}) copy-start(f32[128]{0:T(128)} %param.11) | copy-start | bytes 1540
  2.7 0.7 %copy-start.4 = (f32[128]{0:T(128)S(1)}, f32[128]{0:T(128)}, u32[]{:S(2)}) copy-start(f32[128]{0:T(128)} %param.10) | copy-start | bytes 1540
  4.7 15.5 %all-to-all-start = ((bf16[128,4,128]{2,1,0:T(4,128)(2,1)}), bf16[128,4,128]{2,1,0:T(4,128)(2,1)S(1)}, u32[]{:S(2)}, u32[]{:S(2)}) async-start(bf16[128,4,128]{2,1,0:T(4,128)(2,1)} %copy.18), calls=%async_computation | async-start | bytes 262144 | tf_op jit(solution)/shard_map/all_to_all | solution.py:41
  20.3 10.8 %all-to-all-start.1 = ((bf16[128,4,128]{2,1,0:T(4,128)(2,1)}), bf16[128,4,128]{2,1,0:T(4,128)(2,1)S(1)}, u32[]{:S(2)}, u32[]{:S(2)}) async-start(bf16[128,4,128]{2,1,0:T(4,128)(2,1)} %copy.21), calls=%async_computation.1 | async-start | bytes 262144 | tf_op jit(solution)/shard_map/all_to_all | solution.py:42
  32.2 10.8 %all-to-all-start.2 = ((bf16[4,128,128]{2,0,1:T(4,128)(2,1)}), bf16[4,128,128]{2,0,1:T(4,128)(2,1)S(1)}, u32[]{:S(2)}, u32[]{:S(2)}) async-start(bf16[4,128,128]{2,0,1:T(4,128)(2,1)} %copy.24), calls=%async_computation.2 | async-start | bytes 262144 | tf_op jit(solution)/shard_map/all_to_all | solution.py:50
  43.2 0.7 %copy-start.5 = (f32[128]{0:T(128)S(1)}, f32[128]{0:T(128)}, u32[]{:S(2)}) copy-start(f32[128]{0:T(128)} %param.14) | copy-start | bytes 1540
  43.3 0.7 %copy-start.6 = (f32[128]{0:T(128)S(1)}, f32[128]{0:T(128)}, u32[]{:S(2)}) copy-start(f32[128]{0:T(128)} %param.13) | copy-start | bytes 1540
where the time goes:
time: 45.2 us; the launch traced here: 44.9 us
  waiting for transfers between devices  23.4 us (52%)
  starting transfers between devices  12.5 us (28%)
  local copies, waits for them, and re-layouts  3.87 us (9%)
  other arithmetic  3.11 us (7%)
  matrix products  1.85 us (4%)
    all_to_all x1, waiting for transfers between devices, local(): lax.all_to_all(right_side, ('wide', 'narrow'), split_axis=0, concat_axis=...  8.09 us
    all_to_all x1, waiting for transfers between devices, local(): lax.all_to_all(summed, ('wide', 'narrow'), split_axis=1, concat_axis=0, t...  7.89 us
    all_to_all x1, waiting for transfers between devices, local(): lax.all_to_all(left_side, ('wide', 'narrow'), split_axis=0, concat_axis=1...  7.45 us
    all_to_all x1, starting transfers between devices, local(): lax.all_to_all(left_side, ('wide', 'narrow'), split_axis=0, concat_axis=1...  7.31 us
    all_to_all x1, starting transfers between devices, local(): lax.all_to_all(summed, ('wide', 'narrow'), split_axis=1, concat_axis=0, t...  2.58 us
    all_to_all x1, starting transfers between devices, local(): lax.all_to_all(right_side, ('wide', 'narrow'), split_axis=0, concat_axis=...  2.57 us
    unnamed x14, local copies, waits for them, and re-layouts  1.25 us
    reduce_sum x2, other arithmetic, layer_norm(): average = jnp.mean(values, axis=axis_dim, keepdims=True)  1.07 us
  transfers between devices with their start and end apart: 3, of which 3 were waited for; matrix products, arithmetic and copies ran while one was open for 3% of the time, Pallas kernels for 0%

commit v1 on v0

--- a/solution.py
+++ b/solution.py
@@ -37,10 +37,11 @@
             "rkc,cd->rkd", normed, w_proj[:, 4 * chan_count :], preferred_element_type=jnp.float32
         )
     ).astype(jnp.bfloat16)
-    left_group, right_group = (
-        lax.all_to_all(left_side, ("wide", "narrow"), split_axis=0, concat_axis=1, tiled=True),
-        lax.all_to_all(right_side, ("wide", "narrow"), split_axis=0, concat_axis=1, tiled=True),
+    both_sides = jnp.stack([left_side, right_side], axis=1)
+    both_group = lax.all_to_all(
+        both_sides, ("wide", "narrow"), split_axis=0, concat_axis=2, tiled=True
     )
+    left_group, right_group = both_group[:, 0], both_group[:, 1]
     partial_sums = jnp.einsum(
         "cik,cjk->cij", left_group, right_group, preferred_element_type=jnp.float32
     )

time: 45.2 us -> 36 us (0.80)
  blocking collectives: 0 us -> 17.7 us
  waiting for transfers between devices: 23.4 us -> 7.89 us
  starting transfers between devices: 12.5 us -> 2.58 us
  local copies, waits for them, and re-layouts: 3.87 us -> 2.48 us
    all_to_all x0 -> x1, blocking collectives: none -> 17.7 us  [local(): lax.all_to_all(both_sides, ('wide', 'narrow'), split_axis=0, concat_axis=...]
    all_to_all x2 -> x0, waiting for transfers between devices: 15.5 us -> none  [the longest x1 8.09 us: local(): lax.all_to_all(right_side, ('wide', 'narrow'), split_axis=0, concat_axis=...]
    all_to_all x2 -> x0, starting transfers between devices: 9.88 us -> none  [the longest x1 7.31 us: local(): lax.all_to_all(left_side, ('wide', 'narrow'), split_axis=0, concat_axis=1...]
    convert_element_type x2 -> x0, local copies, waits for them, and re-layouts: 1.57 us -> none  [the longest x1 0.79 us: local(): left_side = (jax.nn.sigmoid(projected[:chan_count]) * projected[chan_coun...]
  transfers between devices with their start and end apart: 3 -> 1, of which waited for: 3 -> 1; matrix products, arithmetic and copies ran while one was open for 3% -> 1% of each run, Pallas kernels for 0% -> 0%
where the time goes in v1:
time: 36 us; the launch traced here: 35.8 us
  blocking collectives  17.7 us (49%)
  waiting for transfers between devices  7.89 us (22%)
  other arithmetic  3.14 us (9%)
  starting transfers between devices  2.58 us (7%)
  local copies, waits for them, and re-layouts  2.48 us (7%)
  matrix products  1.85 us (5%)
    all_to_all x1, blocking collectives, local(): lax.all_to_all(both_sides, ('wide', 'narrow'), split_axis=0, concat_axis=...  17.7 us
    all_to_all x1, waiting for transfers between devices, local(): lax.all_to_all(summed, ('wide', 'narrow'), split_axis=1, concat_axis=0, t...  7.89 us
    all_to_all x1, starting transfers between devices, local(): lax.all_to_all(summed, ('wide', 'narrow'), split_axis=1, concat_axis=0, t...  2.58 us
    unnamed x14, local copies, waits for them, and re-layouts  1.25 us
    reduce_sum x2, other arithmetic, layer_norm(): average = jnp.mean(values, axis=axis_dim, keepdims=True)  1.07 us
    dot_general x1, matrix products, local(): jnp.einsum('crj,cd->rjd', normed_out, w_out, preferred_element_type=jnp.f...  0.96 us
    convert_element_type x1, local copies, waits for them, and re-layouts, local(): lax.psum_scatter(partial_sums, 'sub', scatter_dimension=2, tiled=True)  0.76 us
    convert_element_type x1, other arithmetic, local(): lax.dynamic_slice_in_dim(valid, row_start, row_count, 0).astype(jnp.float32)  0.73 us
  transfers between devices with their start and end apart: 1, of which 1 were waited for; matrix products, arithmetic and copies ran while one was open for 1% of the time, Pallas kernels for 0%

profile of v1, /device:TPU:0, one launch (start us, length us, event | category | flops | bytes accessed | tf_op | source)
XLA Modules:
  0.0 35.8 jit_solution(14301553841279045867)
XLA Ops:
  0.0 0.7 %convert_element_type.56 = f32[128]{0:T(128)S(1)} convert(s32[128]{0:T(128)} %param.9) | non-fusion elementwise | flops 128 | bytes 1024 | tf_op jit(solution)/shard_map/convert_element_type | solution.py:21
  0.7 0.7 %dynamic-slice_convert_fusion = f32[4]{0:T(128)S(1)} fusion(s32[128]{0:T(128)} %param.9, s32[]{:T(128)S(6)} %select_n.4), kind=kLoop, calls=%fused_computation.56 | loop fusion | flops 4 | bytes 36 | tf_op jit(solution)/shard_map/convert_element_type | solution.py:20
  1.4 1.0 %convert_reduce_fusion = f32[4,128]{1,0:T(4,128)S(1)} fusion(bf16[4,128,128]{2,1,0:T(8,128)(2,1)} %param.8), kind=kLoop, calls=%fused_computation.11 | loop fusion | flops 130560 | bytes 133120 | tf_op jit(solution)/shard_map/reduce_sum | solution.py:10
  2.5 0.2 fusion.8
  2.7 0.0 copy-start.3
  2.7 0.0 copy-start.4
  2.8 0.1 broadcast_multiply_fusion
  2.8 0.6 %copy-done.3 = f32[128]{0:T(128)S(1)} copy-done((f32[128]{0:T(128)S(1)}, f32[128]{0:T(128)}, u32[]{:S(2)}) %copy-start.3) | copy-done | bytes 536
  3.4 0.0 copy-done.4
  3.4 0.4 convolution_bitcast_fusion
  3.8 0.2 fusion.30
  4.0 0.2 copy.15
  4.2 17.7 %all_to_all.27 = bf16[128,2,4,128]{3,2,1,0:T(4,128)(2,1)S(1)} all-to-all(bf16[128,2,4,128]{3,2,1,0:T(4,128)(2,1)S(1)} %copy.15), channel_id=1, replica_groups=mesh['parts'=1,'wide'=8,'narrow'=4,'sub'=1] {'wide','narrow'}, dimensions={0} | all-to-all | bytes 524288 | tf_op jit(solution)/shard_map/all_to_all | solution.py:41
  21.9 0.2 copy.17
  22.1 0.2 convolution_convert_fusion
  22.4 0.8 %copy.18 = bf16[4,128,128]{2,0,1:T(4,128)(2,1)} copy(bf16[4,128,128]{2,1,0:T(8,128)(2,1)S(1)} %convolution_convert_fusion) | data formatting | bytes 262144 | tf_op jit(solution)/shard_map/convert_element_type | solution.py:48
  23.1 2.6 %all-to-all-start.1 = ((bf16[4,128,128]{2,0,1:T(4,128)(2,1)}), bf16[4,128,128]{2,0,1:T(4,128)(2,1)S(1)}, u32[]{:S(2)}, u32[]{:S(2)}) async-start(bf16[4,128,128]{2,0,1:T(4,128)(2,1)} %copy.18), calls=%async_computation.1 | async-start | bytes 262144 | tf_op jit(solution)/shard_map/all_to_all | solution.py:51
  25.7 0.3 fusion.4
  26.0 7.9 %all-to-all-done.1 = bf16[4,128,128]{2,0,1:T(4,128)(2,1)S(1)} async-done(((bf16[4,128,128]{2,0,1:T(4,128)(2,1)}), bf16[4,128,128]{2,0,1:T(4,128)(2,1)S(1)}, u32[]{:S(2)}, u32[]{:S(2)}) %all-to-all-start.1) | async-done | bytes 131104 | tf_op jit(solution)/shard_map/all_to_all | solution.py:51
  34.0 0.1 bitcast_reduce_fusion
  34.0 0.1 fusion.23
  34.2 0.6 %copy-done.5 = f32[128]{0:T(128)S(1)} copy-done((f32[128]{0:T(128)S(1)}, f32[128]{0:T(128)}, u32[]{:S(2)}) %copy-start.5) | copy-done | bytes 536
  34.8 0.0 copy-done.6
  34.8 1.0 %fusion.5 = bf16[4,128,128]{2,1,0:T(8,128)(2,1)} fusion(f32[4,128,128]{2,1,0:T(8,128)S(1)} %fusion.4, f32[128,4,128]{2,0,1:T(8,128)S(1)} %bitcast.38, f32[128]{0:T(128)S(1)} %copy-done.5, f32[128]{0:T(128)S(1)} %copy-done.6, f32[4,128]{1,0:T(4,128)S(1)} %add_rsqrt_fusion, f32[4,128]{1,0:T(4,128)S(1)} %broadcast_multiply_fusion.1, ...), kind=kOutput, calls=%fused_computation.8 | convolution fusion | flops 17235968 | bytes 693248 | tf_op jit(solution)/shard_map/crj,cd->rjd/dot_general | solution.py:55
  (16 shorter events, 0.2 us)
Async XLA Ops:
  0.0 34.2 %copy-start = (bf16[128,128]{1,0:T(8,128)(2,1)S(1)}, bf16[128,128]{1,0:T(8,128)(2,1)}, u32[]{:S(2)}) copy-start(bf16[128,128]{1,0:T(8,128)(2,1)} %param.15) | copy-start | bytes 98308
  0.0 2.5 %copy-start.1 = (bf16[4,128,128]{2,1,0:T(8,128)(2,1)S(1)}, bf16[4,128,128]{2,1,0:T(8,128)(2,1)}, u32[]{:S(2)}) copy-start(bf16[4,128,128]{2,1,0:T(8,128)(2,1)} %param.8) | copy-start | bytes 393220
  0.0 2.8 %copy-start.2 = (bf16[128,640]{1,0:T(8,128)(2,1)S(1)}, bf16[128,640]{1,0:T(8,128)(2,1)}, u32[]{:S(2)}) copy-start(bf16[128,640]{1,0:T(8,128)(2,1)} %param.12) | copy-start | bytes 491524
  2.7 0.7 %copy-start.3 = (f32[128]{0:T(128)S(1)}, f32[128]{0:T(128)}, u32[]{:S(2)}) copy-start(f32[128]{0:T(128)} %param.11) | copy-start | bytes 1540
  2.7 0.7 %copy-start.4 = (f32[128]{0:T(128)S(1)}, f32[128]{0:T(128)}, u32[]{:S(2)}) copy-start(f32[128]{0:T(128)} %param.10) | copy-start | bytes 1540
  23.1 10.8 %all-to-all-start.1 = ((bf16[4,128,128]{2,0,1:T(4,128)(2,1)}), bf16[4,128,128]{2,0,1:T(4,128)(2,1)S(1)}, u32[]{:S(2)}, u32[]{:S(2)}) async-start(bf16[4,128,128]{2,0,1:T(4,128)(2,1)} %copy.18), calls=%async_computation.1 | async-start | bytes 262144 | tf_op jit(solution)/shard_map/all_to_all | solution.py:51
  34.2 0.7 %copy-start.5 = (f32[128]{0:T(128)S(1)}, f32[128]{0:T(128)}, u32[]{:S(2)}) copy-start(f32[128]{0:T(128)} %param.14) | copy-start | bytes 1540
  34.2 0.7 %copy-start.6 = (f32[128]{0:T(128)S(1)}, f32[128]{0:T(128)}, u32[]{:S(2)}) copy-start(f32[128]{0:T(128)} %param.13) | copy-start | bytes 1540

commit v2 on v1

--- a/solution.py
+++ b/solution.py
@@ -1,9 +1,14 @@
+import functools
+
 import jax
 import jax.numpy as jnp
 from jax import lax
+from jax.experimental import pallas as pl
+from jax.experimental.pallas import tpu as pltpu
 from jax.sharding import PartitionSpec as P
 
 epsilon = 1e-05
+axes = ("wide", "narrow")
 
 
 def layer_norm(values, gain_vec, bias_vec, axis_dim):
@@ -13,7 +18,134 @@
     return centered * lax.rsqrt(variance + epsilon) * gain_vec + bias_vec
 
 
-def local(pair, valid, norm_gain, norm_bias, w_proj, out_gain, out_bias, w_out):
+def swap_halves(low, high):
+    first = lax.broadcasted_iota(jnp.int32, low.shape, 0) < 4
+    return (
+        jnp.where(first, low, pltpu.roll(high, 4, 0)),
+        jnp.where(first, pltpu.roll(low, 4, 0), high),
+    )
+
+
+def project_kernel(flags_ref, valid_ref, pair_ref, gain_ref, bias_ref, w_ref, out_ref, normed_ref):
+    row_count, col_count, chan_count = pair_ref.shape
+    row_start = lax.axis_index(axes) * row_count
+    tokens = pair_ref[...].reshape(row_count * col_count, chan_count).astype(jnp.float32)
+    normed = layer_norm(tokens, gain_ref[...], bias_ref[...], 1).astype(jnp.bfloat16)
+    normed_ref[...] = normed
+    projected = lax.dot_general(
+        w_ref[:, : 4 * chan_count], normed, (((0,), (1,)), ((), ())),
+        preferred_element_type=jnp.float32,
+    )
+    col_flags = valid_ref[...].astype(jnp.float32)
+    flags = jnp.concatenate(
+        [col_flags * flags_ref[row_start + r].astype(jnp.float32) for r in range(row_count)], axis=1
+    )
+    for chan in range(0, chan_count, 8):
+        a_gate, a, b_gate, b = (
+            projected[i * chan_count + chan : i * chan_count + chan + 8] for i in range(4)
+        )
+        left = jax.nn.sigmoid(a_gate) * a * flags
+        right = jax.nn.sigmoid(b_gate) * b * flags
+        for half, block in enumerate(swap_halves(left, right)):
+            for r in range(0, row_count, 2):
+                rows = jnp.concatenate(
+                    [block[:, (r + i) * col_count : (r + i + 1) * col_count] for i in range(2)], axis=0
+                )
+                out_ref[chan // 4 + half, r * 8 : (r + 2) * 8, :] = rows.astype(jnp.bfloat16)
+
+
+def contract_kernel(blocks_ref, out_ref, held_ref):
+    shards, block_rows, cols = blocks_ref.shape
+    total = held_ref.shape[0] // 8
+    held_ref[...] = blocks_ref[...].reshape(shards * block_rows, cols).astype(jnp.float32)
+    products = []
+    for c in range(4):
+        left = held_ref[pl.ds(c, total, stride=8), :].astype(jnp.bfloat16)
+        right = held_ref[pl.ds(4 + c, total, stride=8), :].astype(jnp.bfloat16)
+        products.append(
+            lax.dot_general(
+                left, right, (((1,), (1,)), ((), ())), preferred_element_type=jnp.float32
+            )
+        )
+    for row in range(0, total, 8):
+        pieces = [product[row : row + 8] for product in products]
+        low, high = swap_halves(pieces[0], pieces[1]), swap_halves(pieces[2], pieces[3])
+        for half in range(2):
+            rows = jnp.concatenate([low[half], high[half]], axis=0)
+            out_ref[row // 4 + half] = rows.astype(jnp.bfloat16)
+
+
+def gate_kernel(normed_ref, w_ref, out_ref):
+    chan_count = normed_ref.shape[1]
+    projected = jnp.dot(
+        normed_ref[...], w_ref[:, 4 * chan_count :], preferred_element_type=jnp.float32
+    )
+    out_ref[...] = jax.nn.sigmoid(projected).astype(jnp.bfloat16)
+
+
+def finish_kernel(blocks_ref, gate_ref, gain_ref, bias_ref, w_ref, out_ref, held_ref):
+    row_count, col_count, chan_count = out_ref.shape
+    held_ref[...] = blocks_ref[...].reshape(held_ref.shape).astype(jnp.float32)
+    gain = jnp.transpose(jnp.broadcast_to(gain_ref[...], (col_count, chan_count)))
+    bias = jnp.transpose(jnp.broadcast_to(bias_ref[...], (col_count, chan_count)))
+    for r in range(row_count):
+        triangle = held_ref[pl.ds(r, chan_count, stride=row_count), :]
+        normed = layer_norm(triangle, gain, bias, 0).astype(jnp.bfloat16)
+        result = lax.dot_general(
+            normed, w_ref[...], (((0,), (0,)), ((), ())), preferred_element_type=jnp.float32
+        )
+        gate = gate_ref[r * col_count : (r + 1) * col_count, :].astype(jnp.float32)
+        out_ref[r] = (gate * result).astype(jnp.bfloat16)
+
+
+def local_blocks(pair, valid, norm_gain, norm_bias, w_proj, out_gain, out_bias, w_out):
+    row_count, col_count, chan_count = pair.shape
+    shards = lax.axis_size(axes)
+    tokens = row_count * col_count
+    vmem = pl.BlockSpec(memory_space=pltpu.VMEM)
+    smem = pl.BlockSpec(memory_space=pltpu.SMEM)
+
+    def line(vector):
+        return vector.reshape(1, -1)
+
+    def shaped(*dims):
+        return jax.ShapeDtypeStruct(dims, jnp.bfloat16)
+
+    sides, normed = pl.pallas_call(
+        project_kernel,
+        out_shape=(shaped(shards, 8 * row_count, col_count), shaped(tokens, chan_count)),
+        in_specs=[smem] + [vmem] * 5,
+        out_specs=(vmem, vmem),
+        name="project",
+    )(valid, line(valid), pair, line(norm_gain), line(norm_bias), w_proj)
+    sides = lax.all_to_all(sides, axes, split_axis=0, concat_axis=0, tiled=True)
+    triangle = pl.pallas_call(
+        contract_kernel,
+        out_shape=shaped(shards, 4 * row_count, col_count),
+        in_specs=[vmem],
+        out_specs=vmem,
+        scratch_shapes=[pltpu.VMEM((8 * col_count, col_count), jnp.float32)],
+        name="contract",
+    )(sides)
+    triangle = lax.all_to_all(triangle, axes, split_axis=0, concat_axis=0, tiled=True)
+    gate_values = pl.pallas_call(
+        gate_kernel,
+        out_shape=shaped(tokens, chan_count),
+        in_specs=[vmem] * 2,
+        out_specs=vmem,
+        name="gate",
+    )(normed, w_proj)
+    return pl.pallas_call(
+        finish_kernel,
+        out_shape=shaped(row_count, col_count, chan_count),
+        in_specs=[vmem] * 5,
+        out_specs=vmem,
+        scratch_shapes=[pltpu.VMEM((tokens, chan_count), jnp.float32)],
+        name="finish",
+    )(triangle, gate_values, line(out_gain), line(out_bias), w_out)
+
+
+def local_arrays(pair, valid, norm_gain, norm_bias, w_proj, out_gain, out_bias, w_out):
     row_count, col_count, chan_count = pair.shape
     row_start = lax.axis_index(("wide", "narrow")) * row_count
     col_start = lax.axis_index("sub") * col_count
@@ -56,6 +188,18 @@
     return (gate_values.astype(jnp.float32) * result_out).astype(jnp.bfloat16)
 
 
+def local(pair, *rest):
+    row_count, col_count, chan_count = pair.shape
+    shards = lax.axis_size(axes)
+    fits = (
+        lax.axis_size("sub") == 1
+        and (row_count, col_count, chan_count) == (4, 128, 128)
+        and shards * row_count == col_count
+        and shards * 4 == chan_count
+    )
+    return (local_blocks if fits else local_arrays)(pair, *rest)
+
+
 def solution(mesh):
     in_specs = (
         P(("parts", "wide", "narrow"), "sub", None),

time: 36 us -> 35.8 us (level)
  Pallas kernels: 0 us -> 7.86 us
  other arithmetic: 3.14 us -> 0 us
  matrix products: 1.85 us -> 0 us
  local copies, waits for them, and re-layouts: 2.48 us -> 0.64 us
  waiting for transfers between devices: 7.89 us -> 6.42 us
    pallas_call x0 -> x4, Pallas kernels: none -> 7.86 us  [the longest x1 2.27 us: local_blocks(): pl.pallas_call(project_kernel, out_shape=(shaped(shards, 8 * row_count, c...]
    dot_general x4 -> x0, matrix products: 1.85 us -> none  [the longest x1 0.96 us: local(): jnp.einsum('crj,cd->rjd', normed_out, w_out, preferred_element_type=jnp.f...]
    all_to_all x1, waiting for transfers between devices: 7.89 us -> 6.42 us  [local_blocks(): lax.all_to_all(triangle, axes, split_axis=0, concat_axis=0, tiled=True)]
    convert_element_type x3 -> x0, other arithmetic: 1.45 us -> none  [the longest x1 0.73 us: local(): lax.dynamic_slice_in_dim(valid, row_start, row_count, 0).astype(jnp.float32)]
    reduce_sum x4 -> x0, other arithmetic: 1.39 us -> none  [the longest x2 1.07 us: layer_norm(): average = jnp.mean(values, axis=axis_dim, keepdims=True)]
    convert_element_type x2 -> x0, local copies, waits for them, and re-layouts: 0.8 us -> none  [the longest x1 0.76 us: local(): lax.psum_scatter(partial_sums, 'sub', scatter_dimension=2, tiled=True)]
    unnamed x14 -> x2, local copies, waits for them, and re-layouts: 1.25 us -> 0.64 us
  transfers between devices with their start and end apart: 1 -> 1, of which waited for: 1 -> 1; matrix products, arithmetic and copies ran while one was open for 1% -> 0% of each run, Pallas kernels for 0% -> 5%
where the time goes in v2:
time: 35.8 us; the launch traced here: 35.5 us
  blocking collectives  18 us (50%)
  Pallas kernels  7.86 us (22%)
  waiting for transfers between devices  6.42 us (18%)
  starting transfers between devices  2.56 us (7%)
  local copies, waits for them, and re-layouts  0.64 us (2%)
    all_to_all x1, blocking collectives, local_blocks(): sides = lax.all_to_all(sides, axes, split_axis=0, concat_axis=0, tiled=True)  18 us
    all_to_all x1, waiting for transfers between devices, local_blocks(): lax.all_to_all(triangle, axes, split_axis=0, concat_axis=0, tiled=True)  6.42 us
    all_to_all x1, starting transfers between devices, local_blocks(): lax.all_to_all(triangle, axes, split_axis=0, concat_axis=0, tiled=True)  2.56 us
    pallas_call x1, Pallas kernels, local_blocks(): pl.pallas_call(project_kernel, out_shape=(shaped(shards, 8 * row_count, c...  2.27 us
    pallas_call x1, Pallas kernels, local_blocks(): pl.pallas_call(finish_kernel, out_shape=shaped(row_count, col_count, chan...  1.95 us
    pallas_call x1, Pallas kernels, local_blocks(): pl.pallas_call(contract_kernel, out_shape=shaped(shards, 4 * row_count, c...  1.83 us
    pallas_call x1, Pallas kernels, local_blocks(): pl.pallas_call(gate_kernel, out_shape=shaped(tokens, chan_count), in_spec...  1.81 us
  transfers between devices with their start and end apart: 1, of which 1 were waited for; matrix products, arithmetic and copies ran while one was open for 0% of the time, Pallas kernels for 5%

profile of v2, /device:TPU:0, one launch (start us, length us, event | category | flops | bytes accessed | tf_op | source)
XLA Modules:
  0.0 35.5 jit_solution(6377734873521194593)
XLA Ops:
  0.0 2.3 %project.1 = (bf16[32,32,128]{2,1,0:T(8,128)(2,1)}, bf16[512,128]{1,0:T(8,128)(2,1)}) custom-call(s32[128]{0:T(128)} %flags_ref.1, s32[1,128]{1,0:T(1,128)} %bitcast.5, bf16[4,128,128]{2,1,0:T(8,128)(2,1)} %pair_ref.1, f32[1,128]{1,0:T(1,128)} %bitcast.6, f32[1,128]{1,0:T(1,128)} %bitcast.7, bf16[128,640]{1,0:T(8,128)(2,1)} %w_ref.4), custom_call_target="tpu_custom_call" | custom-call | tf_op jit(solution)/shard_map/project/pallas_call | solution.py:114
  2.3 18.0 %all_to_all.10.blocks_ref = bf16[32,32,128]{2,1,0:T(8,128)(2,1)} all-to-all(bf16[32,32,128]{2,1,0:T(8,128)(2,1)} %get-tuple-element.7), channel_id=1, replica_groups=mesh['parts'=1,'wide'=8,'narrow'=4,'sub'=1] {'wide','narrow'}, dimensions={0} | all-to-all | bytes 524288 | tf_op jit(solution)/shard_map/all_to_all | solution.py:121
  20.3 1.8 %contract.1 = bf16[32,16,128]{2,1,0:T(8,128)(2,1)} custom-call(bf16[32,32,128]{2,1,0:T(8,128)(2,1)} %all_to_all.10.blocks_ref), custom_call_target="tpu_custom_call" | custom-call | tf_op jit(solution)/shard_map/contract/pallas_call | solution.py:122
  22.1 2.6 %all-to-all-start.1 = ((bf16[32,16,128]{2,1,0:T(8,128)(2,1)}), bf16[32,16,128]{2,1,0:T(8,128)(2,1)S(1)}, u32[]{:S(2)}, u32[]{:S(2)}) async-start(bf16[32,16,128]{2,1,0:T(8,128)(2,1)} %contract.1), calls=%async_computation.1 | async-start | bytes 262144 | tf_op jit(solution)/shard_map/all_to_all | solution.py:130
  24.7 1.8 %gate.1.gate_ref = bf16[512,128]{1,0:T(8,128)(2,1)} custom-call(bf16[512,128]{1,0:T(8,128)(2,1)} %get-tuple-element.8.normed_ref, bf16[128,640]{1,0:T(8,128)(2,1)} %w_ref.4), custom_call_target="tpu_custom_call" | custom-call | tf_op jit(solution)/shard_map/gate/pallas_call | solution.py:131
  26.5 6.4 %all-to-all-done.1.blocks_ref = bf16[32,16,128]{2,1,0:T(8,128)(2,1)S(1)} async-done(((bf16[32,16,128]{2,1,0:T(8,128)(2,1)}), bf16[32,16,128]{2,1,0:T(8,128)(2,1)S(1)}, u32[]{:S(2)}, u32[]{:S(2)}) %all-to-all-start.1) | async-done | bytes 131104 | tf_op jit(solution)/shard_map/all_to_all | solution.py:130
  32.9 0.0 copy-start
  32.9 0.6 %copy-done = bf16[32,16,128]{2,1,0:T(8,128)(2,1)} copy-done((bf16[32,16,128]{2,1,0:T(8,128)(2,1)}, bf16[32,16,128]{2,1,0:T(8,128)(2,1)S(1)}, u32[]{:S(2)}) %copy-start) | copy-done | bytes 131096
  33.5 1.9 %finish.1 = bf16[4,128,128]{2,1,0:T(8,128)(2,1)} custom-call(bf16[32,16,128]{2,1,0:T(8,128)(2,1)} %copy-done, bf16[512,128]{1,0:T(8,128)(2,1)} %gate.1.gate_ref, f32[1,128]{1,0:T(1,128)} %bitcast.8, f32[1,128]{1,0:T(1,128)} %bitcast.9, bf16[128,128]{1,0:T(8,128)(2,1)} %w_ref.5), custom_call_target="tpu_custom_call" | custom-call | tf_op jit(solution)/shard_map/finish/pallas_call | solution.py:138
Async XLA Ops:
  22.1 10.8 %all-to-all-start.1 = ((bf16[32,16,128]{2,1,0:T(8,128)(2,1)}), bf16[32,16,128]{2,1,0:T(8,128)(2,1)S(1)}, u32[]{:S(2)}, u32[]{:S(2)}) async-start(bf16[32,16,128]{2,1,0:T(8,128)(2,1)} %contract.1), calls=%async_computation.1 | async-start | bytes 262144 | tf_op jit(solution)/shard_map/all_to_all | solution.py:130
  32.9 0.6 %copy-start = (bf16[32,16,128]{2,1,0:T(8,128)(2,1)}, bf16[32,16,128]{2,1,0:T(8,128)(2,1)S(1)}, u32[]{:S(2)}) copy-start(bf16[32,16,128]{2,1,0:T(8,128)(2,1)S(1)} %all-to-all-done.1.blocks_ref) | copy-start | bytes 393220

commit v3 on v2

--- a/solution.py
+++ b/solution.py
@@ -26,7 +26,23 @@
     )
 
 
-def project_kernel(flags_ref, valid_ref, pair_ref, gain_ref, bias_ref, w_ref, out_ref, normed_ref):
+def send_blocks(held_ref, out_refs):
+    me = lax.axis_index(axes)
+    for s, out_ref in enumerate(out_refs):
+        out_ref[...] = held_ref[me ^ s]
+
+
+def receive_blocks(block_refs, held_ref):
+    me = lax.axis_index(axes)
+    rows = block_refs[0].shape[0]
+    for s, block_ref in enumerate(block_refs):
+        held_ref[pl.ds(pl.multiple_of((me ^ s) * rows, rows), rows), :] = block_ref[...].astype(
+            jnp.float32
+        )
+
+
+def project_kernel(flags_ref, valid_ref, pair_ref, gain_ref, bias_ref, w_ref, normed_ref, *rest):
+    out_refs, out_ref = rest[:-1], rest[-1]
     row_count, col_count, chan_count = pair_ref.shape
     row_start = lax.axis_index(axes) * row_count
     tokens = pair_ref[...].reshape(row_count * col_count, chan_count).astype(jnp.float32)
@@ -52,12 +68,13 @@
                     [block[:, (r + i) * col_count : (r + i + 1) * col_count] for i in range(2)], axis=0
                 )
                 out_ref[chan // 4 + half, r * 8 : (r + 2) * 8, :] = rows.astype(jnp.bfloat16)
-
-
-def contract_kernel(blocks_ref, out_ref, held_ref):
-    shards, block_rows, cols = blocks_ref.shape
+    send_blocks(out_ref, out_refs)
+
+
+def contract_kernel(shards, *refs):
+    block_refs, out_refs, (held_ref, out_ref) = refs[:shards], refs[shards : 2 * shards], refs[2 * shards :]
     total = held_ref.shape[0] // 8
-    held_ref[...] = blocks_ref[...].reshape(shards * block_rows, cols).astype(jnp.float32)
+    receive_blocks(block_refs, held_ref)
     products = []
     for c in range(4):
         left = held_ref[pl.ds(c, total, stride=8), :].astype(jnp.bfloat16)
@@ -73,6 +90,7 @@
         for half in range(2):
             rows = jnp.concatenate([low[half], high[half]], axis=0)
             out_ref[row // 4 + half] = rows.astype(jnp.bfloat16)
+    send_blocks(out_ref, out_refs)
 
 
 def gate_kernel(normed_ref, w_ref, out_ref):
@@ -83,9 +101,10 @@
     out_ref[...] = jax.nn.sigmoid(projected).astype(jnp.bfloat16)
 
 
-def finish_kernel(blocks_ref, gate_ref, gain_ref, bias_ref, w_ref, out_ref, held_ref):
+def finish_kernel(gate_ref, gain_ref, bias_ref, w_ref, *rest):
+    block_refs, out_ref, held_ref = rest[:-2], rest[-2], rest[-1]
     row_count, col_count, chan_count = out_ref.shape
-    held_ref[...] = blocks_ref[...].reshape(held_ref.shape).astype(jnp.float32)
+    receive_blocks(block_refs, held_ref)
     gain = jnp.transpose(jnp.broadcast_to(gain_ref[...], (col_count, chan_count)))
     bias = jnp.transpose(jnp.broadcast_to(bias_ref[...], (col_count, chan_count)))
     for r in range(row_count):
@@ -98,6 +117,14 @@
         out_ref[r] = (gate * result).astype(jnp.bfloat16)
 
 
+def exchange(blocks):
+    shards = len(blocks)
+    return [
+        lax.ppermute(block, axes, [(i, i ^ s) for i in range(shards)]) if s else block
+        for s, block in enumerate(blocks)
+    ]
+
+
 def local_blocks(pair, valid, norm_gain, norm_bias, w_proj, out_gain, out_bias, w_out):
     row_count, col_count, chan_count = pair.shape
     shards = lax.axis_size(axes)
@@ -111,23 +138,30 @@
     def shaped(*dims):
         return jax.ShapeDtypeStruct(dims, jnp.bfloat16)
 
-    sides, normed = pl.pallas_call(
+    side_block = shaped(8 * row_count, col_count)
+    triangle_block = shaped(4 * row_count, col_count)
+
+    def held(block, dtype):
+        dims = block.shape if dtype == jnp.bfloat16 else (shards * block.shape[0],) + block.shape[1:]
+        return pltpu.VMEM((shards,) + dims if dtype == jnp.bfloat16 else dims, dtype)
+
+    normed, *sides = pl.pallas_call(
         project_kernel,
-        out_shape=(shaped(shards, 8 * row_count, col_count), shaped(tokens, chan_count)),
+        out_shape=[shaped(tokens, chan_count)] + [side_block] * shards,
         in_specs=[smem] + [vmem] * 5,
-        out_specs=(vmem, vmem),
+        out_specs=[vmem] * (shards + 1),
+        scratch_shapes=[held(side_block, jnp.bfloat16)],
         name="project",
     )(valid, line(valid), pair, line(norm_gain), line(norm_bias), w_proj)
-    sides = lax.all_to_all(sides, axes, split_axis=0, concat_axis=0, tiled=True)
     triangle = pl.pallas_call(
-        contract_kernel,
-        out_shape=shaped(shards, 4 * row_count, col_count),
-        in_specs=[vmem],
-        out_specs=vmem,
-        scratch_shapes=[pltpu.VMEM((8 * col_count, col_count), jnp.float32)],
+        functools.partial(contract_kernel, shards),
+        out_shape=[triangle_block] * shards,
+        in_specs=[vmem] * shards,
+        out_specs=[vmem] * shards,
+        scratch_shapes=[held(side_block, jnp.float32), held(triangle_block, jnp.bfloat16)],
         name="contract",
-    )(sides)
-    triangle = lax.all_to_all(triangle, axes, split_axis=0, concat_axis=0, tiled=True)
+    )(*exchange(sides))
+    triangle = exchange(triangle)
     gate_values = pl.pallas_call(
         gate_kernel,
         out_shape=shaped(tokens, chan_count),
@@ -138,11 +172,11 @@
     return pl.pallas_call(
         finish_kernel,
         out_shape=shaped(row_count, col_count, chan_count),
-        in_specs=[vmem] * 5,
+        in_specs=[vmem] * (4 + shards),
         out_specs=vmem,
-        scratch_shapes=[pltpu.VMEM((tokens, chan_count), jnp.float32)],
+        scratch_shapes=[held(triangle_block, jnp.float32)],
         name="finish",
-    )(triangle, gate_values, line(out_gain), line(out_bias), w_out)
+    )(gate_values, line(out_gain), line(out_bias), w_out, *triangle)
 
 
 def local_arrays(pair, valid, norm_gain, norm_bias, w_proj, out_gain, out_bias, w_out):
@@ -196,6 +230,7 @@
         and (row_count, col_count, chan_count) == (4, 128, 128)
         and shards * row_count == col_count
         and shards * 4 == chan_count
+        and shards & (shards - 1) == 0
     )
     return (local_blocks if fits else local_arrays)(pair, *rest)
 

time: 35.8 us -> 118 us (3.30)
  starting transfers between devices: 2.56 us -> 101 us
  blocking collectives: 18 us -> 0 us
    ppermute x0 -> x62, starting transfers between devices: none -> 101 us  [exchange(): lax.ppermute(block, axes, [(i, i ^ s) for i in range(shards)])]
    all_to_all x1 -> x0, blocking collectives: 18 us -> none  [local_blocks(): sides = lax.all_to_all(sides, axes, split_axis=0, concat_axis=0, tiled=True)]
    ppermute x0 -> x62, waiting for transfers between devices: none -> 6.69 us  [exchange(): lax.ppermute(block, axes, [(i, i ^ s) for i in range(shards)])]
    all_to_all x1 -> x0, waiting for transfers between devices: 6.42 us -> none  [local_blocks(): lax.all_to_all(triangle, axes, split_axis=0, concat_axis=0, tiled=True)]
    all_to_all x1 -> x0, starting transfers between devices: 2.56 us -> none  [local_blocks(): lax.all_to_all(triangle, axes, split_axis=0, concat_axis=0, tiled=True)]
  transfers between devices with their start and end apart: 1 -> 62, of which waited for: 1 -> 3; matrix products, arithmetic and copies ran while one was open for 0% -> 0% of each run, Pallas kernels for 5% -> 2%
where the time goes in v3:
time: 118 us
  starting transfers between devices  101 us (86%)
  Pallas kernels  8.07 us (7%)
  waiting for transfers between devices  6.69 us (6%)
  local copies, waits for them, and re-layouts  1.21 us (1%)
    ppermute x62, starting transfers between devices, exchange(): lax.ppermute(block, axes, [(i, i ^ s) for i in range(shards)])  101 us
    ppermute x62, waiting for transfers between devices, exchange(): lax.ppermute(block, axes, [(i, i ^ s) for i in range(shards)])  6.69 us
  transfers between devices with their start and end apart: 62, of which 3 were waited for; matrix products, arithmetic and copies ran while one was open for 0% of the time, Pallas kernels for 2%

profile of v3, /device:TPU:0, one launch (start us, length us, event | category | flops | bytes accessed | tf_op | source)
XLA Modules:
  0.0 117.5 jit_solution(15641225795366530088)
XLA Ops:
  2.8 2.6 %collective-permute-start.1 = (bf16[32,128]{1,0:T(8,128)(2,1)}, bf16[32,128]{1,0:T(8,128)(2,1)S(1)}, u32[]{:S(2)}, u32[]{:S(2)}) collective-permute-start(bf16[32,128]{1,0:T(8,128)(2,1)} %get-tuple-element.73), channel_id=1, source_target_pairs={{0,2},{1,3},{2,0},{3,1},{4,6},{5,7},{6,4},{7,5},{8,10},{9,11},{10,... | collective-permute-start | bytes 24584 | tf_op jit(solution)/shard_map/ppermute | solution.py:123
  7.3 2.6 %collective-permute-start.5 = (bf16[32,128]{1,0:T(8,128)(2,1)}, bf16[32,128]{1,0:T(8,128)(2,1)S(1)}, u32[]{:S(2)}, u32[]{:S(2)}) collective-permute-start(bf16[32,128]{1,0:T(8,128)(2,1)} %get-tuple-element.77), channel_id=1, source_target_pairs={{0,6},{1,7},{2,4},{3,5},{4,2},{5,3},{6,0},{7,1},{8,14},{9,15},{10,... | collective-permute-start | bytes 24584 | tf_op jit(solution)/shard_map/ppermute | solution.py:123
  11.8 2.6 %collective-permute-start.9 = (bf16[32,128]{1,0:T(8,128)(2,1)}, bf16[32,128]{1,0:T(8,128)(2,1)S(1)}, u32[]{:S(2)}, u32[]{:S(2)}) collective-permute-start(bf16[32,128]{1,0:T(8,128)(2,1)} %get-tuple-element.81), channel_id=1, source_target_pairs={{0,10},{1,11},{2,8},{3,9},{4,14},{5,15},{6,12},{7,13},{8,2},{9,3},... | collective-permute-start | bytes 24584 | tf_op jit(solution)/shard_map/ppermute | solution.py:123
  14.5 2.6 %collective-permute-start.11 = (bf16[32,128]{1,0:T(8,128)(2,1)}, bf16[32,128]{1,0:T(8,128)(2,1)S(1)}, u32[]{:S(2)}, u32[]{:S(2)}) collective-permute-start(bf16[32,128]{1,0:T(8,128)(2,1)} %get-tuple-element.83), channel_id=1, source_target_pairs={{0,12},{1,13},{2,14},{3,15},{4,8},{5,9},{6,10},{7,11},{8,4},{9,5},... | collective-permute-start | bytes 24584 | tf_op jit(solution)/shard_map/ppermute | solution.py:123
  17.1 3.5 %collective-permute-start.13 = (bf16[32,128]{1,0:T(8,128)(2,1)}, bf16[32,128]{1,0:T(8,128)(2,1)S(1)}, u32[]{:S(2)}, u32[]{:S(2)}) collective-permute-start(bf16[32,128]{1,0:T(8,128)(2,1)} %get-tuple-element.85), channel_id=1, source_target_pairs={{0,14},{1,15},{2,12},{3,13},{4,10},{5,11},{6,8},{7,9},{8,6},{9,7},... | collective-permute-start | bytes 24584 | tf_op jit(solution)/shard_map/ppermute | solution.py:123
  20.9 2.6 %collective-permute-start.15 = (bf16[32,128]{1,0:T(8,128)(2,1)}, bf16[32,128]{1,0:T(8,128)(2,1)S(1)}, u32[]{:S(2)}, u32[]{:S(2)}) collective-permute-start(bf16[32,128]{1,0:T(8,128)(2,1)} %get-tuple-element.87), channel_id=1, source_target_pairs={{0,16},{1,17},{2,18},{3,19},{4,20},{5,21},{6,22},{7,23},{8,24},{9,... | collective-permute-start | bytes 24584 | tf_op jit(solution)/shard_map/ppermute | solution.py:123
  23.6 3.5 %collective-permute-start.17 = (bf16[32,128]{1,0:T(8,128)(2,1)}, bf16[32,128]{1,0:T(8,128)(2,1)S(1)}, u32[]{:S(2)}, u32[]{:S(2)}) collective-permute-start(bf16[32,128]{1,0:T(8,128)(2,1)} %get-tuple-element.89), channel_id=1, source_target_pairs={{0,18},{1,19},{2,16},{3,17},{4,22},{5,23},{6,20},{7,21},{8,26},{9,... | collective-permute-start | bytes 24584 | tf_op jit(solution)/shard_map/ppermute | solution.py:123
  27.2 3.5 %collective-permute-start.19 = (bf16[32,128]{1,0:T(8,128)(2,1)}, bf16[32,128]{1,0:T(8,128)(2,1)S(1)}, u32[]{:S(2)}, u32[]{:S(2)}) collective-permute-start(bf16[32,128]{1,0:T(8,128)(2,1)} %get-tuple-element.91), channel_id=1, source_target_pairs={{0,20},{1,21},{2,22},{3,23},{4,16},{5,17},{6,18},{7,19},{8,28},{9,... | collective-permute-start | bytes 24584 | tf_op jit(solution)/shard_map/ppermute | solution.py:123
  30.7 4.4 %collective-permute-start.21 = (bf16[32,128]{1,0:T(8,128)(2,1)}, bf16[32,128]{1,0:T(8,128)(2,1)S(1)}, u32[]{:S(2)}, u32[]{:S(2)}) collective-permute-start(bf16[32,128]{1,0:T(8,128)(2,1)} %get-tuple-element.93), channel_id=1, source_target_pairs={{0,22},{1,23},{2,20},{3,21},{4,18},{5,19},{6,16},{7,17},{8,30},{9,... | collective-permute-start | bytes 24584 | tf_op jit(solution)/shard_map/ppermute | solution.py:123
  35.3 3.4 %collective-permute-start.23 = (bf16[32,128]{1,0:T(8,128)(2,1)}, bf16[32,128]{1,0:T(8,128)(2,1)S(1)}, u32[]{:S(2)}, u32[]{:S(2)}) collective-permute-start(bf16[32,128]{1,0:T(8,128)(2,1)} %get-tuple-element.95), channel_id=1, source_target_pairs={{0,24},{1,25},{2,26},{3,27},{4,28},{5,29},{6,30},{7,31},{8,16},{9,... | collective-permute-start | bytes 24584 | tf_op jit(solution)/shard_map/ppermute | solution.py:123
  38.9 4.4 %collective-permute-start.25 = (bf16[32,128]{1,0:T(8,128)(2,1)S(1)}, bf16[32,128]{1,0:T(8,128)(2,1)S(1)}, u32[]{:S(2)}, u32[]{:S(2)}) collective-permute-start(bf16[32,128]{1,0:T(8,128)(2,1)S(1)} %copy-done.67), channel_id=1, source_target_pairs={{0,26},{1,27},{2,24},{3,25},{4,30},{5,31},{6,28},{7,29},{8,18},{9,... | collective-permute-start | bytes 24584 | tf_op jit(solution)/shard_map/ppermute | solution.py:123
  43.5 4.4 %collective-permute-start.27 = (bf16[32,128]{1,0:T(8,128)(2,1)S(1)}, bf16[32,128]{1,0:T(8,128)(2,1)S(1)}, u32[]{:S(2)}, u32[]{:S(2)}) collective-permute-start(bf16[32,128]{1,0:T(8,128)(2,1)S(1)} %copy-done.65), channel_id=1, source_target_pairs={{0,28},{1,29},{2,30},{3,31},{4,24},{5,25},{6,26},{7,27},{8,20},{9,... | collective-permute-start | bytes 24584 | tf_op jit(solution)/shard_map/ppermute | solution.py:123
  48.1 5.3 %collective-permute-start.29 = (bf16[32,128]{1,0:T(8,128)(2,1)S(1)}, bf16[32,128]{1,0:T(8,128)(2,1)S(1)}, u32[]{:S(2)}, u32[]{:S(2)}) collective-permute-start(bf16[32,128]{1,0:T(8,128)(2,1)S(1)} %copy-done.63), channel_id=1, source_target_pairs={{0,30},{1,31},{2,28},{3,29},{4,26},{5,27},{6,24},{7,25},{8,22},{9,... | collective-permute-start | bytes 24584 | tf_op jit(solution)/shard_map/ppermute | solution.py:123
  55.4 4.8 %collective-permute-done.30.refs_31_ = bf16[32,128]{1,0:T(8,128)(2,1)S(1)} collective-permute-done((bf16[32,128]{1,0:T(8,128)(2,1)S(1)}, bf16[32,128]{1,0:T(8,128)(2,1)S(1)}, u32[]{:S(2)}, u32[]{:S(2)}) %collective-permute-start.30) | collective-permute-done | bytes 8224 | tf_op jit(solution)/shard_map/ppermute | solution.py:123
  73.7 2.6 %collective-permute-start.43 = (bf16[16,128]{1,0:T(8,128)(2,1)}, bf16[16,128]{1,0:T(8,128)(2,1)S(1)}, u32[]{:S(2)}, u32[]{:S(2)}) collective-permute-start(bf16[16,128]{1,0:T(8,128)(2,1)} %get-tuple-element.116), channel_id=1, source_target_pairs={{0,13},{1,12},{2,15},{3,14},{4,9},{5,8},{6,11},{7,10},{8,5},{9,4},... | collective-permute-start | bytes 12296 | tf_op jit(solution)/shard_map/ppermute | solution.py:123
  76.7 3.2 %collective-permute-start.45 = (bf16[16,128]{1,0:T(8,128)(2,1)}, bf16[16,128]{1,0:T(8,128)(2,1)S(1)}, u32[]{:S(2)}, u32[]{:S(2)}) collective-permute-start(bf16[16,128]{1,0:T(8,128)(2,1)} %get-tuple-element.118), channel_id=1, source_target_pairs={{0,15},{1,14},{2,13},{3,12},{4,11},{5,10},{6,9},{7,8},{8,7},{9,6},... | collective-permute-start | bytes 12296 | tf_op jit(solution)/shard_map/ppermute | solution.py:123
  79.9 2.7 %collective-permute-start.47 = (bf16[16,128]{1,0:T(8,128)(2,1)}, bf16[16,128]{1,0:T(8,128)(2,1)S(1)}, u32[]{:S(2)}, u32[]{:S(2)}) collective-permute-start(bf16[16,128]{1,0:T(8,128)(2,1)} %get-tuple-element.120), channel_id=1, source_target_pairs={{0,17},{1,16},{2,19},{3,18},{4,21},{5,20},{6,23},{7,22},{8,25},{9,... | collective-permute-start | bytes 12296 | tf_op jit(solution)/shard_map/ppermute | solution.py:123
  83.0 3.2 %collective-permute-start.49 = (bf16[16,128]{1,0:T(8,128)(2,1)S(1)}, bf16[16,128]{1,0:T(8,128)(2,1)S(1)}, u32[]{:S(2)}, u32[]{:S(2)}) collective-permute-start(bf16[16,128]{1,0:T(8,128)(2,1)S(1)} %copy-done.81), channel_id=1, source_target_pairs={{0,19},{1,18},{2,17},{3,16},{4,23},{5,22},{6,21},{7,20},{8,27},{9,... | collective-permute-start | bytes 12296 | tf_op jit(solution)/shard_map/ppermute | solution.py:123
  86.3 3.6 %collective-permute-start.51 = (bf16[16,128]{1,0:T(8,128)(2,1)S(1)}, bf16[16,128]{1,0:T(8,128)(2,1)S(1)}, u32[]{:S(2)}, u32[]{:S(2)}) collective-permute-start(bf16[16,128]{1,0:T(8,128)(2,1)S(1)} %copy-done.79), channel_id=1, source_target_pairs={{0,21},{1,20},{2,23},{3,22},{4,17},{5,16},{6,19},{7,18},{8,29},{9,... | collective-permute-start | bytes 12296 | tf_op jit(solution)/shard_map/ppermute | solution.py:123
  90.4 4.1 %collective-permute-start.53 = (bf16[16,128]{1,0:T(8,128)(2,1)S(1)}, bf16[16,128]{1,0:T(8,128)(2,1)S(1)}, u32[]{:S(2)}, u32[]{:S(2)}) collective-permute-start(bf16[16,128]{1,0:T(8,128)(2,1)S(1)} %copy-done.77), channel_id=1, source_target_pairs={{0,23},{1,22},{2,21},{3,20},{4,19},{5,18},{6,17},{7,16},{8,31},{9,... | collective-permute-start | bytes 12296 | tf_op jit(solution)/shard_map/ppermute | solution.py:123
  95.0 3.3 %collective-permute-start.55 = (bf16[16,128]{1,0:T(8,128)(2,1)S(1)}, bf16[16,128]{1,0:T(8,128)(2,1)S(1)}, u32[]{:S(2)}, u32[]{:S(2)}) collective-permute-start(bf16[16,128]{1,0:T(8,128)(2,1)S(1)} %copy-done.75), channel_id=1, source_target_pairs={{0,25},{1,24},{2,27},{3,26},{4,29},{5,28},{6,31},{7,30},{8,17},{9,... | collective-permute-start | bytes 12296 | tf_op jit(solution)/shard_map/ppermute | solution.py:123
  98.7 4.1 %collective-permute-start.57 = (bf16[16,128]{1,0:T(8,128)(2,1)S(1)}, bf16[16,128]{1,0:T(8,128)(2,1)S(1)}, u32[]{:S(2)}, u32[]{:S(2)}) collective-permute-start(bf16[16,128]{1,0:T(8,128)(2,1)S(1)} %copy-done.73), channel_id=1, source_target_pairs={{0,27},{1,26},{2,25},{3,24},{4,31},{5,30},{6,29},{7,28},{8,19},{9,... | collective-permute-start | bytes 12296 | tf_op jit(solution)/shard_map/ppermute | solution.py:123
  103.3 4.2 %collective-permute-start.59 = (bf16[16,128]{1,0:T(8,128)(2,1)S(1)}, bf16[16,128]{1,0:T(8,128)(2,1)S(1)}, u32[]{:S(2)}, u32[]{:S(2)}) collective-permute-start(bf16[16,128]{1,0:T(8,128)(2,1)S(1)} %copy-done.71), channel_id=1, source_target_pairs={{0,29},{1,28},{2,31},{3,30},{4,25},{5,24},{6,27},{7,26},{8,21},{9,... | collective-permute-start | bytes 12296 | tf_op jit(solution)/shard_map/ppermute | solution.py:123
  108.0 4.9 %collective-permute-start.61 = (bf16[16,128]{1,0:T(8,128)(2,1)S(1)}, bf16[16,128]{1,0:T(8,128)(2,1)S(1)}, u32[]{:S(2)}, u32[]{:S(2)}) collective-permute-start(bf16[16,128]{1,0:T(8,128)(2,1)S(1)} %copy-done.69), channel_id=1, source_target_pairs={{0,31},{1,30},{2,29},{3,28},{4,27},{5,26},{6,25},{7,24},{8,23},{9,... | collective-permute-start | bytes 12296 | tf_op jit(solution)/shard_map/ppermute | solution.py:123
  (270 shorter events, 30.9 us)
Async XLA Ops:
  11.8 8.9 %collective-permute-start.9 = (bf16[32,128]{1,0:T(8,128)(2,1)}, bf16[32,128]{1,0:T(8,128)(2,1)S(1)}, u32[]{:S(2)}, u32[]{:S(2)}) collective-permute-start(bf16[32,128]{1,0:T(8,128)(2,1)} %get-tuple-element.81), channel_id=1, source_target_pairs={{0,10},{1,11},{2,8},{3,9},{4,14},{5,15},{6,12},{7,13},{8,2},{9,3},... | collective-permute-start | bytes 24584 | tf_op jit(solution)/shard_map/ppermute | solution.py:123
  14.5 9.0 %collective-permute-start.11 = (bf16[32,128]{1,0:T(8,128)(2,1)}, bf16[32,128]{1,0:T(8,128)(2,1)S(1)}, u32[]{:S(2)}, u32[]{:S(2)}) collective-permute-start(bf16[32,128]{1,0:T(8,128)(2,1)} %get-tuple-element.83), channel_id=1, source_target_pairs={{0,12},{1,13},{2,14},{3,15},{4,8},{5,9},{6,10},{7,11},{8,4},{9,5},... | collective-permute-start | bytes 24584 | tf_op jit(solution)/shard_map/ppermute | solution.py:123
  17.1 9.9 %collective-permute-start.13 = (bf16[32,128]{1,0:T(8,128)(2,1)}, bf16[32,128]{1,0:T(8,128)(2,1)S(1)}, u32[]{:S(2)}, u32[]{:S(2)}) collective-permute-start(bf16[32,128]{1,0:T(8,128)(2,1)} %get-tuple-element.85), channel_id=1, source_target_pairs={{0,14},{1,15},{2,12},{3,13},{4,10},{5,11},{6,8},{7,9},{8,6},{9,7},... | collective-permute-start | bytes 24584 | tf_op jit(solution)/shard_map/ppermute | solution.py:123
  20.9 9.8 %collective-permute-start.15 = (bf16[32,128]{1,0:T(8,128)(2,1)}, bf16[32,128]{1,0:T(8,128)(2,1)S(1)}, u32[]{:S(2)}, u32[]{:S(2)}) collective-permute-start(bf16[32,128]{1,0:T(8,128)(2,1)} %get-tuple-element.87), channel_id=1, source_target_pairs={{0,16},{1,17},{2,18},{3,19},{4,20},{5,21},{6,22},{7,23},{8,24},{9,... | collective-permute-start | bytes 24584 | tf_op jit(solution)/shard_map/ppermute | solution.py:123
  23.6 11.5 %collective-permute-start.17 = (bf16[32,128]{1,0:T(8,128)(2,1)}, bf16[32,128]{1,0:T(8,128)(2,1)S(1)}, u32[]{:S(2)}, u32[]{:S(2)}) collective-permute-start(bf16[32,128]{1,0:T(8,128)(2,1)} %get-tuple-element.89), channel_id=1, source_target_pairs={{0,18},{1,19},{2,16},{3,17},{4,22},{5,23},{6,20},{7,21},{8,26},{9,... | collective-permute-start | bytes 24584 | tf_op jit(solution)/shard_map/ppermute | solution.py:123
  27.2 11.5 %collective-permute-start.19 = (bf16[32,128]{1,0:T(8,128)(2,1)}, bf16[32,128]{1,0:T(8,128)(2,1)S(1)}, u32[]{:S(2)}, u32[]{:S(2)}) collective-permute-start(bf16[32,128]{1,0:T(8,128)(2,1)} %get-tuple-element.91), channel_id=1, source_target_pairs={{0,20},{1,21},{2,22},{3,23},{4,16},{5,17},{6,18},{7,19},{8,28},{9,... | collective-permute-start | bytes 24584 | tf_op jit(solution)/shard_map/ppermute | solution.py:123
  30.7 12.6 %collective-permute-start.21 = (bf16[32,128]{1,0:T(8,128)(2,1)}, bf16[32,128]{1,0:T(8,128)(2,1)S(1)}, u32[]{:S(2)}, u32[]{:S(2)}) collective-permute-start(bf16[32,128]{1,0:T(8,128)(2,1)} %get-tuple-element.93), channel_id=1, source_target_pairs={{0,22},{1,23},{2,20},{3,21},{4,18},{5,19},{6,16},{7,17},{8,30},{9,... | collective-permute-start | bytes 24584 | tf_op jit(solution)/shard_map/ppermute | solution.py:123
  35.3 12.6 %collective-permute-start.23 = (bf16[32,128]{1,0:T(8,128)(2,1)}, bf16[32,128]{1,0:T(8,128)(2,1)S(1)}, u32[]{:S(2)}, u32[]{:S(2)}) collective-permute-start(bf16[32,128]{1,0:T(8,128)(2,1)} %get-tuple-element.95), channel_id=1, source_target_pairs={{0,24},{1,25},{2,26},{3,27},{4,28},{5,29},{6,30},{7,31},{8,16},{9,... | collective-permute-start | bytes 24584 | tf_op jit(solution)/shard_map/ppermute | solution.py:123
  38.7 9.3 %collective-permute-start.24 = (bf16[32,128]{1,0:T(8,128)(2,1)S(1)}, bf16[32,128]{1,0:T(8,128)(2,1)S(1)}, u32[]{:S(2)}, u32[]{:S(2)}) collective-permute-start(bf16[32,128]{1,0:T(8,128)(2,1)S(1)} %copy-done.68), channel_id=1, source_target_pairs={{0,25},{1,24},{2,27},{3,26},{4,29},{5,28},{6,31},{7,30},{8,17},{9,... | collective-permute-start | bytes 24584 | tf_op jit(solution)/shard_map/ppermute | solution.py:123
  38.9 14.5 %collective-permute-start.25 = (bf16[32,128]{1,0:T(8,128)(2,1)S(1)}, bf16[32,128]{1,0:T(8,128)(2,1)S(1)}, u32[]{:S(2)}, u32[]{:S(2)}) collective-permute-start(bf16[32,128]{1,0:T(8,128)(2,1)S(1)} %copy-done.67), channel_id=1, source_target_pairs={{0,26},{1,27},{2,24},{3,25},{4,30},{5,31},{6,28},{7,29},{8,18},{9,... | collective-permute-start | bytes 24584 | tf_op jit(solution)/shard_map/ppermute | solution.py:123
  43.3 10.3 %collective-permute-start.26 = (bf16[32,128]{1,0:T(8,128)(2,1)S(1)}, bf16[32,128]{1,0:T(8,128)(2,1)S(1)}, u32[]{:S(2)}, u32[]{:S(2)}) collective-permute-start(bf16[32,128]{1,0:T(8,128)(2,1)S(1)} %copy-done.66), channel_id=1, source_target_pairs={{0,27},{1,26},{2,25},{3,24},{4,31},{5,30},{6,29},{7,28},{8,19},{9,... | collective-permute-start | bytes 24584 | tf_op jit(solution)/shard_map/ppermute | solution.py:123
  43.5 10.1 %collective-permute-start.27 = (bf16[32,128]{1,0:T(8,128)(2,1)S(1)}, bf16[32,128]{1,0:T(8,128)(2,1)S(1)}, u32[]{:S(2)}, u32[]{:S(2)}) collective-permute-start(bf16[32,128]{1,0:T(8,128)(2,1)S(1)} %copy-done.65), channel_id=1, source_target_pairs={{0,28},{1,29},{2,30},{3,31},{4,24},{5,25},{6,26},{7,27},{8,20},{9,... | collective-permute-start | bytes 24584 | tf_op jit(solution)/shard_map/ppermute | solution.py:123
  73.7 8.9 %collective-permute-start.43 = (bf16[16,128]{1,0:T(8,128)(2,1)}, bf16[16,128]{1,0:T(8,128)(2,1)S(1)}, u32[]{:S(2)}, u32[]{:S(2)}) collective-permute-start(bf16[16,128]{1,0:T(8,128)(2,1)} %get-tuple-element.116), channel_id=1, source_target_pairs={{0,13},{1,12},{2,15},{3,14},{4,9},{5,8},{6,11},{7,10},{8,5},{9,4},... | collective-permute-start | bytes 12296 | tf_op jit(solution)/shard_map/ppermute | solution.py:123
  76.7 9.5 %collective-permute-start.45 = (bf16[16,128]{1,0:T(8,128)(2,1)}, bf16[16,128]{1,0:T(8,128)(2,1)S(1)}, u32[]{:S(2)}, u32[]{:S(2)}) collective-permute-start(bf16[16,128]{1,0:T(8,128)(2,1)} %get-tuple-element.118), channel_id=1, source_target_pairs={{0,15},{1,14},{2,13},{3,12},{4,11},{5,10},{6,9},{7,8},{8,7},{9,6},... | collective-permute-start | bytes 12296 | tf_op jit(solution)/shard_map/ppermute | solution.py:123
  79.9 10.1 %collective-permute-start.47 = (bf16[16,128]{1,0:T(8,128)(2,1)}, bf16[16,128]{1,0:T(8,128)(2,1)S(1)}, u32[]{:S(2)}, u32[]{:S(2)}) collective-permute-start(bf16[16,128]{1,0:T(8,128)(2,1)} %get-tuple-element.120), channel_id=1, source_target_pairs={{0,17},{1,16},{2,19},{3,18},{4,21},{5,20},{6,23},{7,22},{8,25},{9,... | collective-permute-start | bytes 12296 | tf_op jit(solution)/shard_map/ppermute | solution.py:123
  83.0 11.5 %collective-permute-start.49 = (bf16[16,128]{1,0:T(8,128)(2,1)S(1)}, bf16[16,128]{1,0:T(8,128)(2,1)S(1)}, u32[]{:S(2)}, u32[]{:S(2)}) collective-permute-start(bf16[16,128]{1,0:T(8,128)(2,1)S(1)} %copy-done.81), channel_id=1, source_target_pairs={{0,19},{1,18},{2,17},{3,16},{4,23},{5,22},{6,21},{7,20},{8,27},{9,... | collective-permute-start | bytes 12296 | tf_op jit(solution)/shard_map/ppermute | solution.py:123
  86.3 11.9 %collective-permute-start.51 = (bf16[16,128]{1,0:T(8,128)(2,1)S(1)}, bf16[16,128]{1,0:T(8,128)(2,1)S(1)}, u32[]{:S(2)}, u32[]{:S(2)}) collective-permute-start(bf16[16,128]{1,0:T(8,128)(2,1)S(1)} %copy-done.79), channel_id=1, source_target_pairs={{0,21},{1,20},{2,23},{3,22},{4,17},{5,16},{6,19},{7,18},{8,29},{9,... | collective-permute-start | bytes 12296 | tf_op jit(solution)/shard_map/ppermute | solution.py:123
  90.4 12.5 %collective-permute-start.53 = (bf16[16,128]{1,0:T(8,128)(2,1)S(1)}, bf16[16,128]{1,0:T(8,128)(2,1)S(1)}, u32[]{:S(2)}, u32[]{:S(2)}) collective-permute-start(bf16[16,128]{1,0:T(8,128)(2,1)S(1)} %copy-done.77), channel_id=1, source_target_pairs={{0,23},{1,22},{2,21},{3,20},{4,19},{5,18},{6,17},{7,16},{8,31},{9,... | collective-permute-start | bytes 12296 | tf_op jit(solution)/shard_map/ppermute | solution.py:123
  94.5 8.8 %collective-permute-start.54 = (bf16[16,128]{1,0:T(8,128)(2,1)S(1)}, bf16[16,128]{1,0:T(8,128)(2,1)S(1)}, u32[]{:S(2)}, u32[]{:S(2)}) collective-permute-start(bf16[16,128]{1,0:T(8,128)(2,1)S(1)} %copy-done.76), channel_id=1, source_target_pairs={{0,24},{1,25},{2,26},{3,27},{4,28},{5,29},{6,30},{7,31},{8,16},{9,... | collective-permute-start | bytes 12296 | tf_op jit(solution)/shard_map/ppermute | solution.py:123
  95.0 12.5 %collective-permute-start.55 = (bf16[16,128]{1,0:T(8,128)(2,1)S(1)}, bf16[16,128]{1,0:T(8,128)(2,1)S(1)}, u32[]{:S(2)}, u32[]{:S(2)}) collective-permute-start(bf16[16,128]{1,0:T(8,128)(2,1)S(1)} %copy-done.75), channel_id=1, source_target_pairs={{0,25},{1,24},{2,27},{3,26},{4,29},{5,28},{6,31},{7,30},{8,17},{9,... | collective-permute-start | bytes 12296 | tf_op jit(solution)/shard_map/ppermute | solution.py:123
  98.3 9.7 %collective-permute-start.56 = (bf16[16,128]{1,0:T(8,128)(2,1)S(1)}, bf16[16,128]{1,0:T(8,128)(2,1)S(1)}, u32[]{:S(2)}, u32[]{:S(2)}) collective-permute-start(bf16[16,128]{1,0:T(8,128)(2,1)S(1)} %copy-done.74), channel_id=1, source_target_pairs={{0,26},{1,27},{2,24},{3,25},{4,30},{5,31},{6,28},{7,29},{8,18},{9,... | collective-permute-start | bytes 12296 | tf_op jit(solution)/shard_map/ppermute | solution.py:123
  98.7 16.1 %collective-permute-start.57 = (bf16[16,128]{1,0:T(8,128)(2,1)S(1)}, bf16[16,128]{1,0:T(8,128)(2,1)S(1)}, u32[]{:S(2)}, u32[]{:S(2)}) collective-permute-start(bf16[16,128]{1,0:T(8,128)(2,1)S(1)} %copy-done.73), channel_id=1, source_target_pairs={{0,27},{1,26},{2,25},{3,24},{4,31},{5,30},{6,29},{7,28},{8,19},{9,... | collective-permute-start | bytes 12296 | tf_op jit(solution)/shard_map/ppermute | solution.py:123
  102.8 12.0 %collective-permute-start.58 = (bf16[16,128]{1,0:T(8,128)(2,1)S(1)}, bf16[16,128]{1,0:T(8,128)(2,1)S(1)}, u32[]{:S(2)}, u32[]{:S(2)}) collective-permute-start(bf16[16,128]{1,0:T(8,128)(2,1)S(1)} %copy-done.72), channel_id=1, source_target_pairs={{0,28},{1,29},{2,30},{3,31},{4,24},{5,25},{6,26},{7,27},{8,20},{9,... | collective-permute-start | bytes 12296 | tf_op jit(solution)/shard_map/ppermute | solution.py:123
  103.3 11.6 %collective-permute-start.59 = (bf16[16,128]{1,0:T(8,128)(2,1)S(1)}, bf16[16,128]{1,0:T(8,128)(2,1)S(1)}, u32[]{:S(2)}, u32[]{:S(2)}) collective-permute-start(bf16[16,128]{1,0:T(8,128)(2,1)S(1)} %copy-done.71), channel_id=1, source_target_pairs={{0,29},{1,28},{2,31},{3,30},{4,25},{5,24},{6,27},{7,26},{8,21},{9,... | collective-permute-start | bytes 12296 | tf_op jit(solution)/shard_map/ppermute | solution.py:123
  (121 other events, 1909.2 us)

commit v4 on v2

--- a/solution.py
+++ b/solution.py
@@ -9,6 +9,7 @@
 
 epsilon = 1e-05
 axes = ("wide", "narrow")
+kernel_vmem = 8 * 2**20
 
 
 def layer_norm(values, gain_vec, bias_vec, axis_dim):
@@ -116,6 +117,7 @@
         out_shape=(shaped(shards, 8 * row_count, col_count), shaped(tokens, chan_count)),
         in_specs=[smem] + [vmem] * 5,
         out_specs=(vmem, vmem),
+        compiler_params=pltpu.CompilerParams(vmem_limit_bytes=kernel_vmem),
         name="project",
     )(valid, line(valid), pair, line(norm_gain), line(norm_bias), w_proj)
     sides = lax.all_to_all(sides, axes, split_axis=0, concat_axis=0, tiled=True)
@@ -125,6 +127,7 @@
         in_specs=[vmem],
         out_specs=vmem,
         scratch_shapes=[pltpu.VMEM((8 * col_count, col_count), jnp.float32)],
+        compiler_params=pltpu.CompilerParams(vmem_limit_bytes=kernel_vmem),
         name="contract",
     )(sides)
     triangle = lax.all_to_all(triangle, axes, split_axis=0, concat_axis=0, tiled=True)
@@ -133,6 +136,7 @@
         out_shape=shaped(tokens, chan_count),
         in_specs=[vmem] * 2,
         out_specs=vmem,
+        compiler_params=pltpu.CompilerParams(vmem_limit_bytes=kernel_vmem),
         name="gate",
     )(normed, w_proj)
     return pl.pallas_call(
@@ -141,6 +145,7 @@
         in_specs=[vmem] * 5,
         out_specs=vmem,
         scratch_shapes=[pltpu.VMEM((tokens, chan_count), jnp.float32)],
+        compiler_params=pltpu.CompilerParams(vmem_limit_bytes=kernel_vmem),
         name="finish",
     )(triangle, gate_values, line(out_gain), line(out_bias), w_out)
 

time: 35.8 us -> 35 us (0.978)
  Pallas kernels: 7.86 us -> 3.12 us
  local copies, waits for them, and re-layouts: 0.64 us -> 3.18 us
  waiting for transfers between devices: 6.42 us -> 8.02 us
    unnamed x2 -> x18, local copies, waits for them, and re-layouts: 0.64 us -> 3.18 us
    pallas_call x1, Pallas kernels: 1.81 us -> 0.18 us  [local_blocks(): pl.pallas_call(gate_kernel, out_shape=shaped(tokens, chan_count), in_spec...]
    all_to_all x1, waiting for transfers between devices: 6.42 us -> 8.02 us  [local_blocks(): lax.all_to_all(triangle, axes, split_axis=0, concat_axis=0, tiled=True)]
    pallas_call x1, Pallas kernels: 2.27 us -> 1.08 us  [local_blocks(): pl.pallas_call(project_kernel, out_shape=(shaped(shards, 8 * row_count, c...]
    pallas_call x1, Pallas kernels: 1.95 us -> 0.96 us  [local_blocks(): pl.pallas_call(finish_kernel, out_shape=shaped(row_count, col_count, chan...]
    pallas_call x1, Pallas kernels: 1.83 us -> 0.9 us  [local_blocks(): pl.pallas_call(contract_kernel, out_shape=shaped(shards, 4 * row_count, c...]
  transfers between devices with their start and end apart: 1 -> 1, of which waited for: 1 -> 1; matrix products, arithmetic and copies ran while one was open for 0% -> 0% of each run, Pallas kernels for 5% -> 1%
where the time goes in v4:
time: 35 us; the launch traced here: 34.8 us
  blocking collectives  17.7 us (51%)
  waiting for transfers between devices  8.02 us (23%)
  local copies, waits for them, and re-layouts  3.18 us (9%)
  Pallas kernels  3.12 us (9%)
  starting transfers between devices  2.71 us (8%)
    all_to_all x1, blocking collectives, local_blocks(): sides = lax.all_to_all(sides, axes, split_axis=0, concat_axis=0, tiled=True)  17.7 us
    all_to_all x1, waiting for transfers between devices, local_blocks(): lax.all_to_all(triangle, axes, split_axis=0, concat_axis=0, tiled=True)  8.02 us
    unnamed x18, local copies, waits for them, and re-layouts  3.18 us
    all_to_all x1, starting transfers between devices, local_blocks(): lax.all_to_all(triangle, axes, split_axis=0, concat_axis=0, tiled=True)  2.71 us
    pallas_call x1, Pallas kernels, local_blocks(): pl.pallas_call(project_kernel, out_shape=(shaped(shards, 8 * row_count, c...  1.08 us
    pallas_call x1, Pallas kernels, local_blocks(): pl.pallas_call(finish_kernel, out_shape=shaped(row_count, col_count, chan...  0.96 us
    pallas_call x1, Pallas kernels, local_blocks(): pl.pallas_call(contract_kernel, out_shape=shaped(shards, 4 * row_count, c...  0.9 us
  transfers between devices with their start and end apart: 1, of which 1 were waited for; matrix products, arithmetic and copies ran while one was open for 0% of the time, Pallas kernels for 1%

profile of v4, /device:TPU:0, one launch (start us, length us, event | category | flops | bytes accessed | tf_op | source)
XLA Modules:
  0.0 34.8 jit_solution(8848547816187554371)
XLA Ops:
  0.0 0.0 copy-start.4
  0.0 0.0 copy-start.5
  0.0 0.0 copy-start.6
  0.0 0.6 %copy-done.4 = s32[128]{0:T(128)S(1)} copy-done((s32[128]{0:T(128)S(1)}, s32[128]{0:T(128)}, u32[]{:S(2)}) %copy-start.4) | copy-done | bytes 536
  0.7 0.0 copy-done.5
  0.7 0.0 copy-done.6
  0.7 0.0 copy-start
  0.7 0.9 %copy-done = bf16[128,640]{1,0:T(8,128)(2,1)S(1)} copy-done((bf16[128,640]{1,0:T(8,128)(2,1)S(1)}, bf16[128,640]{1,0:T(8,128)(2,1)}, u32[]{:S(2)}) %copy-start) | copy-done | bytes 163864
  1.6 0.0 copy-start.2
  1.6 0.9 %copy-done.2 = bf16[4,128,128]{2,1,0:T(8,128)(2,1)S(1)} copy-done((bf16[4,128,128]{2,1,0:T(8,128)(2,1)S(1)}, bf16[4,128,128]{2,1,0:T(8,128)(2,1)}, u32[]{:S(2)}) %copy-start.2) | copy-done | bytes 131096
  2.5 1.1 %project.1 = (bf16[32,32,128]{2,1,0:T(8,128)(2,1)S(1)}, bf16[512,128]{1,0:T(8,128)(2,1)S(1)}) custom-call(s32[128]{0:T(128)S(1)} %copy-done.4, s32[1,128]{1,0:T(1,128)S(1)} %bitcast.5, bf16[4,128,128]{2,1,0:T(8,128)(2,1)S(1)} %copy-done.2, f32[1,128]{1,0:T(1,128)S(1)} %bitcast.6, f32[1,128]{1,0:T(1,128)S(1)} %bitcast.7, bf16[128,640]{1,0:T(8,128)(2,1)S(1)} %copy-done), custom_call_target="tpu_custom_call" | custom-call | tf_op jit(solution)/shard_map/project/pallas_call | solution.py:115
  3.6 17.7 %all_to_all.10.blocks_ref = bf16[32,32,128]{2,1,0:T(8,128)(2,1)S(1)} all-to-all(bf16[32,32,128]{2,1,0:T(8,128)(2,1)S(1)} %get-tuple-element.7), channel_id=1, replica_groups=mesh['parts'=1,'wide'=8,'narrow'=4,'sub'=1] {'wide','narrow'}, dimensions={0} | all-to-all | bytes 524288 | tf_op jit(solution)/shard_map/all_to_all | solution.py:123
  21.3 0.9 %contract.1 = bf16[32,16,128]{2,1,0:T(8,128)(2,1)} custom-call(bf16[32,32,128]{2,1,0:T(8,128)(2,1)S(1)} %all_to_all.10.blocks_ref), custom_call_target="tpu_custom_call" | custom-call | tf_op jit(solution)/shard_map/contract/pallas_call | solution.py:124
  22.2 2.7 %all-to-all-start.1 = ((bf16[32,16,128]{2,1,0:T(8,128)(2,1)}), bf16[32,16,128]{2,1,0:T(8,128)(2,1)S(1)}, u32[]{:S(2)}, u32[]{:S(2)}) async-start(bf16[32,16,128]{2,1,0:T(8,128)(2,1)} %contract.1), calls=%async_computation.1 | async-start | bytes 262144 | tf_op jit(solution)/shard_map/all_to_all | solution.py:133
  24.9 0.0 copy-done.1
  24.9 0.0 copy-start.3
  24.9 0.2 gate.1.gate_ref
  25.1 8.0 %all-to-all-done.1.blocks_ref = bf16[32,16,128]{2,1,0:T(8,128)(2,1)S(1)} async-done(((bf16[32,16,128]{2,1,0:T(8,128)(2,1)}), bf16[32,16,128]{2,1,0:T(8,128)(2,1)S(1)}, u32[]{:S(2)}, u32[]{:S(2)}) %all-to-all-start.1) | async-done | bytes 131104 | tf_op jit(solution)/shard_map/all_to_all | solution.py:133
  33.1 0.0 copy-start.7
  33.1 0.0 copy-start.8
  33.1 0.0 copy-done.3
  33.1 0.6 %copy-done.7 = f32[128]{0:T(128)S(1)} copy-done((f32[128]{0:T(128)S(1)}, f32[128]{0:T(128)}, u32[]{:S(2)}) %copy-start.7) | copy-done | bytes 536
  33.8 0.0 copy-done.8
  33.8 1.0 %finish.1 = bf16[4,128,128]{2,1,0:T(8,128)(2,1)} custom-call(bf16[32,16,128]{2,1,0:T(8,128)(2,1)S(1)} %all-to-all-done.1.blocks_ref, bf16[512,128]{1,0:T(8,128)(2,1)S(1)} %gate.1.gate_ref, f32[1,128]{1,0:T(1,128)S(1)} %bitcast.8, f32[1,128]{1,0:T(1,128)S(1)} %bitcast.9, bf16[128,128]{1,0:T(8,128)(2,1)S(1)} %copy-done.3), custom_call_target="tpu_custom_call" | custom-call | tf_op jit(solution)/shard_map/finish/pallas_call | solution.py:142
  (1 shorter events, 0.0 us)
Async XLA Ops:
  0.0 0.7 %copy-start.4 = (s32[128]{0:T(128)S(1)}, s32[128]{0:T(128)}, u32[]{:S(2)}) copy-start(s32[128]{0:T(128)} %flags_ref.1) | copy-start | bytes 1540
  0.0 0.7 %copy-start.5 = (f32[128]{0:T(128)S(1)}, f32[128]{0:T(128)}, u32[]{:S(2)}) copy-start(f32[128]{0:T(128)} %param.10) | copy-start | bytes 1540
  0.0 0.7 %copy-start.6 = (f32[128]{0:T(128)S(1)}, f32[128]{0:T(128)}, u32[]{:S(2)}) copy-start(f32[128]{0:T(128)} %param.11) | copy-start | bytes 1540
  0.7 0.9 %copy-start = (bf16[128,640]{1,0:T(8,128)(2,1)S(1)}, bf16[128,640]{1,0:T(8,128)(2,1)}, u32[]{:S(2)}) copy-start(bf16[128,640]{1,0:T(8,128)(2,1)} %w_ref.4) | copy-start | bytes 491524
  1.6 0.9 %copy-start.2 = (bf16[4,128,128]{2,1,0:T(8,128)(2,1)S(1)}, bf16[4,128,128]{2,1,0:T(8,128)(2,1)}, u32[]{:S(2)}) copy-start(bf16[4,128,128]{2,1,0:T(8,128)(2,1)} %pair_ref.1) | copy-start | bytes 393220
  22.2 2.7 %copy-start.1 = (bf16[128,640]{1,0:T(8,128)(2,1)S(1)}, bf16[128,640]{1,0:T(8,128)(2,1)}, u32[]{:S(2)}) copy-start(bf16[128,640]{1,0:T(8,128)(2,1)} %w_ref.4) | copy-start | bytes 491524
  22.2 10.9 %all-to-all-start.1 = ((bf16[32,16,128]{2,1,0:T(8,128)(2,1)}), bf16[32,16,128]{2,1,0:T(8,128)(2,1)S(1)}, u32[]{:S(2)}, u32[]{:S(2)}) async-start(bf16[32,16,128]{2,1,0:T(8,128)(2,1)} %contract.1), calls=%async_computation.1 | async-start | bytes 262144 | tf_op jit(solution)/shard_map/all_to_all | solution.py:133
  24.9 8.2 %copy-start.3 = (bf16[128,128]{1,0:T(8,128)(2,1)S(1)}, bf16[128,128]{1,0:T(8,128)(2,1)}, u32[]{:S(2)}) copy-start(bf16[128,128]{1,0:T(8,128)(2,1)} %w_ref.5) | copy-start | bytes 98308
  33.1 0.7 %copy-start.7 = (f32[128]{0:T(128)S(1)}, f32[128]{0:T(128)}, u32[]{:S(2)}) copy-start(f32[128]{0:T(128)} %param.13) | copy-start | bytes 1540
  33.1 0.7 %copy-start.8 = (f32[128]{0:T(128)S(1)}, f32[128]{0:T(128)}, u32[]{:S(2)}) copy-start(f32[128]{0:T(128)} %param.14) | copy-start | bytes 1540

commit v5 on v4

--- a/solution.py
+++ b/solution.py
@@ -27,20 +27,39 @@
     )
 
 
-def project_kernel(flags_ref, valid_ref, pair_ref, gain_ref, bias_ref, w_ref, out_ref, normed_ref):
+def project_kernel(
+    pair_hbm, valid_hbm, gain_hbm, bias_hbm, w_hbm, out_ref, normed_ref,
+    pair_ref, valid_ref, gain_ref, bias_ref, w_ref, sems,
+):
     row_count, col_count, chan_count = pair_ref.shape
+    fetches = [
+        pltpu.make_async_copy(source, held, sems.at[i])
+        for i, (source, held) in enumerate((
+            (pair_hbm, pair_ref), (gain_hbm, gain_ref), (bias_hbm, bias_ref),
+            (w_hbm.at[:, : 4 * chan_count], w_ref), (valid_hbm, valid_ref),
+        ))
+    ]
+    for fetch in fetches:
+        fetch.start()
     row_start = lax.axis_index(axes) * row_count
+    for fetch in fetches[:3]:
+        fetch.wait()
     tokens = pair_ref[...].reshape(row_count * col_count, chan_count).astype(jnp.float32)
     normed = layer_norm(tokens, gain_ref[...], bias_ref[...], 1).astype(jnp.bfloat16)
     normed_ref[...] = normed
+    for fetch in fetches[3:]:
+        fetch.wait()
     projected = lax.dot_general(
-        w_ref[:, : 4 * chan_count], normed, (((0,), (1,)), ((), ())),
+        w_ref[...], normed, (((0,), (1,)), ((), ())),
         preferred_element_type=jnp.float32,
     )
     col_flags = valid_ref[...].astype(jnp.float32)
-    flags = jnp.concatenate(
-        [col_flags * flags_ref[row_start + r].astype(jnp.float32) for r in range(row_count)], axis=1
-    )
+    places = lax.broadcasted_iota(jnp.int32, col_flags.shape, 1)
+    row_flags = [
+        jnp.sum(jnp.where(places == row_start + r, col_flags, 0.0), axis=1, keepdims=True)
+        for r in range(row_count)
+    ]
+    flags = jnp.concatenate([col_flags * row_flag for row_flag in row_flags], axis=1)
     for chan in range(0, chan_count, 8):
         a_gate, a, b_gate, b = (
             projected[i * chan_count + chan : i * chan_count + chan + 8] for i in range(4)
@@ -76,22 +95,23 @@
             out_ref[row // 4 + half] = rows.astype(jnp.bfloat16)
 
 
-def gate_kernel(normed_ref, w_ref, out_ref):
+def gate_kernel(normed_ref, w_ref, gain_ref, bias_ref, w_out_ref, out_ref, scales_ref, weights_ref):
     chan_count = normed_ref.shape[1]
     projected = jnp.dot(
         normed_ref[...], w_ref[:, 4 * chan_count :], preferred_element_type=jnp.float32
     )
     out_ref[...] = jax.nn.sigmoid(projected).astype(jnp.bfloat16)
-
-
-def finish_kernel(blocks_ref, gate_ref, gain_ref, bias_ref, w_ref, out_ref, held_ref):
+    for i, vector_ref in enumerate((gain_ref, bias_ref)):
+        scales_ref[i] = jnp.transpose(jnp.broadcast_to(vector_ref[...], scales_ref.shape[1:]))
+    weights_ref[...] = w_out_ref[...]
+
+
+def finish_kernel(blocks_ref, gate_ref, scales_ref, w_ref, out_ref, held_ref):
     row_count, col_count, chan_count = out_ref.shape
     held_ref[...] = blocks_ref[...].reshape(held_ref.shape).astype(jnp.float32)
-    gain = jnp.transpose(jnp.broadcast_to(gain_ref[...], (col_count, chan_count)))
-    bias = jnp.transpose(jnp.broadcast_to(bias_ref[...], (col_count, chan_count)))
     for r in range(row_count):
         triangle = held_ref[pl.ds(r, chan_count, stride=row_count), :]
-        normed = layer_norm(triangle, gain, bias, 0).astype(jnp.bfloat16)
+        normed = layer_norm(triangle, scales_ref[0], scales_ref[1], 0).astype(jnp.bfloat16)
         result = lax.dot_general(
             normed, w_ref[...], (((0,), (0,)), ((), ())), preferred_element_type=jnp.float32
         )
@@ -104,7 +124,7 @@
     shards = lax.axis_size(axes)
     tokens = row_count * col_count
     vmem = pl.BlockSpec(memory_space=pltpu.VMEM)
-    smem = pl.BlockSpec(memory_space=pltpu.SMEM)
+    hbm = pl.BlockSpec(memory_space=pltpu.HBM)
 
     def line(vector):
         return vector.reshape(1, -1)
@@ -115,11 +135,19 @@
     sides, normed = pl.pallas_call(
         project_kernel,
         out_shape=(shaped(shards, 8 * row_count, col_count), shaped(tokens, chan_count)),
-        in_specs=[smem] + [vmem] * 5,
+        in_specs=[hbm] * 5,
         out_specs=(vmem, vmem),
+        scratch_shapes=[
+            pltpu.VMEM(pair.shape, jnp.bfloat16),
+            pltpu.VMEM((1, col_count), jnp.int32),
+            pltpu.VMEM((1, chan_count), jnp.float32),
+            pltpu.VMEM((1, chan_count), jnp.float32),
+            pltpu.VMEM((chan_count, 4 * chan_count), jnp.bfloat16),
+            pltpu.SemaphoreType.DMA((5,)),
+        ],
         compiler_params=pltpu.CompilerParams(vmem_limit_bytes=kernel_vmem),
         name="project",
-    )(valid, line(valid), pair, line(norm_gain), line(norm_bias), w_proj)
+    )(pair, line(valid), line(norm_gain), line(norm_bias), w_proj)
     sides = lax.all_to_all(sides, axes, split_axis=0, concat_axis=0, tiled=True)
     triangle = pl.pallas_call(
         contract_kernel,
@@ -131,23 +159,27 @@
         name="contract",
     )(sides)
     triangle = lax.all_to_all(triangle, axes, split_axis=0, concat_axis=0, tiled=True)
-    gate_values = pl.pallas_call(
+    gate_values, scales, weights = pl.pallas_call(
         gate_kernel,
-        out_shape=shaped(tokens, chan_count),
-        in_specs=[vmem] * 2,
-        out_specs=vmem,
+        out_shape=(
+            shaped(tokens, chan_count),
+            jax.ShapeDtypeStruct((2, chan_count, col_count), jnp.float32),
+            shaped(chan_count, chan_count),
+        ),
+        in_specs=[vmem] * 5,
+        out_specs=(vmem,) * 3,
         compiler_params=pltpu.CompilerParams(vmem_limit_bytes=kernel_vmem),
         name="gate",
-    )(normed, w_proj)
+    )(normed, w_proj, line(out_gain), line(out_bias), w_out)
     return pl.pallas_call(
         finish_kernel,
         out_shape=shaped(row_count, col_count, chan_count),
-        in_specs=[vmem] * 5,
+        in_specs=[vmem] * 4,
         out_specs=vmem,
         scratch_shapes=[pltpu.VMEM((tokens, chan_count), jnp.float32)],
         compiler_params=pltpu.CompilerParams(vmem_limit_bytes=kernel_vmem),
         name="finish",
-    )(triangle, gate_values, line(out_gain), line(out_bias), w_out)
+    )(triangle, gate_values, scales, weights)
 
 
 def local_arrays(pair, valid, norm_gain, norm_bias, w_proj, out_gain, out_bias, w_out):

time: 35 us -> 34.1 us (0.974)
  waiting for transfers between devices: 8.02 us -> 7.37 us
    all_to_all x1, waiting for transfers between devices: 8.02 us -> 7.37 us  [local_blocks(): lax.all_to_all(triangle, axes, split_axis=0, concat_axis=0, tiled=True)]
where the time goes in v5:
time: 34.1 us; the launch traced here: 33.8 us
  blocking collectives  17.7 us (52%)
  waiting for transfers between devices  7.37 us (22%)
  local copies, waits for them, and re-layouts  3.15 us (9%)
  Pallas kernels  2.85 us (8%)
  starting transfers between devices  2.71 us (8%)
    all_to_all x1, blocking collectives, local_blocks(): sides = lax.all_to_all(sides, axes, split_axis=0, concat_axis=0, tiled=True)  17.7 us
    all_to_all x1, waiting for transfers between devices, local_blocks(): lax.all_to_all(triangle, axes, split_axis=0, concat_axis=0, tiled=True)  7.37 us
    unnamed x18, local copies, waits for them, and re-layouts  3.15 us
    all_to_all x1, starting transfers between devices, local_blocks(): lax.all_to_all(triangle, axes, split_axis=0, concat_axis=0, tiled=True)  2.71 us
    pallas_call x1, Pallas kernels, local_blocks(): pl.pallas_call(finish_kernel, out_shape=shaped(row_count, col_count, chan...  0.97 us
    pallas_call x1, Pallas kernels, local_blocks(): pl.pallas_call(contract_kernel, out_shape=shaped(shards, 4 * row_count, c...  0.9 us
    pallas_call x1, Pallas kernels, local_blocks(): pl.pallas_call(project_kernel, out_shape=(shaped(shards, 8 * row_count, c...  0.81 us
  transfers between devices with their start and end apart: 1, of which 1 were waited for; matrix products, arithmetic and copies ran while one was open for 0% of the time, Pallas kernels for 1%

profile of v5, /device:TPU:0, one launch (start us, length us, event | category | flops | bytes accessed | tf_op | source)
XLA Modules:
  0.0 33.8 jit_solution(16511011784661691631)
XLA Ops:
  0.0 0.0 copy-start.5
  0.0 0.0 copy-start.6
  0.0 0.6 %copy-done.4 = s32[128]{0:T(128)S(1)} copy-done((s32[128]{0:T(128)S(1)}, s32[128]{0:T(128)}, u32[]{:S(2)}) %copy-start.4) | copy-done | bytes 536
  0.7 0.0 copy-done.5
  0.7 0.0 copy-done.6
  0.7 0.0 copy-start
  0.7 0.9 %copy-done = bf16[128,640]{1,0:T(8,128)(2,1)S(1)} copy-done((bf16[128,640]{1,0:T(8,128)(2,1)S(1)}, bf16[128,640]{1,0:T(8,128)(2,1)}, u32[]{:S(2)}) %copy-start) | copy-done | bytes 163864
  1.6 0.0 copy-start.2
  1.6 0.9 %copy-done.2 = bf16[4,128,128]{2,1,0:T(8,128)(2,1)S(1)} copy-done((bf16[4,128,128]{2,1,0:T(8,128)(2,1)S(1)}, bf16[4,128,128]{2,1,0:T(8,128)(2,1)}, u32[]{:S(2)}) %copy-start.2) | copy-done | bytes 131096
  2.5 0.8 %project.1 = (bf16[32,32,128]{2,1,0:T(8,128)(2,1)S(1)}, bf16[512,128]{1,0:T(8,128)(2,1)S(1)}) custom-call(bf16[4,128,128]{2,1,0:T(8,128)(2,1)S(1)} %copy-done.2, s32[1,128]{1,0:T(1,128)S(1)} %bitcast.5, f32[1,128]{1,0:T(1,128)S(1)} %bitcast.6, f32[1,128]{1,0:T(1,128)S(1)} %bitcast.7, bf16[128,640]{1,0:T(8,128)(2,1)S(1)} %copy-done), custom_call_target="tpu_custom_call" | custom-call | tf_op jit(solution)/shard_map/project/pallas_call | solution.py:135
  3.3 17.7 %all_to_all.10.blocks_ref = bf16[32,32,128]{2,1,0:T(8,128)(2,1)S(1)} all-to-all(bf16[32,32,128]{2,1,0:T(8,128)(2,1)S(1)} %get-tuple-element.10), channel_id=1, replica_groups=mesh['parts'=1,'wide'=8,'narrow'=4,'sub'=1] {'wide','narrow'}, dimensions={0} | all-to-all | bytes 524288 | tf_op jit(solution)/shard_map/all_to_all | solution.py:151
  21.0 0.9 %contract.1 = bf16[32,16,128]{2,1,0:T(8,128)(2,1)} custom-call(bf16[32,32,128]{2,1,0:T(8,128)(2,1)S(1)} %all_to_all.10.blocks_ref), custom_call_target="tpu_custom_call" | custom-call | tf_op jit(solution)/shard_map/contract/pallas_call | solution.py:152
  21.9 0.0 copy-start.1
  21.9 0.0 copy-start.3
  21.9 2.7 %all-to-all-start.1 = ((bf16[32,16,128]{2,1,0:T(8,128)(2,1)}), bf16[32,16,128]{2,1,0:T(8,128)(2,1)S(1)}, u32[]{:S(2)}, u32[]{:S(2)}) async-start(bf16[32,16,128]{2,1,0:T(8,128)(2,1)} %contract.1), calls=%async_computation.1 | async-start | bytes 262144 | tf_op jit(solution)/shard_map/all_to_all | solution.py:161
  24.6 0.0 copy-start.7
  24.7 0.0 copy-start.8
  24.7 0.0 copy-done.1
  24.7 0.0 copy-done.3
  24.7 0.6 %copy-done.7 = f32[128]{0:T(128)S(1)} copy-done((f32[128]{0:T(128)S(1)}, f32[128]{0:T(128)}, u32[]{:S(2)}) %copy-start.7) | copy-done | bytes 536
  25.3 0.0 copy-done.8
  25.3 0.2 gate.1
  25.5 7.4 %all-to-all-done.1.blocks_ref = bf16[32,16,128]{2,1,0:T(8,128)(2,1)S(1)} async-done(((bf16[32,16,128]{2,1,0:T(8,128)(2,1)}), bf16[32,16,128]{2,1,0:T(8,128)(2,1)S(1)}, u32[]{:S(2)}, u32[]{:S(2)}) %all-to-all-start.1) | async-done | bytes 131104 | tf_op jit(solution)/shard_map/all_to_all | solution.py:161
  32.9 1.0 %finish.1 = bf16[4,128,128]{2,1,0:T(8,128)(2,1)} custom-call(bf16[32,16,128]{2,1,0:T(8,128)(2,1)S(1)} %all-to-all-done.1.blocks_ref, bf16[512,128]{1,0:T(8,128)(2,1)S(1)} %get-tuple-element.12.gate_ref, f32[2,128,128]{2,1,0:T(8,128)S(1)} %get-tuple-element.13.scales_ref, bf16[128,128]{1,0:T(8,128)(2,1)S(1)} %get-tuple-element.14.w_ref), custom_call_target="tpu_custom_call" | custom-call | tf_op jit(solution)/shard_map/finish/pallas_call | solution.py:174
  (1 shorter events, 0.0 us)
Async XLA Ops:
  0.0 0.7 %copy-start.4 = (s32[128]{0:T(128)S(1)}, s32[128]{0:T(128)}, u32[]{:S(2)}) copy-start(s32[128]{0:T(128)} %param.9) | copy-start | bytes 1540
  0.0 0.7 %copy-start.5 = (f32[128]{0:T(128)S(1)}, f32[128]{0:T(128)}, u32[]{:S(2)}) copy-start(f32[128]{0:T(128)} %param.10) | copy-start | bytes 1540
  0.0 0.7 %copy-start.6 = (f32[128]{0:T(128)S(1)}, f32[128]{0:T(128)}, u32[]{:S(2)}) copy-start(f32[128]{0:T(128)} %param.11) | copy-start | bytes 1540
  0.7 0.9 %copy-start = (bf16[128,640]{1,0:T(8,128)(2,1)S(1)}, bf16[128,640]{1,0:T(8,128)(2,1)}, u32[]{:S(2)}) copy-start(bf16[128,640]{1,0:T(8,128)(2,1)} %w_ref.1) | copy-start | bytes 491524
  1.6 0.9 %copy-start.2 = (bf16[4,128,128]{2,1,0:T(8,128)(2,1)S(1)}, bf16[4,128,128]{2,1,0:T(8,128)(2,1)}, u32[]{:S(2)}) copy-start(bf16[4,128,128]{2,1,0:T(8,128)(2,1)} %pair_hbm.1) | copy-start | bytes 393220
  21.9 2.7 %copy-start.1 = (bf16[128,640]{1,0:T(8,128)(2,1)S(1)}, bf16[128,640]{1,0:T(8,128)(2,1)}, u32[]{:S(2)}) copy-start(bf16[128,640]{1,0:T(8,128)(2,1)} %w_ref.1) | copy-start | bytes 491524
  21.9 2.8 %copy-start.3 = (bf16[128,128]{1,0:T(8,128)(2,1)S(1)}, bf16[128,128]{1,0:T(8,128)(2,1)}, u32[]{:S(2)}) copy-start(bf16[128,128]{1,0:T(8,128)(2,1)} %w_out_ref.1) | copy-start | bytes 98308
  21.9 10.9 %all-to-all-start.1 = ((bf16[32,16,128]{2,1,0:T(8,128)(2,1)}), bf16[32,16,128]{2,1,0:T(8,128)(2,1)S(1)}, u32[]{:S(2)}, u32[]{:S(2)}) async-start(bf16[32,16,128]{2,1,0:T(8,128)(2,1)} %contract.1), calls=%async_computation.1 | async-start | bytes 262144 | tf_op jit(solution)/shard_map/all_to_all | solution.py:161
  24.6 0.7 %copy-start.7 = (f32[128]{0:T(128)S(1)}, f32[128]{0:T(128)}, u32[]{:S(2)}) copy-start(f32[128]{0:T(128)} %param.13) | copy-start | bytes 1540
  24.7 0.7 %copy-start.8 = (f32[128]{0:T(128)S(1)}, f32[128]{0:T(128)}, u32[]{:S(2)}) copy-start(f32[128]{0:T(128)} %param.14) | copy-start | bytes 1540

commit v6 on v5

--- a/solution.py
+++ b/solution.py
@@ -145,7 +145,6 @@
             pltpu.VMEM((chan_count, 4 * chan_count), jnp.bfloat16),
             pltpu.SemaphoreType.DMA((5,)),
         ],
-        compiler_params=pltpu.CompilerParams(vmem_limit_bytes=kernel_vmem),
         name="project",
     )(pair, line(valid), line(norm_gain), line(norm_bias), w_proj)
     sides = lax.all_to_all(sides, axes, split_axis=0, concat_axis=0, tiled=True)

time: 34.1 us -> 33.2 us (0.974)
  local copies, waits for them, and re-layouts: 3.15 us -> 0.64 us
  Pallas kernels: 2.85 us -> 4.28 us
    unnamed x18 -> x10, local copies, waits for them, and re-layouts: 3.15 us -> 0.64 us
    pallas_call x1, Pallas kernels: 0.81 us -> 2.24 us  [local_blocks(): pl.pallas_call(project_kernel, out_shape=(shaped(shards, 8 * row_count, c...]
where the time goes in v6:
time: 33.2 us; the launch traced here: 33 us
  blocking collectives  17.9 us (54%)
  waiting for transfers between devices  7.37 us (22%)
  Pallas kernels  4.28 us (13%)
  starting transfers between devices  2.7 us (8%)
  local copies, waits for them, and re-layouts  0.64 us (2%)
    all_to_all x1, blocking collectives, local_blocks(): sides = lax.all_to_all(sides, axes, split_axis=0, concat_axis=0, tiled=True)  17.9 us
    all_to_all x1, waiting for transfers between devices, local_blocks(): lax.all_to_all(triangle, axes, split_axis=0, concat_axis=0, tiled=True)  7.37 us
    all_to_all x1, starting transfers between devices, local_blocks(): lax.all_to_all(triangle, axes, split_axis=0, concat_axis=0, tiled=True)  2.7 us
    pallas_call x1, Pallas kernels, local_blocks(): pl.pallas_call(project_kernel, out_shape=(shaped(shards, 8 * row_count, c...  2.24 us
    pallas_call x1, Pallas kernels, local_blocks(): pl.pallas_call(finish_kernel, out_shape=shaped(row_count, col_count, chan...  0.97 us
    pallas_call x1, Pallas kernels, local_blocks(): pl.pallas_call(contract_kernel, out_shape=shaped(shards, 4 * row_count, c...  0.89 us
  transfers between devices with their start and end apart: 1, of which 1 were waited for; matrix products, arithmetic and copies ran while one was open for 0% of the time, Pallas kernels for 1%

profile of v6, /device:TPU:0, one launch (start us, length us, event | category | flops | bytes accessed | tf_op | source)
XLA Modules:
  0.0 33.0 jit_solution(8717615544836444889)
XLA Ops:
  0.0 2.2 %project.1 = (bf16[32,32,128]{2,1,0:T(8,128)(2,1)}, bf16[512,128]{1,0:T(8,128)(2,1)}) custom-call(bf16[4,128,128]{2,1,0:T(8,128)(2,1)} %pair_hbm.1, s32[1,128]{1,0:T(1,128)} %bitcast.7, f32[1,128]{1,0:T(1,128)} %bitcast.8, f32[1,128]{1,0:T(1,128)} %bitcast.9, bf16[128,640]{1,0:T(8,128)(2,1)} %w_ref.1), custom_call_target="tpu_custom_call" | custom-call | tf_op jit(solution)/shard_map/project/pallas_call | solution.py:135
  2.3 17.9 %all_to_all.10.blocks_ref = bf16[32,32,128]{2,1,0:T(8,128)(2,1)S(1)} all-to-all(bf16[32,32,128]{2,1,0:T(8,128)(2,1)} %get-tuple-element.10), channel_id=1, replica_groups=mesh['parts'=1,'wide'=8,'narrow'=4,'sub'=1] {'wide','narrow'}, dimensions={0} | all-to-all | bytes 524288 | tf_op jit(solution)/shard_map/all_to_all | solution.py:150
  20.2 0.0 copy-start.1
  20.2 0.9 %contract.1 = bf16[32,16,128]{2,1,0:T(8,128)(2,1)} custom-call(bf16[32,32,128]{2,1,0:T(8,128)(2,1)S(1)} %all_to_all.10.blocks_ref), custom_call_target="tpu_custom_call" | custom-call | tf_op jit(solution)/shard_map/contract/pallas_call | solution.py:151
  21.1 0.0 copy-start
  21.1 0.0 copy-start.2
  21.1 2.7 %all-to-all-start.1 = ((bf16[32,16,128]{2,1,0:T(8,128)(2,1)}), bf16[32,16,128]{2,1,0:T(8,128)(2,1)S(1)}, u32[]{:S(2)}, u32[]{:S(2)}) async-start(bf16[32,16,128]{2,1,0:T(8,128)(2,1)} %contract.1), calls=%async_computation.1 | async-start | bytes 262144 | tf_op jit(solution)/shard_map/all_to_all | solution.py:160
  23.8 0.0 copy-start.3
  23.8 0.0 copy-start.4
  23.8 0.0 copy-done.1
  23.8 0.0 copy-done
  23.8 0.0 copy-done.2
  23.8 0.6 %copy-done.3 = f32[128]{0:T(128)S(1)} copy-done((f32[128]{0:T(128)S(1)}, f32[128]{0:T(128)}, u32[]{:S(2)}) %copy-start.3) | copy-done | bytes 536
  24.4 0.0 copy-done.4
  24.4 0.2 gate.1
  24.6 7.4 %all-to-all-done.1.blocks_ref = bf16[32,16,128]{2,1,0:T(8,128)(2,1)S(1)} async-done(((bf16[32,16,128]{2,1,0:T(8,128)(2,1)}), bf16[32,16,128]{2,1,0:T(8,128)(2,1)S(1)}, u32[]{:S(2)}, u32[]{:S(2)}) %all-to-all-start.1) | async-done | bytes 131104 | tf_op jit(solution)/shard_map/all_to_all | solution.py:160
  32.0 1.0 %finish.1 = bf16[4,128,128]{2,1,0:T(8,128)(2,1)} custom-call(bf16[32,16,128]{2,1,0:T(8,128)(2,1)S(1)} %all-to-all-done.1.blocks_ref, bf16[512,128]{1,0:T(8,128)(2,1)S(1)} %get-tuple-element.12.gate_ref, f32[2,128,128]{2,1,0:T(8,128)S(1)} %get-tuple-element.13.scales_ref, bf16[128,128]{1,0:T(8,128)(2,1)S(1)} %get-tuple-element.14.w_ref), custom_call_target="tpu_custom_call" | custom-call | tf_op jit(solution)/shard_map/finish/pallas_call | solution.py:173
Async XLA Ops:
  20.2 3.6 %copy-start.1 = (bf16[512,128]{1,0:T(8,128)(2,1)S(1)}, bf16[512,128]{1,0:T(8,128)(2,1)}, u32[]{:S(2)}) copy-start(bf16[512,128]{1,0:T(8,128)(2,1)} %get-tuple-element.11.normed_ref) | copy-start | bytes 393220
  21.1 2.8 %copy-start = (bf16[128,640]{1,0:T(8,128)(2,1)S(1)}, bf16[128,640]{1,0:T(8,128)(2,1)}, u32[]{:S(2)}) copy-start(bf16[128,640]{1,0:T(8,128)(2,1)} %w_ref.1) | copy-start | bytes 491524
  21.1 2.8 %copy-start.2 = (bf16[128,128]{1,0:T(8,128)(2,1)S(1)}, bf16[128,128]{1,0:T(8,128)(2,1)}, u32[]{:S(2)}) copy-start(bf16[128,128]{1,0:T(8,128)(2,1)} %w_out_ref.1) | copy-start | bytes 98308
  21.1 10.9 %all-to-all-start.1 = ((bf16[32,16,128]{2,1,0:T(8,128)(2,1)}), bf16[32,16,128]{2,1,0:T(8,128)(2,1)S(1)}, u32[]{:S(2)}, u32[]{:S(2)}) async-start(bf16[32,16,128]{2,1,0:T(8,128)(2,1)} %contract.1), calls=%async_computation.1 | async-start | bytes 262144 | tf_op jit(solution)/shard_map/all_to_all | solution.py:160
  23.8 0.7 %copy-start.3 = (f32[128]{0:T(128)S(1)}, f32[128]{0:T(128)}, u32[]{:S(2)}) copy-start(f32[128]{0:T(128)} %param.13) | copy-start | bytes 1540
  23.8 0.7 %copy-start.4 = (f32[128]{0:T(128)S(1)}, f32[128]{0:T(128)}, u32[]{:S(2)}) copy-start(f32[128]{0:T(128)} %param.14) | copy-start | bytes 1540

commit v7 on v6

--- a/solution.py
+++ b/solution.py
@@ -10,6 +10,7 @@
 epsilon = 1e-05
 axes = ("wide", "narrow")
 kernel_vmem = 8 * 2**20
+places = 4
 
 
 def layer_norm(values, gain_vec, bias_vec, axis_dim):
@@ -27,11 +28,39 @@
     )
 
 
+def plane_place():
+    return lax.rem(lax.axis_index("wide"), 2) * 2 + lax.axis_index("narrow") // 2
+
+
+def ring_place(position):
+    return position ^ (position >> 1)
+
+
+def send_blocks(held_ref, out_refs):
+    for s, out_ref in enumerate(out_refs):
+        out_ref[...] = held_ref[plane_place() ^ s]
+
+
+def receive_blocks(block_refs, held_ref):
+    rows = block_refs[0].shape[0]
+    for s, block_ref in enumerate(block_refs):
+        start = pl.multiple_of((plane_place() ^ s) * rows, rows)
+        held_ref[pl.ds(start, rows), :] = block_ref[...].astype(jnp.float32)
+
+
+def pack_rows(held_ref, out_ref):
+    chans, rows, _ = out_ref.shape
+    for c in range(chans):
+        out_ref[c] = held_ref[pl.ds(c, rows, stride=chans), :].astype(jnp.bfloat16)
+
+
 def project_kernel(
-    pair_hbm, valid_hbm, gain_hbm, bias_hbm, w_hbm, out_ref, normed_ref,
-    pair_ref, valid_ref, gain_ref, bias_ref, w_ref, sems,
+    pair_hbm, valid_hbm, gain_hbm, bias_hbm, w_hbm, normed_ref, left_ref, *rest
 ):
+    right_refs, rest = rest[:places], rest[places:]
+    right_ref, pair_ref, valid_ref, gain_ref, bias_ref, w_ref, sems = rest
     row_count, col_count, chan_count = pair_ref.shape
+    group = chan_count // places
     fetches = [
         pltpu.make_async_copy(source, held, sems.at[i])
         for i, (source, held) in enumerate((
@@ -49,50 +78,57 @@
     normed_ref[...] = normed
     for fetch in fetches[3:]:
         fetch.wait()
-    projected = lax.dot_general(
-        w_ref[...], normed, (((0,), (1,)), ((), ())),
-        preferred_element_type=jnp.float32,
-    )
     col_flags = valid_ref[...].astype(jnp.float32)
-    places = lax.broadcasted_iota(jnp.int32, col_flags.shape, 1)
+    columns = lax.broadcasted_iota(jnp.int32, col_flags.shape, 1)
     row_flags = [
-        jnp.sum(jnp.where(places == row_start + r, col_flags, 0.0), axis=1, keepdims=True)
+        jnp.sum(jnp.where(columns == row_start + r, col_flags, 0.0), axis=1, keepdims=True)
         for r in range(row_count)
     ]
     flags = jnp.concatenate([col_flags * row_flag for row_flag in row_flags], axis=1)
-    for chan in range(0, chan_count, 8):
-        a_gate, a, b_gate, b = (
-            projected[i * chan_count + chan : i * chan_count + chan + 8] for i in range(4)
+    for first, out_ref in ((2, right_ref), (0, left_ref)):
+        projected = lax.dot_general(
+            w_ref[:, first * chan_count : (first + 2) * chan_count], normed,
+            (((0,), (1,)), ((), ())), preferred_element_type=jnp.float32,
         )
-        left = jax.nn.sigmoid(a_gate) * a * flags
-        right = jax.nn.sigmoid(b_gate) * b * flags
-        for half, block in enumerate(swap_halves(left, right)):
-            for r in range(0, row_count, 2):
-                rows = jnp.concatenate(
-                    [block[:, (r + i) * col_count : (r + i + 1) * col_count] for i in range(2)], axis=0
-                )
-                out_ref[chan // 4 + half, r * 8 : (r + 2) * 8, :] = rows.astype(jnp.bfloat16)
-
-
-def contract_kernel(blocks_ref, out_ref, held_ref):
-    shards, block_rows, cols = blocks_ref.shape
-    total = held_ref.shape[0] // 8
-    held_ref[...] = blocks_ref[...].reshape(shards * block_rows, cols).astype(jnp.float32)
-    products = []
-    for c in range(4):
-        left = held_ref[pl.ds(c, total, stride=8), :].astype(jnp.bfloat16)
-        right = held_ref[pl.ds(4 + c, total, stride=8), :].astype(jnp.bfloat16)
-        products.append(
+        side = jax.nn.sigmoid(projected[:chan_count]) * projected[chan_count:] * flags
+        side = side.astype(jnp.bfloat16)
+        for place in range(places):
+            for r in range(row_count):
+                out_ref[place, r * group : (r + 1) * group, :] = side[
+                    place * group : (place + 1) * group, r * col_count : (r + 1) * col_count
+                ]
+    send_blocks(right_ref, right_refs)
+
+
+def pack_kernel(left_ref, *refs):
+    right_refs, (packed_ref, *left_refs), held_ref = refs[:places], refs[places:-1], refs[-1]
+    receive_blocks(right_refs, held_ref)
+    pack_rows(held_ref, packed_ref)
+    send_blocks(left_ref, left_refs)
+
+
+def contract_kernel(*refs):
+    left_refs, right_refs = refs[:places], refs[places : 2 * places + places]
+    out_refs, (left_held, packed_ref, out_ref) = refs[3 * places : 4 * places], refs[4 * places :]
+    receive_blocks(left_refs, left_held)
+    pack_rows(left_held, packed_ref)
+    for chan in range(0, packed_ref.shape[0], 4):
+        products = [
             lax.dot_general(
-                left, right, (((1,), (1,)), ((), ())), preferred_element_type=jnp.float32
+                packed_ref[c],
+                jnp.concatenate([right_ref[c] for right_ref in right_refs], axis=0),
+                (((1,), (1,)), ((), ())),
+                preferred_element_type=jnp.float32,
             )
-        )
-    for row in range(0, total, 8):
-        pieces = [product[row : row + 8] for product in products]
-        low, high = swap_halves(pieces[0], pieces[1]), swap_halves(pieces[2], pieces[3])
-        for half in range(2):
-            rows = jnp.concatenate([low[half], high[half]], axis=0)
-            out_ref[row // 4 + half] = rows.astype(jnp.bfloat16)
+            for c in range(chan, chan + 4)
+        ]
+        for row in range(0, packed_ref.shape[1], 8):
+            pieces = [product[row : row + 8] for product in products]
+            low, high = swap_halves(pieces[0], pieces[1]), swap_halves(pieces[2], pieces[3])
+            for half in range(2):
+                rows = jnp.concatenate([low[half], high[half]], axis=0).astype(jnp.bfloat16)
+                out_ref[row // 4 + half, chan * 4 : (chan + 4) * 4, :] = rows
+    send_blocks(out_ref, out_refs)
 
 
 def gate_kernel(normed_ref, w_ref, gain_ref, bias_ref, w_out_ref, out_ref, scales_ref, weights_ref):
@@ -106,17 +142,54 @@
     weights_ref[...] = w_out_ref[...]
 
 
-def finish_kernel(blocks_ref, gate_ref, scales_ref, w_ref, out_ref, held_ref):
+def finish_kernel(gate_ref, scales_ref, w_ref, *refs):
+    block_refs, out_ref, held_ref = refs[:places], refs[places], refs[places + 1]
     row_count, col_count, chan_count = out_ref.shape
-    held_ref[...] = blocks_ref[...].reshape(held_ref.shape).astype(jnp.float32)
+    receive_blocks(block_refs, held_ref)
+    plane_rows = 2 * places * row_count
+    planes = col_count // plane_rows
+    position = ring_place(lax.axis_index("wide") // 2)
+    even_core = lax.rem(lax.axis_index("narrow"), 2) == 0
     for r in range(row_count):
         triangle = held_ref[pl.ds(r, chan_count, stride=row_count), :]
         normed = layer_norm(triangle, scales_ref[0], scales_ref[1], 0).astype(jnp.bfloat16)
         result = lax.dot_general(
             normed, w_ref[...], (((0,), (0,)), ((), ())), preferred_element_type=jnp.float32
         )
-        gate = gate_ref[r * col_count : (r + 1) * col_count, :].astype(jnp.float32)
-        out_ref[r] = (gate * result).astype(jnp.bfloat16)
+        for step in range(planes):
+            own, other = (
+                result[step * plane_rows + i * plane_rows // 2 :][: plane_rows // 2] for i in range(2)
+            )
+            low, high = jnp.where(even_core, own, other), jnp.where(even_core, other, own)
+            rows = []
+            for row in range(0, plane_rows // 2, 8):
+                rows.extend(swap_halves(low[row : row + 8], high[row : row + 8]))
+            rows = jnp.concatenate(rows, axis=0)
+            plane = ring_place(lax.rem(position + planes - step, planes))
+            start = pl.multiple_of(plane * plane_rows, plane_rows)
+            gate = gate_ref[r, pl.ds(start, plane_rows), :].astype(jnp.float32)
+            out_ref[r, pl.ds(start, plane_rows), :] = (gate * rows).astype(jnp.bfloat16)
+
+
+def exchange(blocks, shards):
+    return [
+        lax.ppermute(block, axes, [(i, i ^ (2 * s)) for i in range(shards)]) if s else block
+        for s, block in enumerate(blocks)
+    ]
+
+
+def to_other_core(block, shards):
+    return lax.ppermute(block, axes, [(i, i ^ 1) for i in range(shards)])
+
+
+def to_next_plane(block, shards):
+    size = 2 * places
+    planes = shards // size
+    perm = []
+    for position in range(planes):
+        here, there = ring_place(position), ring_place((position + 1) % planes)
+        perm.extend((here * size + q, there * size + q) for q in range(size))
+    return lax.ppermute(block, axes, perm)
 
 
 def local_blocks(pair, valid, norm_gain, norm_bias, w_proj, out_gain, out_bias, w_out):
@@ -132,12 +205,20 @@
     def shaped(*dims):
         return jax.ShapeDtypeStruct(dims, jnp.bfloat16)
 
-    sides, normed = pl.pallas_call(
+    group = chan_count // places
+    block = shaped(row_count * group, col_count)
+    packed = shaped(group, places * row_count, col_count)
+    limit = pltpu.CompilerParams(vmem_limit_bytes=kernel_vmem)
+    held_blocks = pltpu.VMEM((places,) + block.shape, jnp.bfloat16)
+    held_rows = pltpu.VMEM((places * block.shape[0], col_count), jnp.float32)
+
+    normed, left, *right = pl.pallas_call(
         project_kernel,
-        out_shape=(shaped(shards, 8 * row_count, col_count), shaped(tokens, chan_count)),
+        out_shape=[shaped(tokens, chan_count), shaped(places, *block.shape)] + [block] * places,
         in_specs=[hbm] * 5,
-        out_specs=(vmem, vmem),
+        out_specs=[vmem] * (2 + places),
         scratch_shapes=[
+            held_blocks,
             pltpu.VMEM(pair.shape, jnp.bfloat16),
             pltpu.VMEM((1, col_count), jnp.int32),
             pltpu.VMEM((1, chan_count), jnp.float32),
@@ -147,17 +228,31 @@
         ],
         name="project",
     )(pair, line(valid), line(norm_gain), line(norm_bias), w_proj)
-    sides = lax.all_to_all(sides, axes, split_axis=0, concat_axis=0, tiled=True)
+    right, *left = pl.pallas_call(
+        pack_kernel,
+        out_shape=[packed] + [block] * places,
+        in_specs=[vmem] * (1 + places),
+        out_specs=[vmem] * (1 + places),
+        scratch_shapes=[held_rows],
+        compiler_params=limit,
+        name="pack",
+    )(left, *exchange(right, shards))
+    rights = []
+    for step in range(shards // (2 * places)):
+        if step:
+            right = to_next_plane(right, shards)
+        rights += [right, to_other_core(right, shards)]
+    left = exchange(left, shards)
     triangle = pl.pallas_call(
         contract_kernel,
-        out_shape=shaped(shards, 4 * row_count, col_count),
-        in_specs=[vmem],
-        out_specs=vmem,
-        scratch_shapes=[pltpu.VMEM((8 * col_count, col_count), jnp.float32)],
-        compiler_params=pltpu.CompilerParams(vmem_limit_bytes=kernel_vmem),
+        out_shape=[block] * places,
+        in_specs=[vmem] * (places + len(rights)),
+        out_specs=[vmem] * places,
+        scratch_shapes=[held_rows, pltpu.VMEM(packed.shape, jnp.bfloat16), held_blocks],
+        compiler_params=limit,
         name="contract",
-    )(sides)
-    triangle = lax.all_to_all(triangle, axes, split_axis=0, concat_axis=0, tiled=True)
+    )(*left, *rights)
+    triangle = exchange(triangle, shards)
     gate_values, scales, weights = pl.pallas_call(
         gate_kernel,
         out_shape=(
@@ -167,18 +262,18 @@
         ),
         in_specs=[vmem] * 5,
         out_specs=(vmem,) * 3,
-        compiler_params=pltpu.CompilerParams(vmem_limit_bytes=kernel_vmem),
+        compiler_params=limit,
         name="gate",
     )(normed, w_proj, line(out_gain), line(out_bias), w_out)
     return pl.pallas_call(
         finish_kernel,
         out_shape=shaped(row_count, col_count, chan_count),
-        in_specs=[vmem] * 4,
+        in_specs=[vmem] * (3 + places),
         out_specs=vmem,
-        scratch_shapes=[pltpu.VMEM((tokens, chan_count), jnp.float32)],
-        compiler_params=pltpu.CompilerParams(vmem_limit_bytes=kernel_vmem),
+        scratch_shapes=[held_rows],
+        compiler_params=limit,
         name="finish",
-    )(triangle, gate_values, scales, weights)
+    )(gate_values.reshape(pair.shape), scales, weights, *triangle)
 
 
 def local_arrays(pair, valid, norm_gain, norm_bias, w_proj, out_gain, out_bias, w_out):
@@ -226,12 +321,10 @@
 
 def local(pair, *rest):
     row_count, col_count, chan_count = pair.shape
-    shards = lax.axis_size(axes)
     fits = (
         lax.axis_size("sub") == 1
+        and (lax.axis_size("wide"), lax.axis_size("narrow")) == (8, 4)
         and (row_count, col_count, chan_count) == (4, 128, 128)
-        and shards * row_count == col_count
-        and shards * 4 == chan_count
     )
     return (local_blocks if fits else local_arrays)(pair, *rest)
 

time: 33.2 us -> 52.1 us (1.57)
  waiting for transfers between devices: 7.37 us -> 32.3 us
  blocking collectives: 17.9 us -> 0 us
  starting transfers between devices: 2.7 us -> 13 us
  local copies, waits for them, and re-layouts: 0.64 us -> 2.33 us
    ppermute x0 -> x16, waiting for transfers between devices: none -> 32.3 us  [the longest x9 17.7 us: exchange(): lax.ppermute(block, axes, [(i, i ^ 2 * s) for i in range(shards)])]
    all_to_all x1 -> x0, blocking collectives: 17.9 us -> none  [local_blocks(): sides = lax.all_to_all(sides, axes, split_axis=0, concat_axis=0, tiled=True)]
    ppermute x0 -> x16, starting transfers between devices: none -> 13 us  [the longest x9 9.22 us: exchange(): lax.ppermute(block, axes, [(i, i ^ 2 * s) for i in range(shards)])]
    all_to_all x1 -> x0, waiting for transfers between devices: 7.37 us -> none  [local_blocks(): lax.all_to_all(triangle, axes, split_axis=0, concat_axis=0, tiled=True)]
    all_to_all x1 -> x0, starting transfers between devices: 2.7 us -> none  [local_blocks(): lax.all_to_all(triangle, axes, split_axis=0, concat_axis=0, tiled=True)]
    unnamed x10 -> x14, local copies, waits for them, and re-layouts: 0.64 us -> 2.33 us
    pallas_call x2 -> x3, Pallas kernels: 3.14 us -> 3.04 us  [the longest x1 2.18 us: local_blocks(): pl.pallas_call(project_kernel, out_shape=[shaped(tokens, chan_count), sha...]
  transfers between devices with their start and end apart: 1 -> 16, of which waited for: 1 -> 11; matrix products, arithmetic and copies ran while one was open for 0% -> 0% of each run, Pallas kernels for 1% -> 0%
where the time goes in v7:
time: 52.1 us; the launch traced here: 51.9 us
  waiting for transfers between devices  32.3 us (62%)
  starting transfers between devices  13 us (25%)
  Pallas kernels  4.2 us (8%)
  local copies, waits for them, and re-layouts  2.33 us (4%)
    ppermute x9, waiting for transfers between devices, exchange(): lax.ppermute(block, axes, [(i, i ^ 2 * s) for i in range(shards)])  17.7 us
    ppermute x3, waiting for transfers between devices, to_next_plane(): return lax.ppermute(block, axes, perm)  14.6 us
    ppermute x9, starting transfers between devices, exchange(): lax.ppermute(block, axes, [(i, i ^ 2 * s) for i in range(shards)])  9.22 us
    ppermute x3, starting transfers between devices, to_next_plane(): return lax.ppermute(block, axes, perm)  3.25 us
    unnamed x14, local copies, waits for them, and re-layouts  2.33 us
    pallas_call x1, Pallas kernels, local_blocks(): pl.pallas_call(project_kernel, out_shape=[shaped(tokens, chan_count), sha...  2.18 us
  transfers between devices with their start and end apart: 16, of which 11 were waited for; matrix products, arithmetic and copies ran while one was open for 0% of the time, Pallas kernels for 0%

profile of v7, /device:TPU:0, one launch (start us, length us, event | category | flops | bytes accessed | tf_op | source)
XLA Modules:
  0.0 51.9 jit_solution(9334931266142065284)
XLA Ops:
  0.0 2.2 %project.1 = (bf16[512,128]{1,0:T(8,128)(2,1)}, bf16[4,128,128]{2,1,0:T(8,128)(2,1)}, bf16[128,128]{1,0:T(8,128)(2,1)}, bf16[128,128]{1,0:T(8,128)(2,1)}, bf16[1...) custom-call(bf16[4,128,128]{2,1,0:T(8,128)(2,1)} %pair_hbm.1, s32[1,128]{1,0:T(1,128)} %bitcast.9, f32[1,128]{1,0:T(1,128)} %bitcast.10, ...), custom_call_target="tpu_custom_call" | custom-call | tf_op jit(solution)/shard_map/project/pallas_call | solution.py:215
  2.2 3.0 %collective-permute-start = (bf16[128,128]{1,0:T(8,128)(2,1)}, bf16[128,128]{1,0:T(8,128)(2,1)S(1)}, u32[]{:S(2)}, u32[]{:S(2)}) collective-permute-start(bf16[128,128]{1,0:T(8,128)(2,1)} %get-tuple-element.29), channel_id=1, source_target_pairs={{0,2},{1,3},{2,0},{3,1},{4,6},{5,7},{6,4},{7,5},{8,10},{9,11},{10,... | collective-permute-start | bytes 98312 | tf_op jit(solution)/shard_map/ppermute | solution.py:176
  5.2 1.5 %collective-permute-start.1 = (bf16[128,128]{1,0:T(8,128)(2,1)}, bf16[128,128]{1,0:T(8,128)(2,1)S(1)}, u32[]{:S(2)}, u32[]{:S(2)}) collective-permute-start(bf16[128,128]{1,0:T(8,128)(2,1)} %get-tuple-element.30), channel_id=1, source_target_pairs={{0,4},{1,5},{2,6},{3,7},{4,0},{5,1},{6,2},{7,3},{8,12},{9,13},{10,... | collective-permute-start | bytes 98312 | tf_op jit(solution)/shard_map/ppermute | solution.py:176
  6.7 0.6 %collective-permute-done.refs_1_ = bf16[128,128]{1,0:T(8,128)(2,1)S(1)} collective-permute-done((bf16[128,128]{1,0:T(8,128)(2,1)}, bf16[128,128]{1,0:T(8,128)(2,1)S(1)}, u32[]{:S(2)}, u32[]{:S(2)}) %collective-permute-start) | collective-permute-done | bytes 32800 | tf_op jit(solution)/shard_map/ppermute | solution.py:176
  7.3 2.0 %collective-permute-done.1.refs_2_ = bf16[128,128]{1,0:T(8,128)(2,1)S(1)} collective-permute-done((bf16[128,128]{1,0:T(8,128)(2,1)}, bf16[128,128]{1,0:T(8,128)(2,1)S(1)}, u32[]{:S(2)}, u32[]{:S(2)}) %collective-permute-start.1) | collective-permute-done | bytes 32800 | tf_op jit(solution)/shard_map/ppermute | solution.py:176
  9.3 2.4 %collective-permute-done.2.refs_3_ = bf16[128,128]{1,0:T(8,128)(2,1)S(1)} collective-permute-done((bf16[128,128]{1,0:T(8,128)(2,1)}, bf16[128,128]{1,0:T(8,128)(2,1)S(1)}, u32[]{:S(2)}, u32[]{:S(2)}) %collective-permute-start.2) | collective-permute-done | bytes 32800 | tf_op jit(solution)/shard_map/ppermute | solution.py:176
  11.7 0.9 %copy-done.2 = bf16[4,128,128]{2,1,0:T(8,128)(2,1)S(1)} copy-done((bf16[4,128,128]{2,1,0:T(8,128)(2,1)S(1)}, bf16[4,128,128]{2,1,0:T(8,128)(2,1)}, u32[]{:S(2)}) %copy-start.2) | copy-done | bytes 131096
  12.6 0.8 %copy-done.4 = bf16[128,128]{1,0:T(8,128)(2,1)S(1)} copy-done((bf16[128,128]{1,0:T(8,128)(2,1)S(1)}, bf16[128,128]{1,0:T(8,128)(2,1)}, u32[]{:S(2)}) %copy-start.4) | copy-done | bytes 32792
  13.6 1.6 %collective-permute-start.7 = (bf16[32,16,128]{2,1,0:T(8,128)(2,1)S(1)}, bf16[32,16,128]{2,1,0:T(8,128)(2,1)S(1)}, u32[]{:S(2)}, u32[]{:S(2)}) collective-permute-start(bf16[32,16,128]{2,1,0:T(8,128)(2,1)S(1)} %get-tuple-element.36.refs_4_), channel_id=1, source_target_pairs={{0,8},{1,9},{2,10},{3,11},{4,12},{5,13},{6,14},{7,15},{8,24},{9,25... | collective-permute-start | bytes 393224 | tf_op jit(solution)/shard_map/ppermute | solution.py:192
  15.2 4.3 %collective-permute-done.7.refs_6_ = bf16[32,16,128]{2,1,0:T(8,128)(2,1)S(1)} collective-permute-done((bf16[32,16,128]{2,1,0:T(8,128)(2,1)S(1)}, bf16[32,16,128]{2,1,0:T(8,128)(2,1)S(1)}, u32[]{:S(2)}, u32[]{:S(2)}) %collective-permute-start.7) | collective-permute-done | bytes 131104 | tf_op jit(solution)/shard_map/ppermute | solution.py:192
  19.5 0.8 %collective-permute-start.9 = (bf16[32,16,128]{2,1,0:T(8,128)(2,1)S(1)}, bf16[32,16,128]{2,1,0:T(8,128)(2,1)S(1)}, u32[]{:S(2)}, u32[]{:S(2)}) collective-permute-start(bf16[32,16,128]{2,1,0:T(8,128)(2,1)S(1)} %collective-permute-done.7.refs_6_), channel_id=1, source_target_pairs={{0,8},{1,9},{2,10},{3,11},{4,12},{5,13},{6,14},{7,15},{8,24},{9,25... | collective-permute-start | bytes 393224 | tf_op jit(solution)/shard_map/ppermute | solution.py:192
  20.3 5.8 %collective-permute-done.9.refs_8_ = bf16[32,16,128]{2,1,0:T(8,128)(2,1)S(1)} collective-permute-done((bf16[32,16,128]{2,1,0:T(8,128)(2,1)S(1)}, bf16[32,16,128]{2,1,0:T(8,128)(2,1)S(1)}, u32[]{:S(2)}, u32[]{:S(2)}) %collective-permute-start.9) | collective-permute-done | bytes 131104 | tf_op jit(solution)/shard_map/ppermute | solution.py:192
  26.1 0.8 %collective-permute-start.11 = (bf16[32,16,128]{2,1,0:T(8,128)(2,1)S(1)}, bf16[32,16,128]{2,1,0:T(8,128)(2,1)S(1)}, u32[]{:S(2)}, u32[]{:S(2)}) collective-permute-start(bf16[32,16,128]{2,1,0:T(8,128)(2,1)S(1)} %collective-permute-done.9.refs_8_), channel_id=1, source_target_pairs={{0,8},{1,9},{2,10},{3,11},{4,12},{5,13},{6,14},{7,15},{8,24},{9,25... | collective-permute-start | bytes 393224 | tf_op jit(solution)/shard_map/ppermute | solution.py:192
  27.4 4.6 %collective-permute-done.11.refs_10_ = bf16[32,16,128]{2,1,0:T(8,128)(2,1)S(1)} collective-permute-done((bf16[32,16,128]{2,1,0:T(8,128)(2,1)S(1)}, bf16[32,16,128]{2,1,0:T(8,128)(2,1)S(1)}, u32[]{:S(2)}, u32[]{:S(2)}) %collective-permute-start.11) | collective-permute-done | bytes 131104 | tf_op jit(solution)/shard_map/ppermute | solution.py:192
  32.4 3.4 %collective-permute-done.3.refs_1_ = bf16[128,128]{1,0:T(8,128)(2,1)S(1)} collective-permute-done((bf16[128,128]{1,0:T(8,128)(2,1)S(1)}, bf16[128,128]{1,0:T(8,128)(2,1)S(1)}, u32[]{:S(2)}, u32[]{:S(2)}) %collective-permute-start.3) | collective-permute-done | bytes 32800 | tf_op jit(solution)/shard_map/ppermute | solution.py:176
  35.9 0.5 collective-permute-start.4
  36.4 3.4 %collective-permute-done.4.refs_2_ = bf16[128,128]{1,0:T(8,128)(2,1)S(1)} collective-permute-done((bf16[128,128]{1,0:T(8,128)(2,1)S(1)}, bf16[128,128]{1,0:T(8,128)(2,1)S(1)}, u32[]{:S(2)}, u32[]{:S(2)}) %collective-permute-start.4) | collective-permute-done | bytes 32800 | tf_op jit(solution)/shard_map/ppermute | solution.py:176
  39.9 4.7 %collective-permute-done.5.refs_3_ = bf16[128,128]{1,0:T(8,128)(2,1)S(1)} collective-permute-done((bf16[128,128]{1,0:T(8,128)(2,1)S(1)}, bf16[128,128]{1,0:T(8,128)(2,1)S(1)}, u32[]{:S(2)}, u32[]{:S(2)}) %collective-permute-start.5) | collective-permute-done | bytes 32800 | tf_op jit(solution)/shard_map/ppermute | solution.py:176
  44.6 0.7 %contract.1 = (bf16[128,128]{1,0:T(8,128)(2,1)S(1)}, bf16[128,128]{1,0:T(8,128)(2,1)S(1)}, bf16[128,128]{1,0:T(8,128)(2,1)S(1)}, bf16[128,128]{1,0:T(8,128)(2,1)S(1)}) custom-call(bf16[128,128]{1,0:T(8,128)(2,1)S(1)} %get-tuple-element.32.refs_0_, bf16[128,128]{1,0:T(8,128)(2,1)S(1)} %collective-permute-done.3.refs_1_, ...), custom_call_target="tpu_custom_call" | custom-call | tf_op jit(solution)/shard_map/contract/pallas_call | solution.py:246
  45.3 0.6 %collective-permute-start.13 = (bf16[128,128]{1,0:T(8,128)(2,1)S(1)}, bf16[128,128]{1,0:T(8,128)(2,1)S(1)}, u32[]{:S(2)}, u32[]{:S(2)}) collective-permute-start(bf16[128,128]{1,0:T(8,128)(2,1)S(1)} %get-tuple-element.38), channel_id=1, source_target_pairs={{0,2},{1,3},{2,0},{3,1},{4,6},{5,7},{6,4},{7,5},{8,10},{9,11},{10,... | collective-permute-start | bytes 98312 | tf_op jit(solution)/shard_map/ppermute | solution.py:176
  46.1 2.8 %collective-permute-start.15 = (bf16[128,128]{1,0:T(8,128)(2,1)S(1)}, bf16[128,128]{1,0:T(8,128)(2,1)S(1)}, u32[]{:S(2)}, u32[]{:S(2)}) collective-permute-start(bf16[128,128]{1,0:T(8,128)(2,1)S(1)} %get-tuple-element.40), channel_id=1, source_target_pairs={{0,6},{1,7},{2,4},{3,5},{4,2},{5,3},{6,0},{7,1},{8,14},{9,15},{10,... | collective-permute-start | bytes 98312 | tf_op jit(solution)/shard_map/ppermute | solution.py:176
  48.9 0.6 %copy-done.5 = f32[128]{0:T(128)S(1)} copy-done((f32[128]{0:T(128)S(1)}, f32[128]{0:T(128)}, u32[]{:S(2)}) %copy-start.5) | copy-done | bytes 536
  49.8 1.1 %collective-permute-done.15.refs_3_ = bf16[128,128]{1,0:T(8,128)(2,1)S(1)} collective-permute-done((bf16[128,128]{1,0:T(8,128)(2,1)S(1)}, bf16[128,128]{1,0:T(8,128)(2,1)S(1)}, u32[]{:S(2)}, u32[]{:S(2)}) %collective-permute-start.15) | collective-permute-done | bytes 32800 | tf_op jit(solution)/shard_map/ppermute | solution.py:176
  50.9 1.0 %finish.1 = bf16[4,128,128]{2,1,0:T(8,128)(2,1)} custom-call(bf16[4,128,128]{2,1,0:T(8,128)(2,1)S(1)} %bitcast.6, f32[2,128,128]{2,1,0:T(8,128)S(1)} %get-tuple-element.25.scales_ref, bf16[128,128]{1,0:T(8,128)(2,1)S(1)} %get-tuple-element.26.w_ref, bf16[128,128]{1,0:T(8,128)(2,1)S(1)} %get-tuple-element.37.refs_0_, ...), custom_call_target="tpu_custom_call" | custom-call | tf_op jit(solution)/shard_map/finish/pallas_call | solution.py:268
  (27 shorter events, 1.8 us)
Async XLA Ops:
  2.2 5.1 %collective-permute-start = (bf16[128,128]{1,0:T(8,128)(2,1)}, bf16[128,128]{1,0:T(8,128)(2,1)S(1)}, u32[]{:S(2)}, u32[]{:S(2)}) collective-permute-start(bf16[128,128]{1,0:T(8,128)(2,1)} %get-tuple-element.29), channel_id=1, source_target_pairs={{0,2},{1,3},{2,0},{3,1},{4,6},{5,7},{6,4},{7,5},{8,10},{9,11},{10,... | collective-permute-start | bytes 98312 | tf_op jit(solution)/shard_map/ppermute | solution.py:176
  5.2 4.1 %collective-permute-start.1 = (bf16[128,128]{1,0:T(8,128)(2,1)}, bf16[128,128]{1,0:T(8,128)(2,1)S(1)}, u32[]{:S(2)}, u32[]{:S(2)}) collective-permute-start(bf16[128,128]{1,0:T(8,128)(2,1)} %get-tuple-element.30), channel_id=1, source_target_pairs={{0,4},{1,5},{2,6},{3,7},{4,0},{5,1},{6,2},{7,3},{8,12},{9,13},{10,... | collective-permute-start | bytes 98312 | tf_op jit(solution)/shard_map/ppermute | solution.py:176
  6.7 5.0 %collective-permute-start.2 = (bf16[128,128]{1,0:T(8,128)(2,1)}, bf16[128,128]{1,0:T(8,128)(2,1)S(1)}, u32[]{:S(2)}, u32[]{:S(2)}) collective-permute-start(bf16[128,128]{1,0:T(8,128)(2,1)} %get-tuple-element.31), channel_id=1, source_target_pairs={{0,6},{1,7},{2,4},{3,5},{4,2},{5,3},{6,0},{7,1},{8,14},{9,15},{10,... | collective-permute-start | bytes 98312 | tf_op jit(solution)/shard_map/ppermute | solution.py:176
  11.7 0.9 %copy-start.2 = (bf16[4,128,128]{2,1,0:T(8,128)(2,1)S(1)}, bf16[4,128,128]{2,1,0:T(8,128)(2,1)}, u32[]{:S(2)}) copy-start(bf16[4,128,128]{2,1,0:T(8,128)(2,1)} %get-tuple-element.27.left_ref) | copy-start | bytes 393220
  12.6 0.8 %copy-start.4 = (bf16[128,128]{1,0:T(8,128)(2,1)S(1)}, bf16[128,128]{1,0:T(8,128)(2,1)}, u32[]{:S(2)}) copy-start(bf16[128,128]{1,0:T(8,128)(2,1)} %get-tuple-element.28.refs_0_) | copy-start | bytes 98308
  13.6 5.9 %collective-permute-start.7 = (bf16[32,16,128]{2,1,0:T(8,128)(2,1)S(1)}, bf16[32,16,128]{2,1,0:T(8,128)(2,1)S(1)}, u32[]{:S(2)}, u32[]{:S(2)}) collective-permute-start(bf16[32,16,128]{2,1,0:T(8,128)(2,1)S(1)} %get-tuple-element.36.refs_4_), channel_id=1, source_target_pairs={{0,8},{1,9},{2,10},{3,11},{4,12},{5,13},{6,14},{7,15},{8,24},{9,25... | collective-permute-start | bytes 393224 | tf_op jit(solution)/shard_map/ppermute | solution.py:192
  19.5 6.6 %collective-permute-start.9 = (bf16[32,16,128]{2,1,0:T(8,128)(2,1)S(1)}, bf16[32,16,128]{2,1,0:T(8,128)(2,1)S(1)}, u32[]{:S(2)}, u32[]{:S(2)}) collective-permute-start(bf16[32,16,128]{2,1,0:T(8,128)(2,1)S(1)} %collective-permute-done.7.refs_6_), channel_id=1, source_target_pairs={{0,8},{1,9},{2,10},{3,11},{4,12},{5,13},{6,14},{7,15},{8,24},{9,25... | collective-permute-start | bytes 393224 | tf_op jit(solution)/shard_map/ppermute | solution.py:192
  26.1 5.9 %collective-permute-start.11 = (bf16[32,16,128]{2,1,0:T(8,128)(2,1)S(1)}, bf16[32,16,128]{2,1,0:T(8,128)(2,1)S(1)}, u32[]{:S(2)}, u32[]{:S(2)}) collective-permute-start(bf16[32,16,128]{2,1,0:T(8,128)(2,1)S(1)} %collective-permute-done.9.refs_8_), channel_id=1, source_target_pairs={{0,8},{1,9},{2,10},{3,11},{4,12},{5,13},{6,14},{7,15},{8,24},{9,25... | collective-permute-start | bytes 393224 | tf_op jit(solution)/shard_map/ppermute | solution.py:192
  26.9 17.7 %collective-permute-start.6 = (bf16[32,16,128]{2,1,0:T(8,128)(2,1)S(1)}, bf16[32,16,128]{2,1,0:T(8,128)(2,1)S(1)}, u32[]{:S(2)}, u32[]{:S(2)}) collective-permute-start(bf16[32,16,128]{2,1,0:T(8,128)(2,1)S(1)} %get-tuple-element.36.refs_4_), channel_id=1, source_target_pairs={{0,1},{1,0},{2,3},{3,2},{4,5},{5,4},{6,7},{7,6},{8,9},{9,8},{10,11... | collective-permute-start | bytes 393224 | tf_op jit(solution)/shard_map/ppermute | solution.py:182
  26.9 17.7 %collective-permute-start.8 = (bf16[32,16,128]{2,1,0:T(8,128)(2,1)S(1)}, bf16[32,16,128]{2,1,0:T(8,128)(2,1)S(1)}, u32[]{:S(2)}, u32[]{:S(2)}) collective-permute-start(bf16[32,16,128]{2,1,0:T(8,128)(2,1)S(1)} %collective-permute-done.7.refs_6_), channel_id=1, source_target_pairs={{0,1},{1,0},{2,3},{3,2},{4,5},{5,4},{6,7},{7,6},{8,9},{9,8},{10,11... | collective-permute-start | bytes 393224 | tf_op jit(solution)/shard_map/ppermute | solution.py:182
  27.4 17.2 %collective-permute-start.10 = (bf16[32,16,128]{2,1,0:T(8,128)(2,1)S(1)}, bf16[32,16,128]{2,1,0:T(8,128)(2,1)S(1)}, u32[]{:S(2)}, u32[]{:S(2)}) collective-permute-start(bf16[32,16,128]{2,1,0:T(8,128)(2,1)S(1)} %collective-permute-done.9.refs_8_), channel_id=1, source_target_pairs={{0,1},{1,0},{2,3},{3,2},{4,5},{5,4},{6,7},{7,6},{8,9},{9,8},{10,11... | collective-permute-start | bytes 393224 | tf_op jit(solution)/shard_map/ppermute | solution.py:182
  31.9 12.7 %collective-permute-start.12 = (bf16[32,16,128]{2,1,0:T(8,128)(2,1)S(1)}, bf16[32,16,128]{2,1,0:T(8,128)(2,1)S(1)}, u32[]{:S(2)}, u32[]{:S(2)}) collective-permute-start(bf16[32,16,128]{2,1,0:T(8,128)(2,1)S(1)} %collective-permute-done.11.refs_10_), channel_id=1, source_target_pairs={{0,1},{1,0},{2,3},{3,2},{4,5},{5,4},{6,7},{7,6},{8,9},{9,8},{10,11... | collective-permute-start | bytes 393224 | tf_op jit(solution)/shard_map/ppermute | solution.py:182
  31.9 3.9 %collective-permute-start.3 = (bf16[128,128]{1,0:T(8,128)(2,1)S(1)}, bf16[128,128]{1,0:T(8,128)(2,1)S(1)}, u32[]{:S(2)}, u32[]{:S(2)}) collective-permute-start(bf16[128,128]{1,0:T(8,128)(2,1)S(1)} %get-tuple-element.33), channel_id=1, source_target_pairs={{0,2},{1,3},{2,0},{3,1},{4,6},{5,7},{6,4},{7,5},{8,10},{9,11},{10,... | collective-permute-start | bytes 98312 | tf_op jit(solution)/shard_map/ppermute | solution.py:176
  35.9 3.9 %collective-permute-start.4 = (bf16[128,128]{1,0:T(8,128)(2,1)S(1)}, bf16[128,128]{1,0:T(8,128)(2,1)S(1)}, u32[]{:S(2)}, u32[]{:S(2)}) collective-permute-start(bf16[128,128]{1,0:T(8,128)(2,1)S(1)} %get-tuple-element.34), channel_id=1, source_target_pairs={{0,4},{1,5},{2,6},{3,7},{4,0},{5,1},{6,2},{7,3},{8,12},{9,13},{10,... | collective-permute-start | bytes 98312 | tf_op jit(solution)/shard_map/ppermute | solution.py:176
  39.8 4.8 %collective-permute-start.5 = (bf16[128,128]{1,0:T(8,128)(2,1)S(1)}, bf16[128,128]{1,0:T(8,128)(2,1)S(1)}, u32[]{:S(2)}, u32[]{:S(2)}) collective-permute-start(bf16[128,128]{1,0:T(8,128)(2,1)S(1)} %get-tuple-element.35), channel_id=1, source_target_pairs={{0,6},{1,7},{2,4},{3,5},{4,2},{5,3},{6,0},{7,1},{8,14},{9,15},{10,... | collective-permute-start | bytes 98312 | tf_op jit(solution)/shard_map/ppermute | solution.py:176
  44.6 4.3 %copy-start = (bf16[128,640]{1,0:T(8,128)(2,1)S(1)}, bf16[128,640]{1,0:T(8,128)(2,1)}, u32[]{:S(2)}) copy-start(bf16[128,640]{1,0:T(8,128)(2,1)} %w_ref.1) | copy-start | bytes 491524
  44.6 4.3 %copy-start.1 = (bf16[512,128]{1,0:T(8,128)(2,1)S(1)}, bf16[512,128]{1,0:T(8,128)(2,1)}, u32[]{:S(2)}) copy-start(bf16[512,128]{1,0:T(8,128)(2,1)} %get-tuple-element.23.normed_ref) | copy-start | bytes 393220
  44.6 4.3 %copy-start.3 = (bf16[128,128]{1,0:T(8,128)(2,1)S(1)}, bf16[128,128]{1,0:T(8,128)(2,1)}, u32[]{:S(2)}) copy-start(bf16[128,128]{1,0:T(8,128)(2,1)} %w_out_ref.1) | copy-start | bytes 98308
  45.3 4.4 %collective-permute-start.13 = (bf16[128,128]{1,0:T(8,128)(2,1)S(1)}, bf16[128,128]{1,0:T(8,128)(2,1)S(1)}, u32[]{:S(2)}, u32[]{:S(2)}) collective-permute-start(bf16[128,128]{1,0:T(8,128)(2,1)S(1)} %get-tuple-element.38), channel_id=1, source_target_pairs={{0,2},{1,3},{2,0},{3,1},{4,6},{5,7},{6,4},{7,5},{8,10},{9,11},{10,... | collective-permute-start | bytes 98312 | tf_op jit(solution)/shard_map/ppermute | solution.py:176
  45.9 3.9 %collective-permute-start.14 = (bf16[128,128]{1,0:T(8,128)(2,1)S(1)}, bf16[128,128]{1,0:T(8,128)(2,1)S(1)}, u32[]{:S(2)}, u32[]{:S(2)}) collective-permute-start(bf16[128,128]{1,0:T(8,128)(2,1)S(1)} %get-tuple-element.39), channel_id=1, source_target_pairs={{0,4},{1,5},{2,6},{3,7},{4,0},{5,1},{6,2},{7,3},{8,12},{9,13},{10,... | collective-permute-start | bytes 98312 | tf_op jit(solution)/shard_map/ppermute | solution.py:176
  46.1 4.8 %collective-permute-start.15 = (bf16[128,128]{1,0:T(8,128)(2,1)S(1)}, bf16[128,128]{1,0:T(8,128)(2,1)S(1)}, u32[]{:S(2)}, u32[]{:S(2)}) collective-permute-start(bf16[128,128]{1,0:T(8,128)(2,1)S(1)} %get-tuple-element.40), channel_id=1, source_target_pairs={{0,6},{1,7},{2,4},{3,5},{4,2},{5,3},{6,0},{7,1},{8,14},{9,15},{10,... | collective-permute-start | bytes 98312 | tf_op jit(solution)/shard_map/ppermute | solution.py:176
  48.9 0.7 %copy-start.5 = (f32[128]{0:T(128)S(1)}, f32[128]{0:T(128)}, u32[]{:S(2)}) copy-start(f32[128]{0:T(128)} %param.13) | copy-start | bytes 1540
  48.9 0.7 %copy-start.6 = (f32[128]{0:T(128)S(1)}, f32[128]{0:T(128)}, u32[]{:S(2)}) copy-start(f32[128]{0:T(128)} %param.14) | copy-start | bytes 1540

commit v8 on v6

--- a/solution.py
+++ b/solution.py
@@ -10,6 +10,7 @@
 epsilon = 1e-05
 axes = ("wide", "narrow")
 kernel_vmem = 8 * 2**20
+hub = 8
 
 
 def layer_norm(values, gain_vec, bias_vec, axis_dim):
@@ -71,13 +72,25 @@
                 rows = jnp.concatenate(
                     [block[:, (r + i) * col_count : (r + i + 1) * col_count] for i in range(2)], axis=0
                 )
-                out_ref[chan // 4 + half, r * 8 : (r + 2) * 8, :] = rows.astype(jnp.bfloat16)
+                out_ref[(chan // 4 + half) ^ hub, r * 8 : (r + 2) * 8, :] = rows.astype(jnp.bfloat16)
+
+
+def receive_blocks(blocks_ref, held_ref):
+    shards, rows, _ = blocks_ref.shape
+    for i in range(shards):
+        held_ref[(i ^ hub) * rows : ((i ^ hub) + 1) * rows, :] = blocks_ref[i].astype(jnp.float32)
+
+
+def exchange(blocks):
+    groups = [[i ^ hub for i in range(blocks.shape[0])]]
+    return lax.all_to_all(
+        blocks, axes, split_axis=0, concat_axis=0, axis_index_groups=groups, tiled=True
+    )
 
 
 def contract_kernel(blocks_ref, out_ref, held_ref):
-    shards, block_rows, cols = blocks_ref.shape
     total = held_ref.shape[0] // 8
-    held_ref[...] = blocks_ref[...].reshape(shards * block_rows, cols).astype(jnp.float32)
+    receive_blocks(blocks_ref, held_ref)
     products = []
     for c in range(4):
         left = held_ref[pl.ds(c, total, stride=8), :].astype(jnp.bfloat16)
@@ -92,7 +105,7 @@
         low, high = swap_halves(pieces[0], pieces[1]), swap_halves(pieces[2], pieces[3])
         for half in range(2):
             rows = jnp.concatenate([low[half], high[half]], axis=0)
-            out_ref[row // 4 + half] = rows.astype(jnp.bfloat16)
+            out_ref[(row // 4 + half) ^ hub] = rows.astype(jnp.bfloat16)
 
 
 def gate_kernel(normed_ref, w_ref, gain_ref, bias_ref, w_out_ref, out_ref, scales_ref, weights_ref):
@@ -108,7 +121,7 @@
 
 def finish_kernel(blocks_ref, gate_ref, scales_ref, w_ref, out_ref, held_ref):
     row_count, col_count, chan_count = out_ref.shape
-    held_ref[...] = blocks_ref[...].reshape(held_ref.shape).astype(jnp.float32)
+    receive_blocks(blocks_ref, held_ref)
     for r in range(row_count):
         triangle = held_ref[pl.ds(r, chan_count, stride=row_count), :]
         normed = layer_norm(triangle, scales_ref[0], scales_ref[1], 0).astype(jnp.bfloat16)
@@ -147,7 +160,7 @@
         ],
         name="project",
     )(pair, line(valid), line(norm_gain), line(norm_bias), w_proj)
-    sides = lax.all_to_all(sides, axes, split_axis=0, concat_axis=0, tiled=True)
+    sides = exchange(sides)
     triangle = pl.pallas_call(
         contract_kernel,
         out_shape=shaped(shards, 4 * row_count, col_count),
@@ -157,7 +170,7 @@
         compiler_params=pltpu.CompilerParams(vmem_limit_bytes=kernel_vmem),
         name="contract",
     )(sides)
-    triangle = lax.all_to_all(triangle, axes, split_axis=0, concat_axis=0, tiled=True)
+    triangle = exchange(triangle)
     gate_values, scales, weights = pl.pallas_call(
         gate_kernel,
         out_shape=(
@@ -232,6 +245,7 @@
         and (row_count, col_count, chan_count) == (4, 128, 128)
         and shards * row_count == col_count
         and shards * 4 == chan_count
+        and shards % (2 * hub) == 0
     )
     return (local_blocks if fits else local_arrays)(pair, *rest)
 

time: 33.2 us -> 33.5 us (level)
  no operation moved by 1% of the time
where the time goes in v8:
time: 33.5 us; the launch traced here: 33.3 us
  blocking collectives  18 us (54%)
  waiting for transfers between devices  7.59 us (23%)
  Pallas kernels  4.28 us (13%)
  starting transfers between devices  2.7 us (8%)
  local copies, waits for them, and re-layouts  0.64 us (2%)
    all_to_all x1, blocking collectives, exchange(): lax.all_to_all(blocks, axes, split_axis=0, concat_axis=0, axis_index_grou...  18 us
    all_to_all x1, waiting for transfers between devices, exchange(): lax.all_to_all(blocks, axes, split_axis=0, concat_axis=0, axis_index_grou...  7.59 us
    all_to_all x1, starting transfers between devices, exchange(): lax.all_to_all(blocks, axes, split_axis=0, concat_axis=0, axis_index_grou...  2.7 us
    pallas_call x1, Pallas kernels, local_blocks(): pl.pallas_call(project_kernel, out_shape=(shaped(shards, 8 * row_count, c...  2.24 us
    pallas_call x1, Pallas kernels, local_blocks(): pl.pallas_call(finish_kernel, out_shape=shaped(row_count, col_count, chan...  0.97 us
    pallas_call x1, Pallas kernels, local_blocks(): pl.pallas_call(contract_kernel, out_shape=shaped(shards, 4 * row_count, c...  0.89 us
  transfers between devices with their start and end apart: 1, of which 1 were waited for; matrix products, arithmetic and copies ran while one was open for 0% of the time, Pallas kernels for 1%

profile of v8, /device:TPU:0, one launch (start us, length us, event | category | flops | bytes accessed | tf_op | source)
XLA Modules:
  0.0 33.3 jit_solution(9823883939957981240)
XLA Ops:
  0.0 2.2 %project.1 = (bf16[32,32,128]{2,1,0:T(8,128)(2,1)}, bf16[512,128]{1,0:T(8,128)(2,1)}) custom-call(bf16[4,128,128]{2,1,0:T(8,128)(2,1)} %pair_hbm.1, s32[1,128]{1,0:T(1,128)} %bitcast.7, f32[1,128]{1,0:T(1,128)} %bitcast.8, f32[1,128]{1,0:T(1,128)} %bitcast.9, bf16[128,640]{1,0:T(8,128)(2,1)} %w_ref.1), custom_call_target="tpu_custom_call" | custom-call | tf_op jit(solution)/shard_map/project/pallas_call | solution.py:148
  2.3 18.0 %all_to_all.10.blocks_ref = bf16[32,32,128]{2,1,0:T(8,128)(2,1)S(1)} all-to-all(bf16[32,32,128]{2,1,0:T(8,128)(2,1)} %get-tuple-element.10), channel_id=1, replica_groups={{8,9,10,11,12,13,14,15,0,1,2,3,4,5,6,7,24,25,26,27,28,29,30,31,16,17,18..., dimensions={0} | all-to-all | bytes 524288 | tf_op jit(solution)/shard_map/all_to_all | solution.py:86
  20.3 0.0 copy-start.1
  20.3 0.9 %contract.1 = bf16[32,16,128]{2,1,0:T(8,128)(2,1)} custom-call(bf16[32,32,128]{2,1,0:T(8,128)(2,1)S(1)} %all_to_all.10.blocks_ref), custom_call_target="tpu_custom_call" | custom-call | tf_op jit(solution)/shard_map/contract/pallas_call | solution.py:164
  21.1 0.0 copy-start
  21.1 0.0 copy-start.2
  21.2 2.7 %all-to-all-start.1 = ((bf16[32,16,128]{2,1,0:T(8,128)(2,1)}), bf16[32,16,128]{2,1,0:T(8,128)(2,1)S(1)}, u32[]{:S(2)}, u32[]{:S(2)}) async-start(bf16[32,16,128]{2,1,0:T(8,128)(2,1)} %contract.1), calls=%async_computation.1 | async-start | bytes 262144 | tf_op jit(solution)/shard_map/all_to_all | solution.py:86
  23.9 0.0 copy-start.3
  23.9 0.0 copy-start.4
  23.9 0.0 copy-done.1
  23.9 0.0 copy-done
  23.9 0.0 copy-done.2
  23.9 0.6 %copy-done.3 = f32[128]{0:T(128)S(1)} copy-done((f32[128]{0:T(128)S(1)}, f32[128]{0:T(128)}, u32[]{:S(2)}) %copy-start.3) | copy-done | bytes 536
  24.5 0.0 copy-done.4
  24.5 0.2 gate.1
  24.7 7.6 %all-to-all-done.1.blocks_ref = bf16[32,16,128]{2,1,0:T(8,128)(2,1)S(1)} async-done(((bf16[32,16,128]{2,1,0:T(8,128)(2,1)}), bf16[32,16,128]{2,1,0:T(8,128)(2,1)S(1)}, u32[]{:S(2)}, u32[]{:S(2)}) %all-to-all-start.1) | async-done | bytes 131104 | tf_op jit(solution)/shard_map/all_to_all | solution.py:86
  32.3 1.0 %finish.1 = bf16[4,128,128]{2,1,0:T(8,128)(2,1)} custom-call(bf16[32,16,128]{2,1,0:T(8,128)(2,1)S(1)} %all-to-all-done.1.blocks_ref, bf16[512,128]{1,0:T(8,128)(2,1)S(1)} %get-tuple-element.12.gate_ref, f32[2,128,128]{2,1,0:T(8,128)S(1)} %get-tuple-element.13.scales_ref, bf16[128,128]{1,0:T(8,128)(2,1)S(1)} %get-tuple-element.14.w_ref), custom_call_target="tpu_custom_call" | custom-call | tf_op jit(solution)/shard_map/finish/pallas_call | solution.py:186
Async XLA Ops:
  20.3 3.6 %copy-start.1 = (bf16[512,128]{1,0:T(8,128)(2,1)S(1)}, bf16[512,128]{1,0:T(8,128)(2,1)}, u32[]{:S(2)}) copy-start(bf16[512,128]{1,0:T(8,128)(2,1)} %get-tuple-element.11.normed_ref) | copy-start | bytes 393220
  21.1 2.7 %copy-start = (bf16[128,640]{1,0:T(8,128)(2,1)S(1)}, bf16[128,640]{1,0:T(8,128)(2,1)}, u32[]{:S(2)}) copy-start(bf16[128,640]{1,0:T(8,128)(2,1)} %w_ref.1) | copy-start | bytes 491524
  21.1 2.8 %copy-start.2 = (bf16[128,128]{1,0:T(8,128)(2,1)S(1)}, bf16[128,128]{1,0:T(8,128)(2,1)}, u32[]{:S(2)}) copy-start(bf16[128,128]{1,0:T(8,128)(2,1)} %w_out_ref.1) | copy-start | bytes 98308
  21.2 11.2 %all-to-all-start.1 = ((bf16[32,16,128]{2,1,0:T(8,128)(2,1)}), bf16[32,16,128]{2,1,0:T(8,128)(2,1)S(1)}, u32[]{:S(2)}, u32[]{:S(2)}) async-start(bf16[32,16,128]{2,1,0:T(8,128)(2,1)} %contract.1), calls=%async_computation.1 | async-start | bytes 262144 | tf_op jit(solution)/shard_map/all_to_all | solution.py:86
  23.9 0.7 %copy-start.3 = (f32[128]{0:T(128)S(1)}, f32[128]{0:T(128)}, u32[]{:S(2)}) copy-start(f32[128]{0:T(128)} %param.13) | copy-start | bytes 1540
  23.9 0.7 %copy-start.4 = (f32[128]{0:T(128)S(1)}, f32[128]{0:T(128)}, u32[]{:S(2)}) copy-start(f32[128]{0:T(128)} %param.14) | copy-start | bytes 1540

commit v9 on v8

--- a/solution.py
+++ b/solution.py
@@ -10,7 +10,7 @@
 epsilon = 1e-05
 axes = ("wide", "narrow")
 kernel_vmem = 8 * 2**20
-hub = 8
+hub = 31
 
 
 def layer_norm(values, gain_vec, bias_vec, axis_dim):
@@ -245,7 +245,7 @@
         and (row_count, col_count, chan_count) == (4, 128, 128)
         and shards * row_count == col_count
         and shards * 4 == chan_count
-        and shards % (2 * hub) == 0
+        and shards == hub + 1
     )
     return (local_blocks if fits else local_arrays)(pair, *rest)
 

time: 33.5 us -> 32.7 us (0.976)
  blocking collectives: 18 us -> 17.2 us
  waiting for transfers between devices: 7.59 us -> 7.05 us
  starting transfers between devices: 2.7 us -> 3.07 us
    all_to_all x1, blocking collectives: 18 us -> 17.2 us  [exchange(): lax.all_to_all(blocks, axes, split_axis=0, concat_axis=0, axis_index_grou...]
    all_to_all x1, waiting for transfers between devices: 7.59 us -> 7.05 us  [exchange(): lax.all_to_all(blocks, axes, split_axis=0, concat_axis=0, axis_index_grou...]
    all_to_all x1, starting transfers between devices: 2.7 us -> 3.07 us  [exchange(): lax.all_to_all(blocks, axes, split_axis=0, concat_axis=0, axis_index_grou...]
where the time goes in v9:
time: 32.7 us; the launch traced here: 32.4 us
  blocking collectives  17.2 us (53%)
  waiting for transfers between devices  7.05 us (22%)
  Pallas kernels  4.29 us (13%)
  starting transfers between devices  3.07 us (9%)
  local copies, waits for them, and re-layouts  0.64 us (2%)
    all_to_all x1, blocking collectives, exchange(): lax.all_to_all(blocks, axes, split_axis=0, concat_axis=0, axis_index_grou...  17.2 us
    all_to_all x1, waiting for transfers between devices, exchange(): lax.all_to_all(blocks, axes, split_axis=0, concat_axis=0, axis_index_grou...  7.05 us
    all_to_all x1, starting transfers between devices, exchange(): lax.all_to_all(blocks, axes, split_axis=0, concat_axis=0, axis_index_grou...  3.07 us
    pallas_call x1, Pallas kernels, local_blocks(): pl.pallas_call(project_kernel, out_shape=(shaped(shards, 8 * row_count, c...  2.24 us
    pallas_call x1, Pallas kernels, local_blocks(): pl.pallas_call(finish_kernel, out_shape=shaped(row_count, col_count, chan...  0.97 us
    pallas_call x1, Pallas kernels, local_blocks(): pl.pallas_call(contract_kernel, out_shape=shaped(shards, 4 * row_count, c...  0.89 us
  transfers between devices with their start and end apart: 1, of which 1 were waited for; matrix products, arithmetic and copies ran while one was open for 0% of the time, Pallas kernels for 1%

profile of v9, /device:TPU:0, one launch (start us, length us, event | category | flops | bytes accessed | tf_op | source)
XLA Modules:
  0.0 32.4 jit_solution(6477865618569566680)
XLA Ops:
  0.0 2.2 %project.1 = (bf16[32,32,128]{2,1,0:T(8,128)(2,1)}, bf16[512,128]{1,0:T(8,128)(2,1)}) custom-call(bf16[4,128,128]{2,1,0:T(8,128)(2,1)} %pair_hbm.1, s32[1,128]{1,0:T(1,128)} %bitcast.7, f32[1,128]{1,0:T(1,128)} %bitcast.8, f32[1,128]{1,0:T(1,128)} %bitcast.9, bf16[128,640]{1,0:T(8,128)(2,1)} %w_ref.1), custom_call_target="tpu_custom_call" | custom-call | tf_op jit(solution)/shard_map/project/pallas_call | solution.py:148
  2.3 17.2 %all_to_all.10.blocks_ref = bf16[32,32,128]{2,1,0:T(8,128)(2,1)S(1)} all-to-all(bf16[32,32,128]{2,1,0:T(8,128)(2,1)} %get-tuple-element.10), channel_id=1, replica_groups={{31,30,29,28,27,26,25,24,23,22,21,20,19,18,17,16,15,14,13,12,11,10,9,8,..., dimensions={0} | all-to-all | bytes 524288 | tf_op jit(solution)/shard_map/all_to_all | solution.py:86
  19.5 0.0 copy-start.1
  19.5 0.9 %contract.1 = bf16[32,16,128]{2,1,0:T(8,128)(2,1)} custom-call(bf16[32,32,128]{2,1,0:T(8,128)(2,1)S(1)} %all_to_all.10.blocks_ref), custom_call_target="tpu_custom_call" | custom-call | tf_op jit(solution)/shard_map/contract/pallas_call | solution.py:164
  20.4 0.0 copy-start
  20.4 0.0 copy-start.2
  20.4 3.1 %all-to-all-start.1 = ((bf16[32,16,128]{2,1,0:T(8,128)(2,1)}), bf16[32,16,128]{2,1,0:T(8,128)(2,1)S(1)}, u32[]{:S(2)}, u32[]{:S(2)}) async-start(bf16[32,16,128]{2,1,0:T(8,128)(2,1)} %contract.1), calls=%async_computation.1 | async-start | bytes 262144 | tf_op jit(solution)/shard_map/all_to_all | solution.py:86
  23.5 0.0 copy-start.3
  23.5 0.0 copy-start.4
  23.5 0.0 copy-done.1
  23.5 0.0 copy-done
  23.5 0.0 copy-done.2
  23.5 0.6 %copy-done.3 = f32[128]{0:T(128)S(1)} copy-done((f32[128]{0:T(128)S(1)}, f32[128]{0:T(128)}, u32[]{:S(2)}) %copy-start.3) | copy-done | bytes 536
  24.1 0.0 copy-done.4
  24.2 0.2 gate.1
  24.3 7.0 %all-to-all-done.1.blocks_ref = bf16[32,16,128]{2,1,0:T(8,128)(2,1)S(1)} async-done(((bf16[32,16,128]{2,1,0:T(8,128)(2,1)}), bf16[32,16,128]{2,1,0:T(8,128)(2,1)S(1)}, u32[]{:S(2)}, u32[]{:S(2)}) %all-to-all-start.1) | async-done | bytes 131104 | tf_op jit(solution)/shard_map/all_to_all | solution.py:86
  31.4 1.0 %finish.1 = bf16[4,128,128]{2,1,0:T(8,128)(2,1)} custom-call(bf16[32,16,128]{2,1,0:T(8,128)(2,1)S(1)} %all-to-all-done.1.blocks_ref, bf16[512,128]{1,0:T(8,128)(2,1)S(1)} %get-tuple-element.12.gate_ref, f32[2,128,128]{2,1,0:T(8,128)S(1)} %get-tuple-element.13.scales_ref, bf16[128,128]{1,0:T(8,128)(2,1)S(1)} %get-tuple-element.14.w_ref), custom_call_target="tpu_custom_call" | custom-call | tf_op jit(solution)/shard_map/finish/pallas_call | solution.py:186
Async XLA Ops:
  19.5 4.0 %copy-start.1 = (bf16[512,128]{1,0:T(8,128)(2,1)S(1)}, bf16[512,128]{1,0:T(8,128)(2,1)}, u32[]{:S(2)}) copy-start(bf16[512,128]{1,0:T(8,128)(2,1)} %get-tuple-element.11.normed_ref) | copy-start | bytes 393220
  20.4 3.1 %copy-start = (bf16[128,640]{1,0:T(8,128)(2,1)S(1)}, bf16[128,640]{1,0:T(8,128)(2,1)}, u32[]{:S(2)}) copy-start(bf16[128,640]{1,0:T(8,128)(2,1)} %w_ref.1) | copy-start | bytes 491524
  20.4 3.1 %copy-start.2 = (bf16[128,128]{1,0:T(8,128)(2,1)S(1)}, bf16[128,128]{1,0:T(8,128)(2,1)}, u32[]{:S(2)}) copy-start(bf16[128,128]{1,0:T(8,128)(2,1)} %w_out_ref.1) | copy-start | bytes 98308
  20.4 11.0 %all-to-all-start.1 = ((bf16[32,16,128]{2,1,0:T(8,128)(2,1)}), bf16[32,16,128]{2,1,0:T(8,128)(2,1)S(1)}, u32[]{:S(2)}, u32[]{:S(2)}) async-start(bf16[32,16,128]{2,1,0:T(8,128)(2,1)} %contract.1), calls=%async_computation.1 | async-start | bytes 262144 | tf_op jit(solution)/shard_map/all_to_all | solution.py:86
  23.5 0.7 %copy-start.3 = (f32[128]{0:T(128)S(1)}, f32[128]{0:T(128)}, u32[]{:S(2)}) copy-start(f32[128]{0:T(128)} %param.13) | copy-start | bytes 1540
  23.5 0.7 %copy-start.4 = (f32[128]{0:T(128)S(1)}, f32[128]{0:T(128)}, u32[]{:S(2)}) copy-start(f32[128]{0:T(128)} %param.14) | copy-start | bytes 1540

commit v10 on v9

--- a/solution.py
+++ b/solution.py
@@ -10,7 +10,7 @@
 epsilon = 1e-05
 axes = ("wide", "narrow")
 kernel_vmem = 8 * 2**20
-hub = 31
+planes = 4
 
 
 def layer_norm(values, gain_vec, bias_vec, axis_dim):
@@ -33,6 +33,7 @@
     pair_ref, valid_ref, gain_ref, bias_ref, w_ref, sems,
 ):
     row_count, col_count, chan_count = pair_ref.shape
+    shards = out_ref.shape[0]
     fetches = [
         pltpu.make_async_copy(source, held, sems.at[i])
         for i, (source, held) in enumerate((
@@ -72,19 +73,28 @@
                 rows = jnp.concatenate(
                     [block[:, (r + i) * col_count : (r + i + 1) * col_count] for i in range(2)], axis=0
                 )
-                out_ref[(chan // 4 + half) ^ hub, r * 8 : (r + 2) * 8, :] = rows.astype(jnp.bfloat16)
+                out_ref[spot(chan // 4 + half, shards), r * 8 : (r + 2) * 8, :] = rows.astype(jnp.bfloat16)
+
+
+def group_order(shards):
+    size = shards // planes
+    return [plane * size + place for place in range(size) for plane in range(planes)]
+
+
+def spot(device, shards):
+    return group_order(shards).index(device)
 
 
 def receive_blocks(blocks_ref, held_ref):
     shards, rows, _ = blocks_ref.shape
-    for i in range(shards):
-        held_ref[(i ^ hub) * rows : ((i ^ hub) + 1) * rows, :] = blocks_ref[i].astype(jnp.float32)
+    for i, device in enumerate(group_order(shards)):
+        held_ref[device * rows : (device + 1) * rows, :] = blocks_ref[i].astype(jnp.float32)
 
 
 def exchange(blocks):
-    groups = [[i ^ hub for i in range(blocks.shape[0])]]
     return lax.all_to_all(
-        blocks, axes, split_axis=0, concat_axis=0, axis_index_groups=groups, tiled=True
+        blocks, axes, split_axis=0, concat_axis=0,
+        axis_index_groups=[group_order(blocks.shape[0])], tiled=True,
     )
 
 
@@ -105,7 +115,7 @@
         low, high = swap_halves(pieces[0], pieces[1]), swap_halves(pieces[2], pieces[3])
         for half in range(2):
             rows = jnp.concatenate([low[half], high[half]], axis=0)
-            out_ref[(row // 4 + half) ^ hub] = rows.astype(jnp.bfloat16)
+            out_ref[spot(row // 4 + half, out_ref.shape[0])] = rows.astype(jnp.bfloat16)
 
 
 def gate_kernel(normed_ref, w_ref, gain_ref, bias_ref, w_out_ref, out_ref, scales_ref, weights_ref):
@@ -245,7 +255,7 @@
         and (row_count, col_count, chan_count) == (4, 128, 128)
         and shards * row_count == col_count
         and shards * 4 == chan_count
-        and shards == hub + 1
+        and shards % planes == 0
     )
     return (local_blocks if fits else local_arrays)(pair, *rest)
 

time: 32.7 us -> 33.1 us (1.012)
  waiting for transfers between devices: 7.05 us -> 7.54 us
  starting transfers between devices: 3.07 us -> 2.73 us
    all_to_all x1, waiting for transfers between devices: 7.05 us -> 7.54 us  [exchange(): lax.all_to_all(blocks, axes, split_axis=0, concat_axis=0, axis_index_grou...]
    all_to_all x1, starting transfers between devices: 3.07 us -> 2.73 us  [exchange(): lax.all_to_all(blocks, axes, split_axis=0, concat_axis=0, axis_index_grou...]
where the time goes in v10:
time: 33.1 us; the launch traced here: 32.8 us
  blocking collectives  17.5 us (53%)
  waiting for transfers between devices  7.54 us (23%)
  Pallas kernels  4.29 us (13%)
  starting transfers between devices  2.73 us (8%)
  local copies, waits for them, and re-layouts  0.64 us (2%)
    all_to_all x1, blocking collectives, exchange(): lax.all_to_all(blocks, axes, split_axis=0, concat_axis=0, axis_index_grou...  17.5 us
    all_to_all x1, waiting for transfers between devices, exchange(): lax.all_to_all(blocks, axes, split_axis=0, concat_axis=0, axis_index_grou...  7.54 us
    all_to_all x1, starting transfers between devices, exchange(): lax.all_to_all(blocks, axes, split_axis=0, concat_axis=0, axis_index_grou...  2.73 us
    pallas_call x1, Pallas kernels, local_blocks(): pl.pallas_call(project_kernel, out_shape=(shaped(shards, 8 * row_count, c...  2.24 us
    pallas_call x1, Pallas kernels, local_blocks(): pl.pallas_call(finish_kernel, out_shape=shaped(row_count, col_count, chan...  0.98 us
    pallas_call x1, Pallas kernels, local_blocks(): pl.pallas_call(contract_kernel, out_shape=shaped(shards, 4 * row_count, c...  0.89 us
  transfers between devices with their start and end apart: 1, of which 1 were waited for; matrix products, arithmetic and copies ran while one was open for 0% of the time, Pallas kernels for 1%

profile of v10, /device:TPU:0, one launch (start us, length us, event | category | flops | bytes accessed | tf_op | source)
XLA Modules:
  0.0 32.8 jit_solution(11504997991288885665)
XLA Ops:
  0.0 2.2 %project.1 = (bf16[32,32,128]{2,1,0:T(8,128)(2,1)}, bf16[512,128]{1,0:T(8,128)(2,1)}) custom-call(bf16[4,128,128]{2,1,0:T(8,128)(2,1)} %pair_hbm.1, s32[1,128]{1,0:T(1,128)} %bitcast.7, f32[1,128]{1,0:T(1,128)} %bitcast.8, f32[1,128]{1,0:T(1,128)} %bitcast.9, bf16[128,640]{1,0:T(8,128)(2,1)} %w_ref.1), custom_call_target="tpu_custom_call" | custom-call | tf_op jit(solution)/shard_map/project/pallas_call | solution.py:158
  2.3 17.5 %all_to_all.10.blocks_ref = bf16[32,32,128]{2,1,0:T(8,128)(2,1)S(1)} all-to-all(bf16[32,32,128]{2,1,0:T(8,128)(2,1)} %get-tuple-element.10), channel_id=1, replica_groups={{0,8,16,24,1,9,17,25,2,10,18,26,3,11,19,27,4,12,20,28,5,13,21,29,6,14,2..., dimensions={0} | all-to-all | bytes 524288 | tf_op jit(solution)/shard_map/all_to_all | solution.py:95
  19.8 0.0 copy-start.1
  19.8 0.9 %contract.1 = bf16[32,16,128]{2,1,0:T(8,128)(2,1)} custom-call(bf16[32,32,128]{2,1,0:T(8,128)(2,1)S(1)} %all_to_all.10.blocks_ref), custom_call_target="tpu_custom_call" | custom-call | tf_op jit(solution)/shard_map/contract/pallas_call | solution.py:174
  20.7 0.0 copy-start
  20.7 0.0 copy-start.2
  20.7 2.7 %all-to-all-start.1 = ((bf16[32,16,128]{2,1,0:T(8,128)(2,1)}), bf16[32,16,128]{2,1,0:T(8,128)(2,1)S(1)}, u32[]{:S(2)}, u32[]{:S(2)}) async-start(bf16[32,16,128]{2,1,0:T(8,128)(2,1)} %contract.1), calls=%async_computation.1 | async-start | bytes 262144 | tf_op jit(solution)/shard_map/all_to_all | solution.py:95
  23.4 0.0 copy-start.3
  23.4 0.0 copy-start.4
  23.4 0.0 copy-done.1
  23.4 0.0 copy-done
  23.4 0.0 copy-done.2
  23.5 0.6 %copy-done.3 = f32[128]{0:T(128)S(1)} copy-done((f32[128]{0:T(128)S(1)}, f32[128]{0:T(128)}, u32[]{:S(2)}) %copy-start.3) | copy-done | bytes 536
  24.1 0.0 copy-done.4
  24.1 0.2 gate.1
  24.3 7.5 %all-to-all-done.1.blocks_ref = bf16[32,16,128]{2,1,0:T(8,128)(2,1)S(1)} async-done(((bf16[32,16,128]{2,1,0:T(8,128)(2,1)}), bf16[32,16,128]{2,1,0:T(8,128)(2,1)S(1)}, u32[]{:S(2)}, u32[]{:S(2)}) %all-to-all-start.1) | async-done | bytes 131104 | tf_op jit(solution)/shard_map/all_to_all | solution.py:95
  31.8 1.0 %finish.1 = bf16[4,128,128]{2,1,0:T(8,128)(2,1)} custom-call(bf16[32,16,128]{2,1,0:T(8,128)(2,1)S(1)} %all-to-all-done.1.blocks_ref, bf16[512,128]{1,0:T(8,128)(2,1)S(1)} %get-tuple-element.12.gate_ref, f32[2,128,128]{2,1,0:T(8,128)S(1)} %get-tuple-element.13.scales_ref, bf16[128,128]{1,0:T(8,128)(2,1)S(1)} %get-tuple-element.14.w_ref), custom_call_target="tpu_custom_call" | custom-call | tf_op jit(solution)/shard_map/finish/pallas_call | solution.py:196
Async XLA Ops:
  19.8 3.7 %copy-start.1 = (bf16[512,128]{1,0:T(8,128)(2,1)S(1)}, bf16[512,128]{1,0:T(8,128)(2,1)}, u32[]{:S(2)}) copy-start(bf16[512,128]{1,0:T(8,128)(2,1)} %get-tuple-element.11.normed_ref) | copy-start | bytes 393220
  20.7 2.8 %copy-start = (bf16[128,640]{1,0:T(8,128)(2,1)S(1)}, bf16[128,640]{1,0:T(8,128)(2,1)}, u32[]{:S(2)}) copy-start(bf16[128,640]{1,0:T(8,128)(2,1)} %w_ref.1) | copy-start | bytes 491524
  20.7 2.8 %copy-start.2 = (bf16[128,128]{1,0:T(8,128)(2,1)S(1)}, bf16[128,128]{1,0:T(8,128)(2,1)}, u32[]{:S(2)}) copy-start(bf16[128,128]{1,0:T(8,128)(2,1)} %w_out_ref.1) | copy-start | bytes 98308
  20.7 11.1 %all-to-all-start.1 = ((bf16[32,16,128]{2,1,0:T(8,128)(2,1)}), bf16[32,16,128]{2,1,0:T(8,128)(2,1)S(1)}, u32[]{:S(2)}, u32[]{:S(2)}) async-start(bf16[32,16,128]{2,1,0:T(8,128)(2,1)} %contract.1), calls=%async_computation.1 | async-start | bytes 262144 | tf_op jit(solution)/shard_map/all_to_all | solution.py:95
  23.4 0.7 %copy-start.3 = (f32[128]{0:T(128)S(1)}, f32[128]{0:T(128)}, u32[]{:S(2)}) copy-start(f32[128]{0:T(128)} %param.13) | copy-start | bytes 1540
  23.4 0.7 %copy-start.4 = (f32[128]{0:T(128)S(1)}, f32[128]{0:T(128)}, u32[]{:S(2)}) copy-start(f32[128]{0:T(128)} %param.14) | copy-start | bytes 1540

commit v11 on v10

--- a/solution.py
+++ b/solution.py
@@ -78,7 +78,7 @@
 
 def group_order(shards):
     size = shards // planes
-    return [plane * size + place for place in range(size) for plane in range(planes)]
+    return [plane * size + place for place in range(size) for plane in range(planes)][::-1]
 
 
 def spot(device, shards):

time: 33.1 us -> 33.4 us (level)
  blocking collectives: 17.5 us -> 18.4 us
  waiting for transfers between devices: 7.54 us -> 6.98 us
    all_to_all x1, blocking collectives: 17.5 us -> 18.4 us  [exchange(): lax.all_to_all(blocks, axes, split_axis=0, concat_axis=0, axis_index_grou...]
    all_to_all x1, waiting for transfers between devices: 7.54 us -> 6.98 us  [exchange(): lax.all_to_all(blocks, axes, split_axis=0, concat_axis=0, axis_index_grou...]
where the time goes in v11:
time: 33.4 us; the launch traced here: 33.1 us
  blocking collectives  18.4 us (55%)
  waiting for transfers between devices  6.98 us (21%)
  Pallas kernels  4.29 us (13%)
  starting transfers between devices  2.7 us (8%)
  local copies, waits for them, and re-layouts  0.64 us (2%)
    all_to_all x1, blocking collectives, exchange(): lax.all_to_all(blocks, axes, split_axis=0, concat_axis=0, axis_index_grou...  18.4 us
    all_to_all x1, waiting for transfers between devices, exchange(): lax.all_to_all(blocks, axes, split_axis=0, concat_axis=0, axis_index_grou...  6.98 us
    all_to_all x1, starting transfers between devices, exchange(): lax.all_to_all(blocks, axes, split_axis=0, concat_axis=0, axis_index_grou...  2.7 us
    pallas_call x1, Pallas kernels, local_blocks(): pl.pallas_call(project_kernel, out_shape=(shaped(shards, 8 * row_count, c...  2.24 us
    pallas_call x1, Pallas kernels, local_blocks(): pl.pallas_call(finish_kernel, out_shape=shaped(row_count, col_count, chan...  0.98 us
    pallas_call x1, Pallas kernels, local_blocks(): pl.pallas_call(contract_kernel, out_shape=shaped(shards, 4 * row_count, c...  0.89 us
  transfers between devices with their start and end apart: 1, of which 1 were waited for; matrix products, arithmetic and copies ran while one was open for 0% of the time, Pallas kernels for 1%

profile of v11, /device:TPU:0, one launch (start us, length us, event | category | flops | bytes accessed | tf_op | source)
XLA Modules:
  0.0 33.1 jit_solution(4364071293612434602)
XLA Ops:
  0.0 2.2 %project.1 = (bf16[32,32,128]{2,1,0:T(8,128)(2,1)}, bf16[512,128]{1,0:T(8,128)(2,1)}) custom-call(bf16[4,128,128]{2,1,0:T(8,128)(2,1)} %pair_hbm.1, s32[1,128]{1,0:T(1,128)} %bitcast.7, f32[1,128]{1,0:T(1,128)} %bitcast.8, f32[1,128]{1,0:T(1,128)} %bitcast.9, bf16[128,640]{1,0:T(8,128)(2,1)} %w_ref.1), custom_call_target="tpu_custom_call" | custom-call | tf_op jit(solution)/shard_map/project/pallas_call | solution.py:158
  2.3 18.4 %all_to_all.10.blocks_ref = bf16[32,32,128]{2,1,0:T(8,128)(2,1)S(1)} all-to-all(bf16[32,32,128]{2,1,0:T(8,128)(2,1)} %get-tuple-element.10), channel_id=1, replica_groups={{31,23,15,7,30,22,14,6,29,21,13,5,28,20,12,4,27,19,11,3,26,18,10,2,25,1..., dimensions={0} | all-to-all | bytes 524288 | tf_op jit(solution)/shard_map/all_to_all | solution.py:95
  20.7 0.0 copy-start.1
  20.7 0.9 %contract.1 = bf16[32,16,128]{2,1,0:T(8,128)(2,1)} custom-call(bf16[32,32,128]{2,1,0:T(8,128)(2,1)S(1)} %all_to_all.10.blocks_ref), custom_call_target="tpu_custom_call" | custom-call | tf_op jit(solution)/shard_map/contract/pallas_call | solution.py:174
  21.6 0.0 copy-start
  21.6 0.0 copy-start.2
  21.6 2.7 %all-to-all-start.1 = ((bf16[32,16,128]{2,1,0:T(8,128)(2,1)}), bf16[32,16,128]{2,1,0:T(8,128)(2,1)S(1)}, u32[]{:S(2)}, u32[]{:S(2)}) async-start(bf16[32,16,128]{2,1,0:T(8,128)(2,1)} %contract.1), calls=%async_computation.1 | async-start | bytes 262144 | tf_op jit(solution)/shard_map/all_to_all | solution.py:95
  24.3 0.0 copy-start.3
  24.3 0.0 copy-start.4
  24.3 0.0 copy-done.1
  24.3 0.0 copy-done
  24.3 0.0 copy-done.2
  24.4 0.6 %copy-done.3 = f32[128]{0:T(128)S(1)} copy-done((f32[128]{0:T(128)S(1)}, f32[128]{0:T(128)}, u32[]{:S(2)}) %copy-start.3) | copy-done | bytes 536
  25.0 0.0 copy-done.4
  25.0 0.2 gate.1
  25.2 7.0 %all-to-all-done.1.blocks_ref = bf16[32,16,128]{2,1,0:T(8,128)(2,1)S(1)} async-done(((bf16[32,16,128]{2,1,0:T(8,128)(2,1)}), bf16[32,16,128]{2,1,0:T(8,128)(2,1)S(1)}, u32[]{:S(2)}, u32[]{:S(2)}) %all-to-all-start.1) | async-done | bytes 131104 | tf_op jit(solution)/shard_map/all_to_all | solution.py:95
  32.1 1.0 %finish.1 = bf16[4,128,128]{2,1,0:T(8,128)(2,1)} custom-call(bf16[32,16,128]{2,1,0:T(8,128)(2,1)S(1)} %all-to-all-done.1.blocks_ref, bf16[512,128]{1,0:T(8,128)(2,1)S(1)} %get-tuple-element.12.gate_ref, f32[2,128,128]{2,1,0:T(8,128)S(1)} %get-tuple-element.13.scales_ref, bf16[128,128]{1,0:T(8,128)(2,1)S(1)} %get-tuple-element.14.w_ref), custom_call_target="tpu_custom_call" | custom-call | tf_op jit(solution)/shard_map/finish/pallas_call | solution.py:196
Async XLA Ops:
  20.7 3.6 %copy-start.1 = (bf16[512,128]{1,0:T(8,128)(2,1)S(1)}, bf16[512,128]{1,0:T(8,128)(2,1)}, u32[]{:S(2)}) copy-start(bf16[512,128]{1,0:T(8,128)(2,1)} %get-tuple-element.11.normed_ref) | copy-start | bytes 393220
  21.6 2.7 %copy-start = (bf16[128,640]{1,0:T(8,128)(2,1)S(1)}, bf16[128,640]{1,0:T(8,128)(2,1)}, u32[]{:S(2)}) copy-start(bf16[128,640]{1,0:T(8,128)(2,1)} %w_ref.1) | copy-start | bytes 491524
  21.6 2.8 %copy-start.2 = (bf16[128,128]{1,0:T(8,128)(2,1)S(1)}, bf16[128,128]{1,0:T(8,128)(2,1)}, u32[]{:S(2)}) copy-start(bf16[128,128]{1,0:T(8,128)(2,1)} %w_out_ref.1) | copy-start | bytes 98308
  21.6 10.6 %all-to-all-start.1 = ((bf16[32,16,128]{2,1,0:T(8,128)(2,1)}), bf16[32,16,128]{2,1,0:T(8,128)(2,1)S(1)}, u32[]{:S(2)}, u32[]{:S(2)}) async-start(bf16[32,16,128]{2,1,0:T(8,128)(2,1)} %contract.1), calls=%async_computation.1 | async-start | bytes 262144 | tf_op jit(solution)/shard_map/all_to_all | solution.py:95
  24.3 0.7 %copy-start.3 = (f32[128]{0:T(128)S(1)}, f32[128]{0:T(128)}, u32[]{:S(2)}) copy-start(f32[128]{0:T(128)} %param.13) | copy-start | bytes 1540
  24.3 0.7 %copy-start.4 = (f32[128]{0:T(128)S(1)}, f32[128]{0:T(128)}, u32[]{:S(2)}) copy-start(f32[128]{0:T(128)} %param.14) | copy-start | bytes 1540

commit v12 on v9

--- a/solution.py
+++ b/solution.py
@@ -88,7 +88,10 @@
     )
 
 
-def contract_kernel(blocks_ref, out_ref, held_ref):
+def contract_kernel(
+    blocks_ref, normed_ref, w_ref, gain_ref, bias_ref, w_out_ref,
+    out_ref, gate_ref, scales_ref, weights_ref, held_ref,
+):
     total = held_ref.shape[0] // 8
     receive_blocks(blocks_ref, held_ref)
     products = []
@@ -106,14 +109,9 @@
         for half in range(2):
             rows = jnp.concatenate([low[half], high[half]], axis=0)
             out_ref[(row // 4 + half) ^ hub] = rows.astype(jnp.bfloat16)
-
-
-def gate_kernel(normed_ref, w_ref, gain_ref, bias_ref, w_out_ref, out_ref, scales_ref, weights_ref):
     chan_count = normed_ref.shape[1]
-    projected = jnp.dot(
-        normed_ref[...], w_ref[:, 4 * chan_count :], preferred_element_type=jnp.float32
-    )
-    out_ref[...] = jax.nn.sigmoid(projected).astype(jnp.bfloat16)
+    gate = jnp.dot(normed_ref[...], w_ref[:, 4 * chan_count :], preferred_element_type=jnp.float32)
+    gate_ref[...] = jax.nn.sigmoid(gate).astype(jnp.bfloat16)
     for i, vector_ref in enumerate((gain_ref, bias_ref)):
         scales_ref[i] = jnp.transpose(jnp.broadcast_to(vector_ref[...], scales_ref.shape[1:]))
     weights_ref[...] = w_out_ref[...]
@@ -145,11 +143,15 @@
     def shaped(*dims):
         return jax.ShapeDtypeStruct(dims, jnp.bfloat16)
 
+    def in_hbm(array):
+        return pltpu.with_memory_space_constraint(array, pltpu.HBM)
+
+    limit = pltpu.CompilerParams(vmem_limit_bytes=kernel_vmem)
     sides, normed = pl.pallas_call(
         project_kernel,
         out_shape=(shaped(shards, 8 * row_count, col_count), shaped(tokens, chan_count)),
         in_specs=[hbm] * 5,
-        out_specs=(vmem, vmem),
+        out_specs=(vmem,) * 2,
         scratch_shapes=[
             pltpu.VMEM(pair.shape, jnp.bfloat16),
             pltpu.VMEM((1, col_count), jnp.int32),
@@ -158,38 +160,32 @@
             pltpu.VMEM((chan_count, 4 * chan_count), jnp.bfloat16),
             pltpu.SemaphoreType.DMA((5,)),
         ],
+        compiler_params=limit,
         name="project",
-    )(pair, line(valid), line(norm_gain), line(norm_bias), w_proj)
+    )(*map(in_hbm, (pair, line(valid), line(norm_gain), line(norm_bias), w_proj)))
     sides = exchange(sides)
-    triangle = pl.pallas_call(
+    triangle, gate_values, scales, weights = pl.pallas_call(
         contract_kernel,
-        out_shape=shaped(shards, 4 * row_count, col_count),
-        in_specs=[vmem],
-        out_specs=vmem,
-        scratch_shapes=[pltpu.VMEM((8 * col_count, col_count), jnp.float32)],
-        compiler_params=pltpu.CompilerParams(vmem_limit_bytes=kernel_vmem),
-        name="contract",
-    )(sides)
-    triangle = exchange(triangle)
-    gate_values, scales, weights = pl.pallas_call(
-        gate_kernel,
         out_shape=(
+            shaped(shards, 4 * row_count, col_count),
             shaped(tokens, chan_count),
             jax.ShapeDtypeStruct((2, chan_count, col_count), jnp.float32),
             shaped(chan_count, chan_count),
         ),
-        in_specs=[vmem] * 5,
-        out_specs=(vmem,) * 3,
-        compiler_params=pltpu.CompilerParams(vmem_limit_bytes=kernel_vmem),
-        name="gate",
-    )(normed, w_proj, line(out_gain), line(out_bias), w_out)
+        in_specs=[vmem] * 6,
+        out_specs=(vmem,) * 4,
+        scratch_shapes=[pltpu.VMEM((8 * col_count, col_count), jnp.float32)],
+        compiler_params=limit,
+        name="contract",
+    )(sides, normed, w_proj, line(out_gain), line(out_bias), w_out)
+    triangle = exchange(triangle)
     return pl.pallas_call(
         finish_kernel,
         out_shape=shaped(row_count, col_count, chan_count),
         in_specs=[vmem] * 4,
         out_specs=vmem,
         scratch_shapes=[pltpu.VMEM((tokens, chan_count), jnp.float32)],
-        compiler_params=pltpu.CompilerParams(vmem_limit_bytes=kernel_vmem),
+        compiler_params=limit,
         name="finish",
     )(triangle, gate_values, scales, weights)
 

time: 32.7 us -> 31.5 us (0.963)
  blocking collectives: 17.2 us -> 27.8 us
  waiting for transfers between devices: 7.05 us -> 0 us
  starting transfers between devices: 3.07 us -> 0 us
  Pallas kernels: 4.29 us -> 2.79 us
    all_to_all x1 -> x2, blocking collectives: 17.2 us -> 27.8 us  [exchange(): lax.all_to_all(blocks, axes, split_axis=0, concat_axis=0, axis_index_grou...]
    all_to_all x1 -> x0, waiting for transfers between devices: 7.05 us -> none  [exchange(): lax.all_to_all(blocks, axes, split_axis=0, concat_axis=0, axis_index_grou...]
    all_to_all x1 -> x0, starting transfers between devices: 3.07 us -> none  [exchange(): lax.all_to_all(blocks, axes, split_axis=0, concat_axis=0, axis_index_grou...]
    pallas_call x2 -> x1, Pallas kernels: 1.07 us -> 0.27 us  [local_blocks(): pl.pallas_call(contract_kernel, out_shape=(shaped(shards, 4 * row_count,...]
    pallas_call x1, Pallas kernels: 2.24 us -> 1.55 us  [local_blocks(): pl.pallas_call(project_kernel, out_shape=(shaped(shards, 8 * row_count, c...]
    unnamed x10 -> x8, local copies, waits for them, and re-layouts: 0.64 us -> 0.67 us
  transfers between devices with their start and end apart: 1 -> 0, of which waited for: 1 -> 0; matrix products, arithmetic and copies ran while one was open for 0% -> 0% of each run, Pallas kernels for 1% -> 0%
where the time goes in v12:
time: 31.5 us; the launch traced here: 31.3 us
  blocking collectives  27.8 us (88%)
  Pallas kernels  2.79 us (9%)
  local copies, waits for them, and re-layouts  0.67 us (2%)
    all_to_all x2, blocking collectives, exchange(): lax.all_to_all(blocks, axes, split_axis=0, concat_axis=0, axis_index_grou...  27.8 us
    pallas_call x1, Pallas kernels, local_blocks(): pl.pallas_call(project_kernel, out_shape=(shaped(shards, 8 * row_count, c...  1.55 us
    pallas_call x1, Pallas kernels, local_blocks(): pl.pallas_call(finish_kernel, out_shape=shaped(row_count, col_count, chan...  0.98 us
    unnamed x8, local copies, waits for them, and re-layouts  0.67 us

profile of v12, /device:TPU:0, one launch (start us, length us, event | category | flops | bytes accessed | tf_op | source)
XLA Modules:
  0.0 31.3 jit_solution(1869018298748722576)
XLA Ops:
  0.0 1.5 %project.1 = (bf16[32,32,128]{2,1,0:T(8,128)(2,1)S(1)}, bf16[512,128]{1,0:T(8,128)(2,1)S(1)}) custom-call(bf16[4,128,128]{2,1,0:T(8,128)(2,1)} %pair_hbm.1, s32[1,128]{1,0:T(1,128)} %bitcast.7, f32[1,128]{1,0:T(1,128)} %bitcast.8, f32[1,128]{1,0:T(1,128)} %bitcast.9, bf16[128,640]{1,0:T(8,128)(2,1)} %w_ref.1), custom_call_target="tpu_custom_call" | custom-call | tf_op jit(solution)/shard_map/project/pallas_call | solution.py:150
  1.6 0.0 copy-start
  1.6 0.0 copy-start.1
  1.6 17.0 %all_to_all.10.blocks_ref = bf16[32,32,128]{2,1,0:T(8,128)(2,1)S(1)} all-to-all(bf16[32,32,128]{2,1,0:T(8,128)(2,1)S(1)} %get-tuple-element.11), channel_id=1, replica_groups={{31,30,29,28,27,26,25,24,23,22,21,20,19,18,17,16,15,14,13,12,11,10,9,8,..., dimensions={0} | all-to-all | bytes 524288 | tf_op jit(solution)/shard_map/all_to_all | solution.py:86
  18.6 0.0 copy-start.2
  18.6 0.0 copy-start.3
  18.6 0.0 copy-done
  18.6 0.0 copy-done.1
  18.6 0.6 %copy-done.2 = f32[128]{0:T(128)S(1)} copy-done((f32[128]{0:T(128)S(1)}, f32[128]{0:T(128)}, u32[]{:S(2)}) %copy-start.2) | copy-done | bytes 536
  19.3 0.0 copy-done.3
  19.3 0.3 contract.1
  19.6 10.8 %all_to_all.11.blocks_ref = bf16[32,16,128]{2,1,0:T(8,128)(2,1)S(1)} all-to-all(bf16[32,16,128]{2,1,0:T(8,128)(2,1)S(1)} %get-tuple-element.13), channel_id=1, replica_groups={{31,30,29,28,27,26,25,24,23,22,21,20,19,18,17,16,15,14,13,12,11,10,9,8,..., dimensions={0} | all-to-all | bytes 262144 | tf_op jit(solution)/shard_map/all_to_all | solution.py:86
  30.4 1.0 %finish.1 = bf16[4,128,128]{2,1,0:T(8,128)(2,1)} custom-call(bf16[32,16,128]{2,1,0:T(8,128)(2,1)S(1)} %all_to_all.11.blocks_ref, bf16[512,128]{1,0:T(8,128)(2,1)S(1)} %get-tuple-element.14.gate_ref, f32[2,128,128]{2,1,0:T(8,128)S(1)} %get-tuple-element.15.scales_ref, bf16[128,128]{1,0:T(8,128)(2,1)S(1)} %get-tuple-element.16.w_ref), custom_call_target="tpu_custom_call" | custom-call | tf_op jit(solution)/shard_map/finish/pallas_call | solution.py:182
Async XLA Ops:
  1.6 17.1 %copy-start = (bf16[128,640]{1,0:T(8,128)(2,1)S(1)}, bf16[128,640]{1,0:T(8,128)(2,1)}, u32[]{:S(2)}) copy-start(bf16[128,640]{1,0:T(8,128)(2,1)} %w_ref.1) | copy-start | bytes 491524
  1.6 17.1 %copy-start.1 = (bf16[128,128]{1,0:T(8,128)(2,1)S(1)}, bf16[128,128]{1,0:T(8,128)(2,1)}, u32[]{:S(2)}) copy-start(bf16[128,128]{1,0:T(8,128)(2,1)} %w_out_ref.1) | copy-start | bytes 98308
  18.6 0.7 %copy-start.2 = (f32[128]{0:T(128)S(1)}, f32[128]{0:T(128)}, u32[]{:S(2)}) copy-start(f32[128]{0:T(128)} %param.13) | copy-start | bytes 1540
  18.6 0.7 %copy-start.3 = (f32[128]{0:T(128)S(1)}, f32[128]{0:T(128)}, u32[]{:S(2)}) copy-start(f32[128]{0:T(128)} %param.14) | copy-start | bytes 1540

commit v13 on v12

--- a/solution.py
+++ b/solution.py
@@ -29,7 +29,8 @@
 
 
 def project_kernel(
-    pair_hbm, valid_hbm, gain_hbm, bias_hbm, w_hbm, out_ref, normed_ref,
+    pair_hbm, valid_hbm, gain_hbm, bias_hbm, w_hbm, out_gain_hbm, out_bias_hbm, w_out_hbm,
+    out_ref, normed_ref, w_gate_ref, out_gain_ref, out_bias_ref, w_out_ref,
     pair_ref, valid_ref, gain_ref, bias_ref, w_ref, sems,
 ):
     row_count, col_count, chan_count = pair_ref.shape
@@ -38,6 +39,8 @@
         for i, (source, held) in enumerate((
             (pair_hbm, pair_ref), (gain_hbm, gain_ref), (bias_hbm, bias_ref),
             (w_hbm.at[:, : 4 * chan_count], w_ref), (valid_hbm, valid_ref),
+            (w_hbm.at[:, 4 * chan_count :], w_gate_ref), (out_gain_hbm, out_gain_ref),
+            (out_bias_hbm, out_bias_ref), (w_out_hbm, w_out_ref),
         ))
     ]
     for fetch in fetches:
@@ -48,7 +51,7 @@
     tokens = pair_ref[...].reshape(row_count * col_count, chan_count).astype(jnp.float32)
     normed = layer_norm(tokens, gain_ref[...], bias_ref[...], 1).astype(jnp.bfloat16)
     normed_ref[...] = normed
-    for fetch in fetches[3:]:
+    for fetch in fetches[3:5]:
         fetch.wait()
     projected = lax.dot_general(
         w_ref[...], normed, (((0,), (1,)), ((), ())),
@@ -73,6 +76,8 @@
                     [block[:, (r + i) * col_count : (r + i + 1) * col_count] for i in range(2)], axis=0
                 )
                 out_ref[(chan // 4 + half) ^ hub, r * 8 : (r + 2) * 8, :] = rows.astype(jnp.bfloat16)
+    for fetch in fetches[5:]:
+        fetch.wait()
 
 
 def receive_blocks(blocks_ref, held_ref):
@@ -89,8 +94,8 @@
 
 
 def contract_kernel(
-    blocks_ref, normed_ref, w_ref, gain_ref, bias_ref, w_out_ref,
-    out_ref, gate_ref, scales_ref, weights_ref, held_ref,
+    blocks_ref, normed_ref, w_gate_ref, gain_ref, bias_ref,
+    out_ref, gate_ref, scales_ref, held_ref,
 ):
     total = held_ref.shape[0] // 8
     receive_blocks(blocks_ref, held_ref)
@@ -109,12 +114,10 @@
         for half in range(2):
             rows = jnp.concatenate([low[half], high[half]], axis=0)
             out_ref[(row // 4 + half) ^ hub] = rows.astype(jnp.bfloat16)
-    chan_count = normed_ref.shape[1]
-    gate = jnp.dot(normed_ref[...], w_ref[:, 4 * chan_count :], preferred_element_type=jnp.float32)
+    gate = jnp.dot(normed_ref[...], w_gate_ref[...], preferred_element_type=jnp.float32)
     gate_ref[...] = jax.nn.sigmoid(gate).astype(jnp.bfloat16)
     for i, vector_ref in enumerate((gain_ref, bias_ref)):
         scales_ref[i] = jnp.transpose(jnp.broadcast_to(vector_ref[...], scales_ref.shape[1:]))
-    weights_ref[...] = w_out_ref[...]
 
 
 def finish_kernel(blocks_ref, gate_ref, scales_ref, w_ref, out_ref, held_ref):
@@ -147,37 +150,44 @@
         return pltpu.with_memory_space_constraint(array, pltpu.HBM)
 
     limit = pltpu.CompilerParams(vmem_limit_bytes=kernel_vmem)
-    sides, normed = pl.pallas_call(
+    vector = jax.ShapeDtypeStruct((1, chan_count), jnp.float32)
+    square = shaped(chan_count, chan_count)
+    sides, normed, w_gate, out_gain, out_bias, w_out = pl.pallas_call(
         project_kernel,
-        out_shape=(shaped(shards, 8 * row_count, col_count), shaped(tokens, chan_count)),
-        in_specs=[hbm] * 5,
-        out_specs=(vmem,) * 2,
+        out_shape=(
+            shaped(shards, 8 * row_count, col_count), shaped(tokens, chan_count),
+            square, vector, vector, square,
+        ),
+        in_specs=[hbm] * 8,
+        out_specs=(vmem,) * 6,
         scratch_shapes=[
             pltpu.VMEM(pair.shape, jnp.bfloat16),
             pltpu.VMEM((1, col_count), jnp.int32),
             pltpu.VMEM((1, chan_count), jnp.float32),
             pltpu.VMEM((1, chan_count), jnp.float32),
             pltpu.VMEM((chan_count, 4 * chan_count), jnp.bfloat16),
-            pltpu.SemaphoreType.DMA((5,)),
+            pltpu.SemaphoreType.DMA((9,)),
         ],
         compiler_params=limit,
         name="project",
-    )(*map(in_hbm, (pair, line(valid), line(norm_gain), line(norm_bias), w_proj)))
+    )(*map(in_hbm, (
+        pair, line(valid), line(norm_gain), line(norm_bias), w_proj,
+        line(out_gain), line(out_bias), w_out,
+    )))
     sides = exchange(sides)
-    triangle, gate_values, scales, weights = pl.pallas_call(
+    triangle, gate_values, scales = pl.pallas_call(
         contract_kernel,
         out_shape=(
             shaped(shards, 4 * row_count, col_count),
             shaped(tokens, chan_count),
             jax.ShapeDtypeStruct((2, chan_count, col_count), jnp.float32),
-            shaped(chan_count, chan_count),
         ),
-        in_specs=[vmem] * 6,
-        out_specs=(vmem,) * 4,
+        in_specs=[vmem] * 5,
+        out_specs=(vmem,) * 3,
         scratch_shapes=[pltpu.VMEM((8 * col_count, col_count), jnp.float32)],
         compiler_params=limit,
         name="contract",
-    )(sides, normed, w_proj, line(out_gain), line(out_bias), w_out)
+    )(sides, normed, w_gate, out_gain, out_bias)
     triangle = exchange(triangle)
     return pl.pallas_call(
         finish_kernel,
@@ -187,7 +197,7 @@
         scratch_shapes=[pltpu.VMEM((tokens, chan_count), jnp.float32)],
         compiler_params=limit,
         name="finish",
-    )(triangle, gate_values, scales, weights)
+    )(triangle, gate_values, scales, w_out)
 
 
 def local_arrays(pair, valid, norm_gain, norm_bias, w_proj, out_gain, out_bias, w_out):

time: 31.5 us -> 30.8 us (0.978)
  local copies, waits for them, and re-layouts: 0.67 us -> 0 us
    unnamed x8 -> x0, local copies, waits for them, and re-layouts: 0.67 us -> none
where the time goes in v13:
time: 30.8 us; the launch traced here: 30.7 us
  blocking collectives  27.8 us (90%)
  Pallas kernels  2.84 us (9%)
    all_to_all x2, blocking collectives, exchange(): lax.all_to_all(blocks, axes, split_axis=0, concat_axis=0, axis_index_grou...  27.8 us
    pallas_call x1, Pallas kernels, local_blocks(): pl.pallas_call(project_kernel, out_shape=(shaped(shards, 8 * row_count, c...  1.59 us
    pallas_call x1, Pallas kernels, local_blocks(): pl.pallas_call(finish_kernel, out_shape=shaped(row_count, col_count, chan...  0.97 us

profile of v13, /device:TPU:0, one launch (start us, length us, event | category | flops | bytes accessed | tf_op | source)
XLA Modules:
  0.0 30.7 jit_solution(6469701086352238483)
XLA Ops:
  0.0 1.6 %project.1 = (bf16[32,32,128]{2,1,0:T(8,128)(2,1)S(1)}, bf16[512,128]{1,0:T(8,128)(2,1)S(1)}, bf16[128,128]{1,0:T(8,128)(2,1)S(1)}, f32[1,128]{1,0:T(1,128)S(1)}...) custom-call(bf16[4,128,128]{2,1,0:T(8,128)(2,1)} %pair_hbm.1, s32[1,128]{1,0:T(1,128)} %bitcast.5, f32[1,128]{1,0:T(1,128)} %bitcast.6, ...), custom_call_target="tpu_custom_call" | custom-call | tf_op jit(solution)/shard_map/project/pallas_call | solution.py:155
  1.6 17.0 %all_to_all.10.blocks_ref = bf16[32,32,128]{2,1,0:T(8,128)(2,1)S(1)} all-to-all(bf16[32,32,128]{2,1,0:T(8,128)(2,1)S(1)} %get-tuple-element.14), channel_id=1, replica_groups={{31,30,29,28,27,26,25,24,23,22,21,20,19,18,17,16,15,14,13,12,11,10,9,8,..., dimensions={0} | all-to-all | bytes 524288 | tf_op jit(solution)/shard_map/all_to_all | solution.py:91
  18.6 0.3 contract.1
  18.9 10.8 %all_to_all.11.blocks_ref = bf16[32,16,128]{2,1,0:T(8,128)(2,1)S(1)} all-to-all(bf16[32,16,128]{2,1,0:T(8,128)(2,1)S(1)} %get-tuple-element.19), channel_id=1, replica_groups={{31,30,29,28,27,26,25,24,23,22,21,20,19,18,17,16,15,14,13,12,11,10,9,8,..., dimensions={0} | all-to-all | bytes 262144 | tf_op jit(solution)/shard_map/all_to_all | solution.py:91
  29.7 1.0 %finish.1 = bf16[4,128,128]{2,1,0:T(8,128)(2,1)} custom-call(bf16[32,16,128]{2,1,0:T(8,128)(2,1)S(1)} %all_to_all.11.blocks_ref, bf16[512,128]{1,0:T(8,128)(2,1)S(1)} %get-tuple-element.20.gate_ref, f32[2,128,128]{2,1,0:T(8,128)S(1)} %get-tuple-element.21.scales_ref, bf16[128,128]{1,0:T(8,128)(2,1)S(1)} %get-tuple-element.22.w_ref), custom_call_target="tpu_custom_call" | custom-call | tf_op jit(solution)/shard_map/finish/pallas_call | solution.py:192

commit v14 on v13

--- a/solution.py
+++ b/solution.py
@@ -20,6 +20,10 @@
     return centered * lax.rsqrt(variance + epsilon) * gain_vec + bias_vec
 
 
+def sigmoid(values):
+    return 0.5 + 0.5 * jnp.tanh(0.5 * values)
+
+
 def swap_halves(low, high):
     first = lax.broadcasted_iota(jnp.int32, low.shape, 0) < 4
     return (
@@ -34,25 +38,28 @@
     pair_ref, valid_ref, gain_ref, bias_ref, w_ref, sems,
 ):
     row_count, col_count, chan_count = pair_ref.shape
+    quarter = chan_count // 4
+    pairs = [(pair_hbm.at[r], pair_ref.at[r]) for r in range(row_count)]
+    for i in range(0, chan_count, quarter):
+        rows = pl.ds(i, quarter)
+        pairs.append((w_hbm.at[rows, : 4 * chan_count], w_ref.at[rows]))
+    pairs += [(gain_hbm, gain_ref), (bias_hbm, bias_ref), (valid_hbm, valid_ref)]
+    needed = len(pairs)
+    pairs += [
+        (w_hbm.at[:, 4 * chan_count :], w_gate_ref), (out_gain_hbm, out_gain_ref),
+        (out_bias_hbm, out_bias_ref), (w_out_hbm, w_out_ref),
+    ]
     fetches = [
-        pltpu.make_async_copy(source, held, sems.at[i])
-        for i, (source, held) in enumerate((
-            (pair_hbm, pair_ref), (gain_hbm, gain_ref), (bias_hbm, bias_ref),
-            (w_hbm.at[:, : 4 * chan_count], w_ref), (valid_hbm, valid_ref),
-            (w_hbm.at[:, 4 * chan_count :], w_gate_ref), (out_gain_hbm, out_gain_ref),
-            (out_bias_hbm, out_bias_ref), (w_out_hbm, w_out_ref),
-        ))
+        pltpu.make_async_copy(source, held, sems.at[i]) for i, (source, held) in enumerate(pairs)
     ]
     for fetch in fetches:
         fetch.start()
     row_start = lax.axis_index(axes) * row_count
-    for fetch in fetches[:3]:
+    for fetch in fetches[:needed]:
         fetch.wait()
     tokens = pair_ref[...].reshape(row_count * col_count, chan_count).astype(jnp.float32)
     normed = layer_norm(tokens, gain_ref[...], bias_ref[...], 1).astype(jnp.bfloat16)
     normed_ref[...] = normed
-    for fetch in fetches[3:5]:
-        fetch.wait()
     projected = lax.dot_general(
         w_ref[...], normed, (((0,), (1,)), ((), ())),
         preferred_element_type=jnp.float32,
@@ -68,15 +75,15 @@
         a_gate, a, b_gate, b = (
             projected[i * chan_count + chan : i * chan_count + chan + 8] for i in range(4)
         )
-        left = jax.nn.sigmoid(a_gate) * a * flags
-        right = jax.nn.sigmoid(b_gate) * b * flags
+        left = sigmoid(a_gate) * a * flags
+        right = sigmoid(b_gate) * b * flags
         for half, block in enumerate(swap_halves(left, right)):
             for r in range(0, row_count, 2):
                 rows = jnp.concatenate(
                     [block[:, (r + i) * col_count : (r + i + 1) * col_count] for i in range(2)], axis=0
                 )
                 out_ref[(chan // 4 + half) ^ hub, r * 8 : (r + 2) * 8, :] = rows.astype(jnp.bfloat16)
-    for fetch in fetches[5:]:
+    for fetch in fetches[needed:]:
         fetch.wait()
 
 
@@ -115,7 +122,7 @@
             rows = jnp.concatenate([low[half], high[half]], axis=0)
             out_ref[(row // 4 + half) ^ hub] = rows.astype(jnp.bfloat16)
     gate = jnp.dot(normed_ref[...], w_gate_ref[...], preferred_element_type=jnp.float32)
-    gate_ref[...] = jax.nn.sigmoid(gate).astype(jnp.bfloat16)
+    gate_ref[...] = sigmoid(gate).astype(jnp.bfloat16)
     for i, vector_ref in enumerate((gain_ref, bias_ref)):
         scales_ref[i] = jnp.transpose(jnp.broadcast_to(vector_ref[...], scales_ref.shape[1:]))
 
@@ -166,7 +173,7 @@
             pltpu.VMEM((1, chan_count), jnp.float32),
             pltpu.VMEM((1, chan_count), jnp.float32),
             pltpu.VMEM((chan_count, 4 * chan_count), jnp.bfloat16),
-            pltpu.SemaphoreType.DMA((9,)),
+            pltpu.SemaphoreType.DMA((row_count + 11,)),
         ],
         compiler_params=limit,
         name="project",

time: 30.8 us -> 30.9 us (level)
  no operation moved by 1% of the time
where the time goes in v14:
time: 30.9 us; the launch traced here: 30.6 us
  blocking collectives  27.8 us (90%)
  Pallas kernels  2.8 us (9%)
    all_to_all x2, blocking collectives, exchange(): lax.all_to_all(blocks, axes, split_axis=0, concat_axis=0, axis_index_grou...  27.8 us
    pallas_call x1, Pallas kernels, local_blocks(): pl.pallas_call(project_kernel, out_shape=(shaped(shards, 8 * row_count, c...  1.55 us
    pallas_call x1, Pallas kernels, local_blocks(): pl.pallas_call(finish_kernel, out_shape=shaped(row_count, col_count, chan...  0.98 us

profile of v14, /device:TPU:0, one launch (start us, length us, event | category | flops | bytes accessed | tf_op | source)
XLA Modules:
  0.0 30.6 jit_solution(3080099137039119140)
XLA Ops:
  0.0 1.5 %project.1 = (bf16[32,32,128]{2,1,0:T(8,128)(2,1)S(1)}, bf16[512,128]{1,0:T(8,128)(2,1)S(1)}, bf16[128,128]{1,0:T(8,128)(2,1)S(1)}, f32[1,128]{1,0:T(1,128)S(1)}...) custom-call(bf16[4,128,128]{2,1,0:T(8,128)(2,1)} %pair_hbm.1, s32[1,128]{1,0:T(1,128)} %bitcast.5, f32[1,128]{1,0:T(1,128)} %bitcast.6, ...), custom_call_target="tpu_custom_call" | custom-call | tf_op jit(solution)/shard_map/project/pallas_call | solution.py:162
  1.6 17.0 %all_to_all.10.blocks_ref = bf16[32,32,128]{2,1,0:T(8,128)(2,1)S(1)} all-to-all(bf16[32,32,128]{2,1,0:T(8,128)(2,1)S(1)} %get-tuple-element.14), channel_id=1, replica_groups={{31,30,29,28,27,26,25,24,23,22,21,20,19,18,17,16,15,14,13,12,11,10,9,8,..., dimensions={0} | all-to-all | bytes 524288 | tf_op jit(solution)/shard_map/all_to_all | solution.py:98
  18.6 0.3 contract.1
  18.9 10.8 %all_to_all.11.blocks_ref = bf16[32,16,128]{2,1,0:T(8,128)(2,1)S(1)} all-to-all(bf16[32,16,128]{2,1,0:T(8,128)(2,1)S(1)} %get-tuple-element.19), channel_id=1, replica_groups={{31,30,29,28,27,26,25,24,23,22,21,20,19,18,17,16,15,14,13,12,11,10,9,8,..., dimensions={0} | all-to-all | bytes 262144 | tf_op jit(solution)/shard_map/all_to_all | solution.py:98
  29.7 1.0 %finish.1 = bf16[4,128,128]{2,1,0:T(8,128)(2,1)} custom-call(bf16[32,16,128]{2,1,0:T(8,128)(2,1)S(1)} %all_to_all.11.blocks_ref, bf16[512,128]{1,0:T(8,128)(2,1)S(1)} %get-tuple-element.20.gate_ref, f32[2,128,128]{2,1,0:T(8,128)S(1)} %get-tuple-element.21.scales_ref, bf16[128,128]{1,0:T(8,128)(2,1)S(1)} %get-tuple-element.22.w_ref), custom_call_target="tpu_custom_call" | custom-call | tf_op jit(solution)/shard_map/finish/pallas_call | solution.py:199

commit v15 on v14

--- a/solution.py
+++ b/solution.py
@@ -10,7 +10,7 @@
 epsilon = 1e-05
 axes = ("wide", "narrow")
 kernel_vmem = 8 * 2**20
-hub = 31
+hub = 24
 
 
 def layer_norm(values, gain_vec, bias_vec, axis_dim):
@@ -258,7 +258,7 @@
         and (row_count, col_count, chan_count) == (4, 128, 128)
         and shards * row_count == col_count
         and shards * 4 == chan_count
-        and shards == hub + 1
+        and shards == 32
     )
     return (local_blocks if fits else local_arrays)(pair, *rest)
 

time: 30.9 us -> 31.4 us (1.016)
  blocking collectives: 27.8 us -> 28.4 us
    all_to_all x2, blocking collectives: 27.8 us -> 28.4 us  [exchange(): lax.all_to_all(blocks, axes, split_axis=0, concat_axis=0, axis_index_grou...]
where the time goes in v15:
time: 31.4 us; the launch traced here: 31.2 us
  blocking collectives  28.4 us (90%)
  Pallas kernels  2.8 us (9%)
    all_to_all x2, blocking collectives, exchange(): lax.all_to_all(blocks, axes, split_axis=0, concat_axis=0, axis_index_grou...  28.4 us
    pallas_call x1, Pallas kernels, local_blocks(): pl.pallas_call(project_kernel, out_shape=(shaped(shards, 8 * row_count, c...  1.55 us
    pallas_call x1, Pallas kernels, local_blocks(): pl.pallas_call(finish_kernel, out_shape=shaped(row_count, col_count, chan...  0.98 us

profile of v15, /device:TPU:0, one launch (start us, length us, event | category | flops | bytes accessed | tf_op | source)
XLA Modules:
  0.0 31.2 jit_solution(6543326386404344845)
XLA Ops:
  0.0 1.5 %project.1 = (bf16[32,32,128]{2,1,0:T(8,128)(2,1)S(1)}, bf16[512,128]{1,0:T(8,128)(2,1)S(1)}, bf16[128,128]{1,0:T(8,128)(2,1)S(1)}, f32[1,128]{1,0:T(1,128)S(1)}...) custom-call(bf16[4,128,128]{2,1,0:T(8,128)(2,1)} %pair_hbm.1, s32[1,128]{1,0:T(1,128)} %bitcast.5, f32[1,128]{1,0:T(1,128)} %bitcast.6, ...), custom_call_target="tpu_custom_call" | custom-call | tf_op jit(solution)/shard_map/project/pallas_call | solution.py:162
  1.6 17.8 %all_to_all.10.blocks_ref = bf16[32,32,128]{2,1,0:T(8,128)(2,1)S(1)} all-to-all(bf16[32,32,128]{2,1,0:T(8,128)(2,1)S(1)} %get-tuple-element.14), channel_id=1, replica_groups={{24,25,26,27,28,29,30,31,16,17,18,19,20,21,22,23,8,9,10,11,12,13,14,15,..., dimensions={0} | all-to-all | bytes 524288 | tf_op jit(solution)/shard_map/all_to_all | solution.py:98
  19.3 0.3 contract.1
  19.6 10.6 %all_to_all.11.blocks_ref = bf16[32,16,128]{2,1,0:T(8,128)(2,1)S(1)} all-to-all(bf16[32,16,128]{2,1,0:T(8,128)(2,1)S(1)} %get-tuple-element.19), channel_id=1, replica_groups={{24,25,26,27,28,29,30,31,16,17,18,19,20,21,22,23,8,9,10,11,12,13,14,15,..., dimensions={0} | all-to-all | bytes 262144 | tf_op jit(solution)/shard_map/all_to_all | solution.py:98
  30.2 1.0 %finish.1 = bf16[4,128,128]{2,1,0:T(8,128)(2,1)} custom-call(bf16[32,16,128]{2,1,0:T(8,128)(2,1)S(1)} %all_to_all.11.blocks_ref, bf16[512,128]{1,0:T(8,128)(2,1)S(1)} %get-tuple-element.20.gate_ref, f32[2,128,128]{2,1,0:T(8,128)S(1)} %get-tuple-element.21.scales_ref, bf16[128,128]{1,0:T(8,128)(2,1)S(1)} %get-tuple-element.22.w_ref), custom_call_target="tpu_custom_call" | custom-call | tf_op jit(solution)/shard_map/finish/pallas_call | solution.py:199

commit v16 on v15

--- a/solution.py
+++ b/solution.py
@@ -10,7 +10,7 @@
 epsilon = 1e-05
 axes = ("wide", "narrow")
 kernel_vmem = 8 * 2**20
-hub = 24
+hub = 7
 
 
 def layer_norm(values, gain_vec, bias_vec, axis_dim):

time: 31.4 us -> 30.8 us (0.981); the launches traced: 31.2 us -> 30.2 us
  blocking collectives: 28.4 us -> 27.4 us
    all_to_all x2, blocking collectives: 28.4 us -> 27.4 us  [exchange(): lax.all_to_all(blocks, axes, split_axis=0, concat_axis=0, axis_index_grou...]
where the time goes in v16:
time: 30.8 us; the launch traced here: 30.2 us
  blocking collectives  27.4 us (89%)
  Pallas kernels  2.79 us (9%)
    all_to_all x2, blocking collectives, exchange(): lax.all_to_all(blocks, axes, split_axis=0, concat_axis=0, axis_index_grou...  27.4 us
    pallas_call x1, Pallas kernels, local_blocks(): pl.pallas_call(project_kernel, out_shape=(shaped(shards, 8 * row_count, c...  1.55 us
    pallas_call x1, Pallas kernels, local_blocks(): pl.pallas_call(finish_kernel, out_shape=shaped(row_count, col_count, chan...  0.97 us

profile of v16, /device:TPU:0, one launch (start us, length us, event | category | flops | bytes accessed | tf_op | source)
XLA Modules:
  0.0 30.2 jit_solution(5669050579245949183)
XLA Ops:
  0.0 1.5 %project.1 = (bf16[32,32,128]{2,1,0:T(8,128)(2,1)S(1)}, bf16[512,128]{1,0:T(8,128)(2,1)S(1)}, bf16[128,128]{1,0:T(8,128)(2,1)S(1)}, f32[1,128]{1,0:T(1,128)S(1)}...) custom-call(bf16[4,128,128]{2,1,0:T(8,128)(2,1)} %pair_hbm.1, s32[1,128]{1,0:T(1,128)} %bitcast.5, f32[1,128]{1,0:T(1,128)} %bitcast.6, ...), custom_call_target="tpu_custom_call" | custom-call | tf_op jit(solution)/shard_map/project/pallas_call | solution.py:162
  1.6 17.0 %all_to_all.10.blocks_ref = bf16[32,32,128]{2,1,0:T(8,128)(2,1)S(1)} all-to-all(bf16[32,32,128]{2,1,0:T(8,128)(2,1)S(1)} %get-tuple-element.14), channel_id=1, replica_groups={{7,6,5,4,3,2,1,0,15,14,13,12,11,10,9,8,23,22,21,20,19,18,17,16,31,30,29..., dimensions={0} | all-to-all | bytes 524288 | tf_op jit(solution)/shard_map/all_to_all | solution.py:98
  18.6 0.3 contract.1
  18.9 10.4 %all_to_all.11.blocks_ref = bf16[32,16,128]{2,1,0:T(8,128)(2,1)S(1)} all-to-all(bf16[32,16,128]{2,1,0:T(8,128)(2,1)S(1)} %get-tuple-element.19), channel_id=1, replica_groups={{7,6,5,4,3,2,1,0,15,14,13,12,11,10,9,8,23,22,21,20,19,18,17,16,31,30,29..., dimensions={0} | all-to-all | bytes 262144 | tf_op jit(solution)/shard_map/all_to_all | solution.py:98
  29.2 1.0 %finish.1 = bf16[4,128,128]{2,1,0:T(8,128)(2,1)} custom-call(bf16[32,16,128]{2,1,0:T(8,128)(2,1)S(1)} %all_to_all.11.blocks_ref, bf16[512,128]{1,0:T(8,128)(2,1)S(1)} %get-tuple-element.20.gate_ref, f32[2,128,128]{2,1,0:T(8,128)S(1)} %get-tuple-element.21.scales_ref, bf16[128,128]{1,0:T(8,128)(2,1)S(1)} %get-tuple-element.22.w_ref), custom_call_target="tpu_custom_call" | custom-call | tf_op jit(solution)/shard_map/finish/pallas_call | solution.py:199

commit v17 on v14

--- a/solution.py
+++ b/solution.py
@@ -38,6 +38,7 @@
     pair_ref, valid_ref, gain_ref, bias_ref, w_ref, sems,
 ):
     row_count, col_count, chan_count = pair_ref.shape
+    shards = out_ref.shape[0]
     quarter = chan_count // 4
     pairs = [(pair_hbm.at[r], pair_ref.at[r]) for r in range(row_count)]
     for i in range(0, chan_count, quarter):
@@ -55,15 +56,25 @@
     for fetch in fetches:
         fetch.start()
     row_start = lax.axis_index(axes) * row_count
+    place = lax.broadcasted_iota(jnp.int32, (2 * chan_count, 2 * chan_count), 0)
+    column = lax.broadcasted_iota(jnp.int32, (2 * chan_count, 2 * chan_count), 1)
+    wanted = (place >> 3) * 4 + (place & 3) + ((place >> 2) & 1) * chan_count
+    spread = jnp.where(column == wanted, 1.0, 0.0).astype(jnp.bfloat16)
     for fetch in fetches[:needed]:
         fetch.wait()
     tokens = pair_ref[...].reshape(row_count * col_count, chan_count).astype(jnp.float32)
     normed = layer_norm(tokens, gain_ref[...], bias_ref[...], 1).astype(jnp.bfloat16)
     normed_ref[...] = normed
-    projected = lax.dot_general(
-        w_ref[...], normed, (((0,), (1,)), ((), ())),
-        preferred_element_type=jnp.float32,
-    )
+    def project(first):
+        columns = [w_ref[:, i * chan_count : (i + 1) * chan_count] for i in (first, first + 2)]
+        turned = lax.dot_general(
+            spread, jnp.concatenate(columns, axis=1), (((1,), (1,)), ((), ())),
+            preferred_element_type=jnp.float32,
+        ).astype(jnp.bfloat16)
+        return lax.dot_general(
+            turned, normed, (((1,), (1,)), ((), ())), preferred_element_type=jnp.float32
+        )
+
     col_flags = valid_ref[...].astype(jnp.float32)
     places = lax.broadcasted_iota(jnp.int32, col_flags.shape, 1)
     row_flags = [
@@ -71,18 +82,14 @@
         for r in range(row_count)
     ]
     flags = jnp.concatenate([col_flags * row_flag for row_flag in row_flags], axis=1)
-    for chan in range(0, chan_count, 8):
-        a_gate, a, b_gate, b = (
-            projected[i * chan_count + chan : i * chan_count + chan + 8] for i in range(4)
-        )
-        left = sigmoid(a_gate) * a * flags
-        right = sigmoid(b_gate) * b * flags
-        for half, block in enumerate(swap_halves(left, right)):
-            for r in range(0, row_count, 2):
-                rows = jnp.concatenate(
-                    [block[:, (r + i) * col_count : (r + i + 1) * col_count] for i in range(2)], axis=0
-                )
-                out_ref[(chan // 4 + half) ^ hub, r * 8 : (r + 2) * 8, :] = rows.astype(jnp.bfloat16)
+    sides = sigmoid(project(0)) * project(1) * flags
+    for device in range(shards):
+        block = sides[device * 8 : (device + 1) * 8]
+        for r in range(0, row_count, 2):
+            rows = jnp.concatenate(
+                [block[:, (r + i) * col_count : (r + i + 1) * col_count] for i in range(2)], axis=0
+            )
+            out_ref[device ^ hub, r * 8 : (r + 2) * 8, :] = rows.astype(jnp.bfloat16)
     for fetch in fetches[needed:]:
         fetch.wait()
 

time: 30.9 us -> 30.9 us (level)
  no operation moved by 1% of the time
where the time goes in v17:
time: 30.9 us; the launch traced here: 30.7 us
  blocking collectives  27.8 us (90%)
  Pallas kernels  2.85 us (9%)
    all_to_all x2, blocking collectives, exchange(): lax.all_to_all(blocks, axes, split_axis=0, concat_axis=0, axis_index_grou...  27.8 us
    pallas_call x1, Pallas kernels, local_blocks(): pl.pallas_call(project_kernel, out_shape=(shaped(shards, 8 * row_count, c...  1.6 us
    pallas_call x1, Pallas kernels, local_blocks(): pl.pallas_call(finish_kernel, out_shape=shaped(row_count, col_count, chan...  0.98 us

profile of v17, /device:TPU:0, one launch (start us, length us, event | category | flops | bytes accessed | tf_op | source)
XLA Modules:
  0.0 30.7 jit_solution(9880592429624719471)
XLA Ops:
  0.0 1.6 %project.1 = (bf16[32,32,128]{2,1,0:T(8,128)(2,1)S(1)}, bf16[512,128]{1,0:T(8,128)(2,1)S(1)}, bf16[128,128]{1,0:T(8,128)(2,1)S(1)}, f32[1,128]{1,0:T(1,128)S(1)}...) custom-call(bf16[4,128,128]{2,1,0:T(8,128)(2,1)} %pair_hbm.1, s32[1,128]{1,0:T(1,128)} %bitcast.5, f32[1,128]{1,0:T(1,128)} %bitcast.6, ...), custom_call_target="tpu_custom_call" | custom-call | tf_op jit(solution)/shard_map/project/pallas_call | solution.py:169
  1.6 17.0 %all_to_all.10.blocks_ref = bf16[32,32,128]{2,1,0:T(8,128)(2,1)S(1)} all-to-all(bf16[32,32,128]{2,1,0:T(8,128)(2,1)S(1)} %get-tuple-element.14), channel_id=1, replica_groups={{31,30,29,28,27,26,25,24,23,22,21,20,19,18,17,16,15,14,13,12,11,10,9,8,..., dimensions={0} | all-to-all | bytes 524288 | tf_op jit(solution)/shard_map/all_to_all | solution.py:105
  18.6 0.3 contract.1
  18.9 10.8 %all_to_all.11.blocks_ref = bf16[32,16,128]{2,1,0:T(8,128)(2,1)S(1)} all-to-all(bf16[32,16,128]{2,1,0:T(8,128)(2,1)S(1)} %get-tuple-element.19), channel_id=1, replica_groups={{31,30,29,28,27,26,25,24,23,22,21,20,19,18,17,16,15,14,13,12,11,10,9,8,..., dimensions={0} | all-to-all | bytes 262144 | tf_op jit(solution)/shard_map/all_to_all | solution.py:105
  29.7 1.0 %finish.1 = bf16[4,128,128]{2,1,0:T(8,128)(2,1)} custom-call(bf16[32,16,128]{2,1,0:T(8,128)(2,1)S(1)} %all_to_all.11.blocks_ref, bf16[512,128]{1,0:T(8,128)(2,1)S(1)} %get-tuple-element.20.gate_ref, f32[2,128,128]{2,1,0:T(8,128)S(1)} %get-tuple-element.21.scales_ref, bf16[128,128]{1,0:T(8,128)(2,1)S(1)} %get-tuple-element.22.w_ref), custom_call_target="tpu_custom_call" | custom-call | tf_op jit(solution)/shard_map/finish/pallas_call | solution.py:206

commit v18 on v16

--- a/solution.py
+++ b/solution.py
@@ -10,7 +10,7 @@
 epsilon = 1e-05
 axes = ("wide", "narrow")
 kernel_vmem = 8 * 2**20
-hub = 7
+hub = 6
 
 
 def layer_norm(values, gain_vec, bias_vec, axis_dim):

time: 30.8 us -> 30.8 us (level); the launches traced: 30.2 us -> 30.6 us
  blocking collectives: 27.4 us -> 27.8 us
    all_to_all x2, blocking collectives: 27.4 us -> 27.8 us  [exchange(): lax.all_to_all(blocks, axes, split_axis=0, concat_axis=0, axis_index_grou...]
where the time goes in v18:
time: 30.8 us; the launch traced here: 30.6 us
  blocking collectives  27.8 us (90%)
  Pallas kernels  2.79 us (9%)
    all_to_all x2, blocking collectives, exchange(): lax.all_to_all(blocks, axes, split_axis=0, concat_axis=0, axis_index_grou...  27.8 us
    pallas_call x1, Pallas kernels, local_blocks(): pl.pallas_call(project_kernel, out_shape=(shaped(shards, 8 * row_count, c...  1.55 us
    pallas_call x1, Pallas kernels, local_blocks(): pl.pallas_call(finish_kernel, out_shape=shaped(row_count, col_count, chan...  0.97 us

profile of v18, /device:TPU:0, one launch (start us, length us, event | category | flops | bytes accessed | tf_op | source)
XLA Modules:
  0.0 30.6 jit_solution(14792551211606713243)
XLA Ops:
  0.0 1.5 %project.1 = (bf16[32,32,128]{2,1,0:T(8,128)(2,1)S(1)}, bf16[512,128]{1,0:T(8,128)(2,1)S(1)}, bf16[128,128]{1,0:T(8,128)(2,1)S(1)}, f32[1,128]{1,0:T(1,128)S(1)}...) custom-call(bf16[4,128,128]{2,1,0:T(8,128)(2,1)} %pair_hbm.1, s32[1,128]{1,0:T(1,128)} %bitcast.5, f32[1,128]{1,0:T(1,128)} %bitcast.6, ...), custom_call_target="tpu_custom_call" | custom-call | tf_op jit(solution)/shard_map/project/pallas_call | solution.py:162
  1.6 17.0 %all_to_all.10.blocks_ref = bf16[32,32,128]{2,1,0:T(8,128)(2,1)S(1)} all-to-all(bf16[32,32,128]{2,1,0:T(8,128)(2,1)S(1)} %get-tuple-element.14), channel_id=1, replica_groups={{6,7,4,5,2,3,0,1,14,15,12,13,10,11,8,9,22,23,20,21,18,19,16,17,30,31,28..., dimensions={0} | all-to-all | bytes 524288 | tf_op jit(solution)/shard_map/all_to_all | solution.py:98
  18.6 0.3 contract.1
  18.9 10.7 %all_to_all.11.blocks_ref = bf16[32,16,128]{2,1,0:T(8,128)(2,1)S(1)} all-to-all(bf16[32,16,128]{2,1,0:T(8,128)(2,1)S(1)} %get-tuple-element.19), channel_id=1, replica_groups={{6,7,4,5,2,3,0,1,14,15,12,13,10,11,8,9,22,23,20,21,18,19,16,17,30,31,28..., dimensions={0} | all-to-all | bytes 262144 | tf_op jit(solution)/shard_map/all_to_all | solution.py:98
  29.6 1.0 %finish.1 = bf16[4,128,128]{2,1,0:T(8,128)(2,1)} custom-call(bf16[32,16,128]{2,1,0:T(8,128)(2,1)S(1)} %all_to_all.11.blocks_ref, bf16[512,128]{1,0:T(8,128)(2,1)S(1)} %get-tuple-element.20.gate_ref, f32[2,128,128]{2,1,0:T(8,128)S(1)} %get-tuple-element.21.scales_ref, bf16[128,128]{1,0:T(8,128)(2,1)S(1)} %get-tuple-element.22.w_ref), custom_call_target="tpu_custom_call" | custom-call | tf_op jit(solution)/shard_map/finish/pallas_call | solution.py:199

commit v19 on v14

--- a/solution.py
+++ b/solution.py
@@ -30,6 +30,11 @@
         jnp.where(first, low, pltpu.roll(high, 4, 0)),
         jnp.where(first, pltpu.roll(low, 4, 0), high),
     )
+
+
+def row_means(values):
+    ones = jnp.ones((values.shape[1], values.shape[1]), jnp.bfloat16)
+    return jnp.dot(values, ones, preferred_element_type=jnp.float32) * (1 / values.shape[1])
 
 
 def project_kernel(
@@ -57,8 +62,13 @@
     row_start = lax.axis_index(axes) * row_count
     for fetch in fetches[:needed]:
         fetch.wait()
-    tokens = pair_ref[...].reshape(row_count * col_count, chan_count).astype(jnp.float32)
-    normed = layer_norm(tokens, gain_ref[...], bias_ref[...], 1).astype(jnp.bfloat16)
+    tokens = pair_ref[...].reshape(row_count * col_count, chan_count)
+    centered = tokens.astype(jnp.float32) - row_means(tokens)
+    squares = centered * centered
+    high = squares.astype(jnp.bfloat16)
+    low = (squares - high.astype(jnp.float32)).astype(jnp.bfloat16)
+    scale = lax.rsqrt(row_means(high) + row_means(low) + epsilon)
+    normed = (centered * scale * gain_ref[...] + bias_ref[...]).astype(jnp.bfloat16)
     normed_ref[...] = normed
     projected = lax.dot_general(
         w_ref[...], normed, (((0,), (1,)), ((), ())),

time: 30.9 us -> 31 us (level)
  no operation moved by 1% of the time
where the time goes in v19:
time: 31 us; the launch traced here: 30.8 us
  blocking collectives  27.8 us (90%)
  Pallas kernels  2.91 us (9%)
    all_to_all x2, blocking collectives, exchange(): lax.all_to_all(blocks, axes, split_axis=0, concat_axis=0, axis_index_grou...  27.8 us
    pallas_call x1, Pallas kernels, local_blocks(): pl.pallas_call(project_kernel, out_shape=(shaped(shards, 8 * row_count, c...  1.66 us
    pallas_call x1, Pallas kernels, local_blocks(): pl.pallas_call(finish_kernel, out_shape=shaped(row_count, col_count, chan...  0.98 us

profile of v19, /device:TPU:0, one launch (start us, length us, event | category | flops | bytes accessed | tf_op | source)
XLA Modules:
  0.0 30.8 jit_solution(4305296134187399603)
XLA Ops:
  0.0 1.7 %project.1 = (bf16[32,32,128]{2,1,0:T(8,128)(2,1)S(1)}, bf16[512,128]{1,0:T(8,128)(2,1)S(1)}, bf16[128,128]{1,0:T(8,128)(2,1)S(1)}, f32[1,128]{1,0:T(1,128)S(1)}...) custom-call(bf16[4,128,128]{2,1,0:T(8,128)(2,1)} %pair_hbm.1, s32[1,128]{1,0:T(1,128)} %bitcast.5, f32[1,128]{1,0:T(1,128)} %bitcast.6, ...), custom_call_target="tpu_custom_call" | custom-call | tf_op jit(solution)/shard_map/project/pallas_call | solution.py:172
  1.7 17.0 %all_to_all.10.blocks_ref = bf16[32,32,128]{2,1,0:T(8,128)(2,1)S(1)} all-to-all(bf16[32,32,128]{2,1,0:T(8,128)(2,1)S(1)} %get-tuple-element.14), channel_id=1, replica_groups={{31,30,29,28,27,26,25,24,23,22,21,20,19,18,17,16,15,14,13,12,11,10,9,8,..., dimensions={0} | all-to-all | bytes 524288 | tf_op jit(solution)/shard_map/all_to_all | solution.py:108
  18.7 0.3 contract.1
  19.0 10.8 %all_to_all.11.blocks_ref = bf16[32,16,128]{2,1,0:T(8,128)(2,1)S(1)} all-to-all(bf16[32,16,128]{2,1,0:T(8,128)(2,1)S(1)} %get-tuple-element.19), channel_id=1, replica_groups={{31,30,29,28,27,26,25,24,23,22,21,20,19,18,17,16,15,14,13,12,11,10,9,8,..., dimensions={0} | all-to-all | bytes 262144 | tf_op jit(solution)/shard_map/all_to_all | solution.py:108
  29.8 1.0 %finish.1 = bf16[4,128,128]{2,1,0:T(8,128)(2,1)} custom-call(bf16[32,16,128]{2,1,0:T(8,128)(2,1)S(1)} %all_to_all.11.blocks_ref, bf16[512,128]{1,0:T(8,128)(2,1)S(1)} %get-tuple-element.20.gate_ref, f32[2,128,128]{2,1,0:T(8,128)S(1)} %get-tuple-element.21.scales_ref, bf16[128,128]{1,0:T(8,128)(2,1)S(1)} %get-tuple-element.22.w_ref), custom_call_target="tpu_custom_call" | custom-call | tf_op jit(solution)/shard_map/finish/pallas_call | solution.py:209

commit v20 on v18

--- a/solution.py
+++ b/solution.py
@@ -10,7 +10,7 @@
 epsilon = 1e-05
 axes = ("wide", "narrow")
 kernel_vmem = 8 * 2**20
-hub = 6
+planes = 4
 
 
 def layer_norm(values, gain_vec, bias_vec, axis_dim):
@@ -82,21 +82,31 @@
                 rows = jnp.concatenate(
                     [block[:, (r + i) * col_count : (r + i + 1) * col_count] for i in range(2)], axis=0
                 )
-                out_ref[(chan // 4 + half) ^ hub, r * 8 : (r + 2) * 8, :] = rows.astype(jnp.bfloat16)
+                out_ref[spot(chan // 4 + half), r * 8 : (r + 2) * 8, :] = rows.astype(jnp.bfloat16)
     for fetch in fetches[needed:]:
         fetch.wait()
 
 
+def group_order():
+    chips = []
+    for turn, place in enumerate((0, 1, 3, 2)):
+        chips += [plane * 4 + place for plane in range(planes)][:: 1 - 2 * (turn % 2)]
+    return [2 * chip + core for chip in chips for core in range(2)]
+
+
+def spot(device):
+    return group_order().index(device)
+
+
 def receive_blocks(blocks_ref, held_ref):
-    shards, rows, _ = blocks_ref.shape
-    for i in range(shards):
-        held_ref[(i ^ hub) * rows : ((i ^ hub) + 1) * rows, :] = blocks_ref[i].astype(jnp.float32)
+    rows = blocks_ref.shape[1]
+    for i, device in enumerate(group_order()):
+        held_ref[device * rows : (device + 1) * rows, :] = blocks_ref[i].astype(jnp.float32)
 
 
 def exchange(blocks):
-    groups = [[i ^ hub for i in range(blocks.shape[0])]]
     return lax.all_to_all(
-        blocks, axes, split_axis=0, concat_axis=0, axis_index_groups=groups, tiled=True
+        blocks, axes, split_axis=0, concat_axis=0, axis_index_groups=[group_order()], tiled=True
     )
 
 
@@ -120,7 +130,7 @@
         low, high = swap_halves(pieces[0], pieces[1]), swap_halves(pieces[2], pieces[3])
         for half in range(2):
             rows = jnp.concatenate([low[half], high[half]], axis=0)
-            out_ref[(row // 4 + half) ^ hub] = rows.astype(jnp.bfloat16)
+            out_ref[spot(row // 4 + half)] = rows.astype(jnp.bfloat16)
     gate = jnp.dot(normed_ref[...], w_gate_ref[...], preferred_element_type=jnp.float32)
     gate_ref[...] = sigmoid(gate).astype(jnp.bfloat16)
     for i, vector_ref in enumerate((gain_ref, bias_ref)):
@@ -258,7 +268,7 @@
         and (row_count, col_count, chan_count) == (4, 128, 128)
         and shards * row_count == col_count
         and shards * 4 == chan_count
-        and shards == 32
+        and shards == 8 * planes
     )
     return (local_blocks if fits else local_arrays)(pair, *rest)
 

time: 30.8 us -> 31.2 us (1.013)
  blocking collectives: 27.8 us -> 28.2 us
    all_to_all x2, blocking collectives: 27.8 us -> 28.2 us  [exchange(): lax.all_to_all(blocks, axes, split_axis=0, concat_axis=0, axis_index_grou...]
where the time goes in v20:
time: 31.2 us; the launch traced here: 31 us
  blocking collectives  28.2 us (90%)
  Pallas kernels  2.8 us (9%)
    all_to_all x2, blocking collectives, exchange(): lax.all_to_all(blocks, axes, split_axis=0, concat_axis=0, axis_index_grou...  28.2 us
    pallas_call x1, Pallas kernels, local_blocks(): pl.pallas_call(project_kernel, out_shape=(shaped(shards, 8 * row_count, c...  1.55 us
    pallas_call x1, Pallas kernels, local_blocks(): pl.pallas_call(finish_kernel, out_shape=shaped(row_count, col_count, chan...  0.98 us

profile of v20, /device:TPU:0, one launch (start us, length us, event | category | flops | bytes accessed | tf_op | source)
XLA Modules:
  0.0 31.0 jit_solution(13048422404703264179)
XLA Ops:
  0.0 1.5 %project.1 = (bf16[32,32,128]{2,1,0:T(8,128)(2,1)S(1)}, bf16[512,128]{1,0:T(8,128)(2,1)S(1)}, bf16[128,128]{1,0:T(8,128)(2,1)S(1)}, f32[1,128]{1,0:T(1,128)S(1)}...) custom-call(bf16[4,128,128]{2,1,0:T(8,128)(2,1)} %pair_hbm.1, s32[1,128]{1,0:T(1,128)} %bitcast.5, f32[1,128]{1,0:T(1,128)} %bitcast.6, ...), custom_call_target="tpu_custom_call" | custom-call | tf_op jit(solution)/shard_map/project/pallas_call | solution.py:172
  1.6 17.1 %all_to_all.10.blocks_ref = bf16[32,32,128]{2,1,0:T(8,128)(2,1)S(1)} all-to-all(bf16[32,32,128]{2,1,0:T(8,128)(2,1)S(1)} %get-tuple-element.14), channel_id=1, replica_groups={{0,1,8,9,16,17,24,25,26,27,18,19,10,11,2,3,6,7,14,15,22,23,30,31,28,29,..., dimensions={0} | all-to-all | bytes 524288 | tf_op jit(solution)/shard_map/all_to_all | solution.py:108
  18.7 0.3 contract.1
  19.0 11.1 %all_to_all.11.blocks_ref = bf16[32,16,128]{2,1,0:T(8,128)(2,1)S(1)} all-to-all(bf16[32,16,128]{2,1,0:T(8,128)(2,1)S(1)} %get-tuple-element.19), channel_id=1, replica_groups={{0,1,8,9,16,17,24,25,26,27,18,19,10,11,2,3,6,7,14,15,22,23,30,31,28,29,..., dimensions={0} | all-to-all | bytes 262144 | tf_op jit(solution)/shard_map/all_to_all | solution.py:108
  30.0 1.0 %finish.1 = bf16[4,128,128]{2,1,0:T(8,128)(2,1)} custom-call(bf16[32,16,128]{2,1,0:T(8,128)(2,1)S(1)} %all_to_all.11.blocks_ref, bf16[512,128]{1,0:T(8,128)(2,1)S(1)} %get-tuple-element.20.gate_ref, f32[2,128,128]{2,1,0:T(8,128)S(1)} %get-tuple-element.21.scales_ref, bf16[128,128]{1,0:T(8,128)(2,1)S(1)} %get-tuple-element.22.w_ref), custom_call_target="tpu_custom_call" | custom-call | tf_op jit(solution)/shard_map/finish/pallas_call | solution.py:209

commit v21 on v20

--- a/solution.py
+++ b/solution.py
@@ -91,7 +91,7 @@
     chips = []
     for turn, place in enumerate((0, 1, 3, 2)):
         chips += [plane * 4 + place for plane in range(planes)][:: 1 - 2 * (turn % 2)]
-    return [2 * chip + core for chip in chips for core in range(2)]
+    return [2 * chip + core for chip in chips for core in range(2)][::-1]
 
 
 def spot(device):

time: 31.2 us -> 30.9 us (level); the launches traced: 31 us -> 30.4 us
  blocking collectives: 28.2 us -> 27.6 us
    all_to_all x2, blocking collectives: 28.2 us -> 27.6 us  [exchange(): lax.all_to_all(blocks, axes, split_axis=0, concat_axis=0, axis_index_grou...]
where the time goes in v21:
time: 30.9 us; the launch traced here: 30.4 us
  blocking collectives  27.6 us (89%)
  Pallas kernels  2.8 us (9%)
    all_to_all x2, blocking collectives, exchange(): lax.all_to_all(blocks, axes, split_axis=0, concat_axis=0, axis_index_grou...  27.6 us
    pallas_call x1, Pallas kernels, local_blocks(): pl.pallas_call(project_kernel, out_shape=(shaped(shards, 8 * row_count, c...  1.55 us
    pallas_call x1, Pallas kernels, local_blocks(): pl.pallas_call(finish_kernel, out_shape=shaped(row_count, col_count, chan...  0.98 us

profile of v21, /device:TPU:0, one launch (start us, length us, event | category | flops | bytes accessed | tf_op | source)
XLA Modules:
  0.0 30.4 jit_solution(13375729459478205495)
XLA Ops:
  0.0 1.5 %project.1 = (bf16[32,32,128]{2,1,0:T(8,128)(2,1)S(1)}, bf16[512,128]{1,0:T(8,128)(2,1)S(1)}, bf16[128,128]{1,0:T(8,128)(2,1)S(1)}, f32[1,128]{1,0:T(1,128)S(1)}...) custom-call(bf16[4,128,128]{2,1,0:T(8,128)(2,1)} %pair_hbm.1, s32[1,128]{1,0:T(1,128)} %bitcast.5, f32[1,128]{1,0:T(1,128)} %bitcast.6, ...), custom_call_target="tpu_custom_call" | custom-call | tf_op jit(solution)/shard_map/project/pallas_call | solution.py:172
  1.6 17.3 %all_to_all.10.blocks_ref = bf16[32,32,128]{2,1,0:T(8,128)(2,1)S(1)} all-to-all(bf16[32,32,128]{2,1,0:T(8,128)(2,1)S(1)} %get-tuple-element.14), channel_id=1, replica_groups={{5,4,13,12,21,20,29,28,31,30,23,22,15,14,7,6,3,2,11,10,19,18,27,26,25,2..., dimensions={0} | all-to-all | bytes 524288 | tf_op jit(solution)/shard_map/all_to_all | solution.py:108
  18.9 0.3 contract.1
  19.1 10.2 %all_to_all.11.blocks_ref = bf16[32,16,128]{2,1,0:T(8,128)(2,1)S(1)} all-to-all(bf16[32,16,128]{2,1,0:T(8,128)(2,1)S(1)} %get-tuple-element.19), channel_id=1, replica_groups={{5,4,13,12,21,20,29,28,31,30,23,22,15,14,7,6,3,2,11,10,19,18,27,26,25,2..., dimensions={0} | all-to-all | bytes 262144 | tf_op jit(solution)/shard_map/all_to_all | solution.py:108
  29.4 1.0 %finish.1 = bf16[4,128,128]{2,1,0:T(8,128)(2,1)} custom-call(bf16[32,16,128]{2,1,0:T(8,128)(2,1)S(1)} %all_to_all.11.blocks_ref, bf16[512,128]{1,0:T(8,128)(2,1)S(1)} %get-tuple-element.20.gate_ref, f32[2,128,128]{2,1,0:T(8,128)S(1)} %get-tuple-element.21.scales_ref, bf16[128,128]{1,0:T(8,128)(2,1)S(1)} %get-tuple-element.22.w_ref), custom_call_target="tpu_custom_call" | custom-call | tf_op jit(solution)/shard_map/finish/pallas_call | solution.py:209

commit v22 on v20

--- a/solution.py
+++ b/solution.py
@@ -89,7 +89,7 @@
 
 def group_order():
     chips = []
-    for turn, place in enumerate((0, 1, 3, 2)):
+    for turn, place in enumerate((3, 2, 0, 1)):
         chips += [plane * 4 + place for plane in range(planes)][:: 1 - 2 * (turn % 2)]
     return [2 * chip + core for chip in chips for core in range(2)]
 

time: 31.2 us -> 31.2 us (level)
  no operation moved by 1% of the time
where the time goes in v22:
time: 31.2 us; the launch traced here: 31 us
  blocking collectives  28.2 us (90%)
  Pallas kernels  2.8 us (9%)
    all_to_all x2, blocking collectives, exchange(): lax.all_to_all(blocks, axes, split_axis=0, concat_axis=0, axis_index_grou...  28.2 us
    pallas_call x1, Pallas kernels, local_blocks(): pl.pallas_call(project_kernel, out_shape=(shaped(shards, 8 * row_count, c...  1.55 us
    pallas_call x1, Pallas kernels, local_blocks(): pl.pallas_call(finish_kernel, out_shape=shaped(row_count, col_count, chan...  0.98 us

profile of v22, /device:TPU:0, one launch (start us, length us, event | category | flops | bytes accessed | tf_op | source)
XLA Modules:
  0.0 31.0 jit_solution(7174067865593355617)
XLA Ops:
  0.0 1.5 %project.1 = (bf16[32,32,128]{2,1,0:T(8,128)(2,1)S(1)}, bf16[512,128]{1,0:T(8,128)(2,1)S(1)}, bf16[128,128]{1,0:T(8,128)(2,1)S(1)}, f32[1,128]{1,0:T(1,128)S(1)}...) custom-call(bf16[4,128,128]{2,1,0:T(8,128)(2,1)} %pair_hbm.1, s32[1,128]{1,0:T(1,128)} %bitcast.5, f32[1,128]{1,0:T(1,128)} %bitcast.6, ...), custom_call_target="tpu_custom_call" | custom-call | tf_op jit(solution)/shard_map/project/pallas_call | solution.py:172
  1.6 17.1 %all_to_all.10.blocks_ref = bf16[32,32,128]{2,1,0:T(8,128)(2,1)S(1)} all-to-all(bf16[32,32,128]{2,1,0:T(8,128)(2,1)S(1)} %get-tuple-element.14), channel_id=1, replica_groups={{6,7,14,15,22,23,30,31,28,29,20,21,12,13,4,5,0,1,8,9,16,17,24,25,26,27,..., dimensions={0} | all-to-all | bytes 524288 | tf_op jit(solution)/shard_map/all_to_all | solution.py:108
  18.7 0.3 contract.1
  19.0 11.1 %all_to_all.11.blocks_ref = bf16[32,16,128]{2,1,0:T(8,128)(2,1)S(1)} all-to-all(bf16[32,16,128]{2,1,0:T(8,128)(2,1)S(1)} %get-tuple-element.19), channel_id=1, replica_groups={{6,7,14,15,22,23,30,31,28,29,20,21,12,13,4,5,0,1,8,9,16,17,24,25,26,27,..., dimensions={0} | all-to-all | bytes 262144 | tf_op jit(solution)/shard_map/all_to_all | solution.py:108
  30.0 1.0 %finish.1 = bf16[4,128,128]{2,1,0:T(8,128)(2,1)} custom-call(bf16[32,16,128]{2,1,0:T(8,128)(2,1)S(1)} %all_to_all.11.blocks_ref, bf16[512,128]{1,0:T(8,128)(2,1)S(1)} %get-tuple-element.20.gate_ref, f32[2,128,128]{2,1,0:T(8,128)S(1)} %get-tuple-element.21.scales_ref, bf16[128,128]{1,0:T(8,128)(2,1)S(1)} %get-tuple-element.22.w_ref), custom_call_target="tpu_custom_call" | custom-call | tf_op jit(solution)/shard_map/finish/pallas_call | solution.py:209

commit v23 on v21

--- a/solution.py
+++ b/solution.py
@@ -91,7 +91,7 @@
     chips = []
     for turn, place in enumerate((0, 1, 3, 2)):
         chips += [plane * 4 + place for plane in range(planes)][:: 1 - 2 * (turn % 2)]
-    return [2 * chip + core for chip in chips for core in range(2)][::-1]
+    return [2 * chip + core for chip in chips for core in (1, 0)]
 
 
 def spot(device):

time: 30.9 us -> 31.2 us (level); the launches traced: 30.4 us -> 31 us
  blocking collectives: 27.6 us -> 28.2 us
    all_to_all x2, blocking collectives: 27.6 us -> 28.2 us  [exchange(): lax.all_to_all(blocks, axes, split_axis=0, concat_axis=0, axis_index_grou...]
where the time goes in v23:
time: 31.2 us; the launch traced here: 31 us
  blocking collectives  28.2 us (90%)
  Pallas kernels  2.8 us (9%)
    all_to_all x2, blocking collectives, exchange(): lax.all_to_all(blocks, axes, split_axis=0, concat_axis=0, axis_index_grou...  28.2 us
    pallas_call x1, Pallas kernels, local_blocks(): pl.pallas_call(project_kernel, out_shape=(shaped(shards, 8 * row_count, c...  1.55 us
    pallas_call x1, Pallas kernels, local_blocks(): pl.pallas_call(finish_kernel, out_shape=shaped(row_count, col_count, chan...  0.98 us

profile of v23, /device:TPU:0, one launch (start us, length us, event | category | flops | bytes accessed | tf_op | source)
XLA Modules:
  0.0 31.0 jit_solution(4974477088825407978)
XLA Ops:
  0.0 1.5 %project.1 = (bf16[32,32,128]{2,1,0:T(8,128)(2,1)S(1)}, bf16[512,128]{1,0:T(8,128)(2,1)S(1)}, bf16[128,128]{1,0:T(8,128)(2,1)S(1)}, f32[1,128]{1,0:T(1,128)S(1)}...) custom-call(bf16[4,128,128]{2,1,0:T(8,128)(2,1)} %pair_hbm.1, s32[1,128]{1,0:T(1,128)} %bitcast.5, f32[1,128]{1,0:T(1,128)} %bitcast.6, ...), custom_call_target="tpu_custom_call" | custom-call | tf_op jit(solution)/shard_map/project/pallas_call | solution.py:172
  1.6 17.1 %all_to_all.10.blocks_ref = bf16[32,32,128]{2,1,0:T(8,128)(2,1)S(1)} all-to-all(bf16[32,32,128]{2,1,0:T(8,128)(2,1)S(1)} %get-tuple-element.14), channel_id=1, replica_groups={{1,0,9,8,17,16,25,24,27,26,19,18,11,10,3,2,7,6,15,14,23,22,31,30,29,28,..., dimensions={0} | all-to-all | bytes 524288 | tf_op jit(solution)/shard_map/all_to_all | solution.py:108
  18.7 0.3 contract.1
  19.0 11.1 %all_to_all.11.blocks_ref = bf16[32,16,128]{2,1,0:T(8,128)(2,1)S(1)} all-to-all(bf16[32,16,128]{2,1,0:T(8,128)(2,1)S(1)} %get-tuple-element.19), channel_id=1, replica_groups={{1,0,9,8,17,16,25,24,27,26,19,18,11,10,3,2,7,6,15,14,23,22,31,30,29,28,..., dimensions={0} | all-to-all | bytes 262144 | tf_op jit(solution)/shard_map/all_to_all | solution.py:108
  30.0 1.0 %finish.1 = bf16[4,128,128]{2,1,0:T(8,128)(2,1)} custom-call(bf16[32,16,128]{2,1,0:T(8,128)(2,1)S(1)} %all_to_all.11.blocks_ref, bf16[512,128]{1,0:T(8,128)(2,1)S(1)} %get-tuple-element.20.gate_ref, f32[2,128,128]{2,1,0:T(8,128)S(1)} %get-tuple-element.21.scales_ref, bf16[128,128]{1,0:T(8,128)(2,1)S(1)} %get-tuple-element.22.w_ref), custom_call_target="tpu_custom_call" | custom-call | tf_op jit(solution)/shard_map/finish/pallas_call | solution.py:209

commit v24 on v21

--- a/solution.py
+++ b/solution.py
@@ -82,31 +82,31 @@
                 rows = jnp.concatenate(
                     [block[:, (r + i) * col_count : (r + i + 1) * col_count] for i in range(2)], axis=0
                 )
-                out_ref[spot(chan // 4 + half), r * 8 : (r + 2) * 8, :] = rows.astype(jnp.bfloat16)
+                out_ref[sides_order().index(chan // 4 + half), r * 8 : (r + 2) * 8, :] = rows.astype(jnp.bfloat16)
     for fetch in fetches[needed:]:
         fetch.wait()
 
 
-def group_order():
+def sides_order():
+    return list(range(8 * planes))[::-1]
+
+
+def triangle_order():
     chips = []
     for turn, place in enumerate((0, 1, 3, 2)):
         chips += [plane * 4 + place for plane in range(planes)][:: 1 - 2 * (turn % 2)]
     return [2 * chip + core for chip in chips for core in range(2)][::-1]
 
 
-def spot(device):
-    return group_order().index(device)
-
-
-def receive_blocks(blocks_ref, held_ref):
+def receive_blocks(blocks_ref, held_ref, order):
     rows = blocks_ref.shape[1]
-    for i, device in enumerate(group_order()):
+    for i, device in enumerate(order):
         held_ref[device * rows : (device + 1) * rows, :] = blocks_ref[i].astype(jnp.float32)
 
 
-def exchange(blocks):
+def exchange(blocks, order):
     return lax.all_to_all(
-        blocks, axes, split_axis=0, concat_axis=0, axis_index_groups=[group_order()], tiled=True
+        blocks, axes, split_axis=0, concat_axis=0, axis_index_groups=[order], tiled=True
     )
 
 
@@ -115,7 +115,7 @@
     out_ref, gate_ref, scales_ref, held_ref,
 ):
     total = held_ref.shape[0] // 8
-    receive_blocks(blocks_ref, held_ref)
+    receive_blocks(blocks_ref, held_ref, sides_order())
     products = []
     for c in range(4):
         left = held_ref[pl.ds(c, total, stride=8), :].astype(jnp.bfloat16)
@@ -130,7 +130,7 @@
         low, high = swap_halves(pieces[0], pieces[1]), swap_halves(pieces[2], pieces[3])
         for half in range(2):
             rows = jnp.concatenate([low[half], high[half]], axis=0)
-            out_ref[spot(row // 4 + half)] = rows.astype(jnp.bfloat16)
+            out_ref[triangle_order().index(row // 4 + half)] = rows.astype(jnp.bfloat16)
     gate = jnp.dot(normed_ref[...], w_gate_ref[...], preferred_element_type=jnp.float32)
     gate_ref[...] = sigmoid(gate).astype(jnp.bfloat16)
     for i, vector_ref in enumerate((gain_ref, bias_ref)):
@@ -139,7 +139,7 @@
 
 def finish_kernel(blocks_ref, gate_ref, scales_ref, w_ref, out_ref, held_ref):
     row_count, col_count, chan_count = out_ref.shape
-    receive_blocks(blocks_ref, held_ref)
+    receive_blocks(blocks_ref, held_ref, triangle_order())
     for r in range(row_count):
         triangle = held_ref[pl.ds(r, chan_count, stride=row_count), :]
         normed = layer_norm(triangle, scales_ref[0], scales_ref[1], 0).astype(jnp.bfloat16)
@@ -191,7 +191,7 @@
         pair, line(valid), line(norm_gain), line(norm_bias), w_proj,
         line(out_gain), line(out_bias), w_out,
     )))
-    sides = exchange(sides)
+    sides = exchange(sides, sides_order())
     triangle, gate_values, scales = pl.pallas_call(
         contract_kernel,
         out_shape=(
@@ -205,7 +205,7 @@
         compiler_params=limit,
         name="contract",
     )(sides, normed, w_gate, out_gain, out_bias)
-    triangle = exchange(triangle)
+    triangle = exchange(triangle, triangle_order())
     return pl.pallas_call(
         finish_kernel,
         out_shape=shaped(row_count, col_count, chan_count),

time: 30.9 us -> 30.9 us (level)
  no operation moved by 1% of the time
where the time goes in v24:
time: 30.9 us; the launch traced here: 30.5 us
  blocking collectives  27.7 us (90%)
  Pallas kernels  2.8 us (9%)
    all_to_all x2, blocking collectives, exchange(): lax.all_to_all(blocks, axes, split_axis=0, concat_axis=0, axis_index_grou...  27.7 us
    pallas_call x1, Pallas kernels, local_blocks(): pl.pallas_call(project_kernel, out_shape=(shaped(shards, 8 * row_count, c...  1.55 us
    pallas_call x1, Pallas kernels, local_blocks(): pl.pallas_call(finish_kernel, out_shape=shaped(row_count, col_count, chan...  0.98 us

profile of v24, /device:TPU:0, one launch (start us, length us, event | category | flops | bytes accessed | tf_op | source)
XLA Modules:
  0.0 30.5 jit_solution(18175365912402068964)
XLA Ops:
  0.0 1.5 %project.1 = (bf16[32,32,128]{2,1,0:T(8,128)(2,1)S(1)}, bf16[512,128]{1,0:T(8,128)(2,1)S(1)}, bf16[128,128]{1,0:T(8,128)(2,1)S(1)}, f32[1,128]{1,0:T(1,128)S(1)}...) custom-call(bf16[4,128,128]{2,1,0:T(8,128)(2,1)} %pair_hbm.1, s32[1,128]{1,0:T(1,128)} %bitcast.5, f32[1,128]{1,0:T(1,128)} %bitcast.6, ...), custom_call_target="tpu_custom_call" | custom-call | tf_op jit(solution)/shard_map/project/pallas_call | solution.py:172
  1.6 17.0 %all_to_all.10.blocks_ref = bf16[32,32,128]{2,1,0:T(8,128)(2,1)S(1)} all-to-all(bf16[32,32,128]{2,1,0:T(8,128)(2,1)S(1)} %get-tuple-element.14), channel_id=1, replica_groups={{31,30,29,28,27,26,25,24,23,22,21,20,19,18,17,16,15,14,13,12,11,10,9,8,..., dimensions={0} | all-to-all | bytes 524288 | tf_op jit(solution)/shard_map/all_to_all | solution.py:108
  18.6 0.3 contract.1
  18.9 10.6 %all_to_all.11.blocks_ref = bf16[32,16,128]{2,1,0:T(8,128)(2,1)S(1)} all-to-all(bf16[32,16,128]{2,1,0:T(8,128)(2,1)S(1)} %get-tuple-element.19), channel_id=1, replica_groups={{5,4,13,12,21,20,29,28,31,30,23,22,15,14,7,6,3,2,11,10,19,18,27,26,25,2..., dimensions={0} | all-to-all | bytes 262144 | tf_op jit(solution)/shard_map/all_to_all | solution.py:108
  29.5 1.0 %finish.1 = bf16[4,128,128]{2,1,0:T(8,128)(2,1)} custom-call(bf16[32,16,128]{2,1,0:T(8,128)(2,1)S(1)} %all_to_all.11.blocks_ref, bf16[512,128]{1,0:T(8,128)(2,1)S(1)} %get-tuple-element.20.gate_ref, f32[2,128,128]{2,1,0:T(8,128)S(1)} %get-tuple-element.21.scales_ref, bf16[128,128]{1,0:T(8,128)(2,1)S(1)} %get-tuple-element.22.w_ref), custom_call_target="tpu_custom_call" | custom-call | tf_op jit(solution)/shard_map/finish/pallas_call | solution.py:209

commit v25 on v14

--- a/solution.py
+++ b/solution.py
@@ -130,14 +130,17 @@
 def finish_kernel(blocks_ref, gate_ref, scales_ref, w_ref, out_ref, held_ref):
     row_count, col_count, chan_count = out_ref.shape
     receive_blocks(blocks_ref, held_ref)
-    for r in range(row_count):
-        triangle = held_ref[pl.ds(r, chan_count, stride=row_count), :]
-        normed = layer_norm(triangle, scales_ref[0], scales_ref[1], 0).astype(jnp.bfloat16)
-        result = lax.dot_general(
-            normed, w_ref[...], (((0,), (0,)), ((), ())), preferred_element_type=jnp.float32
-        )
-        gate = gate_ref[r * col_count : (r + 1) * col_count, :].astype(jnp.float32)
-        out_ref[r] = (gate * result).astype(jnp.bfloat16)
+    rows = range(row_count)
+    triangle = jnp.concatenate(
+        [held_ref[pl.ds(r, chan_count, stride=row_count), :] for r in rows], axis=1
+    )
+    gain, bias = (jnp.concatenate([scales_ref[i] for r in rows], axis=1) for i in range(2))
+    normed = layer_norm(triangle, gain, bias, 0).astype(jnp.bfloat16)
+    result = lax.dot_general(
+        normed, w_ref[...], (((0,), (0,)), ((), ())), preferred_element_type=jnp.float32
+    )
+    update = (gate_ref[...].astype(jnp.float32) * result).astype(jnp.bfloat16)
+    out_ref[...] = update.reshape(out_ref.shape)
 
 
 def local_blocks(pair, valid, norm_gain, norm_bias, w_proj, out_gain, out_bias, w_out):

time: 30.9 us -> 30.9 us (level)
  no operation moved by 1% of the time
where the time goes in v25:
time: 30.9 us; the launch traced here: 30.6 us
  blocking collectives  27.8 us (90%)
  Pallas kernels  2.79 us (9%)
    all_to_all x2, blocking collectives, exchange(): lax.all_to_all(blocks, axes, split_axis=0, concat_axis=0, axis_index_grou...  27.8 us
    pallas_call x1, Pallas kernels, local_blocks(): pl.pallas_call(project_kernel, out_shape=(shaped(shards, 8 * row_count, c...  1.55 us
    pallas_call x1, Pallas kernels, local_blocks(): pl.pallas_call(finish_kernel, out_shape=shaped(row_count, col_count, chan...  0.97 us

profile of v25, /device:TPU:0, one launch (start us, length us, event | category | flops | bytes accessed | tf_op | source)
XLA Modules:
  0.0 30.6 jit_solution(17832177534113726921)
XLA Ops:
  0.0 1.5 %project.1 = (bf16[32,32,128]{2,1,0:T(8,128)(2,1)S(1)}, bf16[512,128]{1,0:T(8,128)(2,1)S(1)}, bf16[128,128]{1,0:T(8,128)(2,1)S(1)}, f32[1,128]{1,0:T(1,128)S(1)}...) custom-call(bf16[4,128,128]{2,1,0:T(8,128)(2,1)} %pair_hbm.1, s32[1,128]{1,0:T(1,128)} %bitcast.5, f32[1,128]{1,0:T(1,128)} %bitcast.6, ...), custom_call_target="tpu_custom_call" | custom-call | tf_op jit(solution)/shard_map/project/pallas_call | solution.py:165
  1.6 17.0 %all_to_all.10.blocks_ref = bf16[32,32,128]{2,1,0:T(8,128)(2,1)S(1)} all-to-all(bf16[32,32,128]{2,1,0:T(8,128)(2,1)S(1)} %get-tuple-element.14), channel_id=1, replica_groups={{31,30,29,28,27,26,25,24,23,22,21,20,19,18,17,16,15,14,13,12,11,10,9,8,..., dimensions={0} | all-to-all | bytes 524288 | tf_op jit(solution)/shard_map/all_to_all | solution.py:98
  18.6 0.3 contract.1
  18.9 10.8 %all_to_all.11.blocks_ref = bf16[32,16,128]{2,1,0:T(8,128)(2,1)S(1)} all-to-all(bf16[32,16,128]{2,1,0:T(8,128)(2,1)S(1)} %get-tuple-element.19), channel_id=1, replica_groups={{31,30,29,28,27,26,25,24,23,22,21,20,19,18,17,16,15,14,13,12,11,10,9,8,..., dimensions={0} | all-to-all | bytes 262144 | tf_op jit(solution)/shard_map/all_to_all | solution.py:98
  29.7 1.0 %finish.1 = bf16[4,128,128]{2,1,0:T(8,128)(2,1)} custom-call(bf16[32,16,128]{2,1,0:T(8,128)(2,1)S(1)} %all_to_all.11.blocks_ref, bf16[512,128]{1,0:T(8,128)(2,1)S(1)} %get-tuple-element.20.gate_ref, f32[2,128,128]{2,1,0:T(8,128)S(1)} %get-tuple-element.21.scales_ref, bf16[128,128]{1,0:T(8,128)(2,1)S(1)} %get-tuple-element.22.w_ref), custom_call_target="tpu_custom_call" | custom-call | tf_op jit(solution)/shard_map/finish/pallas_call | solution.py:202

commit v26 on v14

--- a/solution.py
+++ b/solution.py
@@ -52,8 +52,8 @@
     fetches = [
         pltpu.make_async_copy(source, held, sems.at[i]) for i, (source, held) in enumerate(pairs)
     ]
-    for fetch in fetches:
-        fetch.start()
+    for i, fetch in enumerate(fetches):
+        fetch.start(priority=i % 2)
     row_start = lax.axis_index(axes) * row_count
     for fetch in fetches[:needed]:
         fetch.wait()

time: 30.9 us -> 30.9 us (level)
  no operation moved by 1% of the time
where the time goes in v26:
time: 30.9 us; the launch traced here: 30.7 us
  blocking collectives  27.8 us (90%)
  Pallas kernels  2.82 us (9%)
    all_to_all x2, blocking collectives, exchange(): lax.all_to_all(blocks, axes, split_axis=0, concat_axis=0, axis_index_grou...  27.8 us
    pallas_call x1, Pallas kernels, local_blocks(): pl.pallas_call(project_kernel, out_shape=(shaped(shards, 8 * row_count, c...  1.57 us
    pallas_call x1, Pallas kernels, local_blocks(): pl.pallas_call(finish_kernel, out_shape=shaped(row_count, col_count, chan...  0.97 us

profile of v26, /device:TPU:0, one launch (start us, length us, event | category | flops | bytes accessed | tf_op | source)
XLA Modules:
  0.0 30.7 jit_solution(3951683871244213375)
XLA Ops:
  0.0 1.6 %project.1 = (bf16[32,32,128]{2,1,0:T(8,128)(2,1)S(1)}, bf16[512,128]{1,0:T(8,128)(2,1)S(1)}, bf16[128,128]{1,0:T(8,128)(2,1)S(1)}, f32[1,128]{1,0:T(1,128)S(1)}...) custom-call(bf16[4,128,128]{2,1,0:T(8,128)(2,1)} %pair_hbm.1, s32[1,128]{1,0:T(1,128)} %bitcast.5, f32[1,128]{1,0:T(1,128)} %bitcast.6, ...), custom_call_target="tpu_custom_call" | custom-call | tf_op jit(solution)/shard_map/project/pallas_call | solution.py:162
  1.6 17.0 %all_to_all.10.blocks_ref = bf16[32,32,128]{2,1,0:T(8,128)(2,1)S(1)} all-to-all(bf16[32,32,128]{2,1,0:T(8,128)(2,1)S(1)} %get-tuple-element.14), channel_id=1, replica_groups={{31,30,29,28,27,26,25,24,23,22,21,20,19,18,17,16,15,14,13,12,11,10,9,8,..., dimensions={0} | all-to-all | bytes 524288 | tf_op jit(solution)/shard_map/all_to_all | solution.py:98
  18.6 0.3 contract.1
  18.9 10.8 %all_to_all.11.blocks_ref = bf16[32,16,128]{2,1,0:T(8,128)(2,1)S(1)} all-to-all(bf16[32,16,128]{2,1,0:T(8,128)(2,1)S(1)} %get-tuple-element.19), channel_id=1, replica_groups={{31,30,29,28,27,26,25,24,23,22,21,20,19,18,17,16,15,14,13,12,11,10,9,8,..., dimensions={0} | all-to-all | bytes 262144 | tf_op jit(solution)/shard_map/all_to_all | solution.py:98
  29.7 1.0 %finish.1 = bf16[4,128,128]{2,1,0:T(8,128)(2,1)} custom-call(bf16[32,16,128]{2,1,0:T(8,128)(2,1)S(1)} %all_to_all.11.blocks_ref, bf16[512,128]{1,0:T(8,128)(2,1)S(1)} %get-tuple-element.20.gate_ref, f32[2,128,128]{2,1,0:T(8,128)S(1)} %get-tuple-element.21.scales_ref, bf16[128,128]{1,0:T(8,128)(2,1)S(1)} %get-tuple-element.22.w_ref), custom_call_target="tpu_custom_call" | custom-call | tf_op jit(solution)/shard_map/finish/pallas_call | solution.py:199

commit v27 on v14

--- a/solution.py
+++ b/solution.py
@@ -38,16 +38,15 @@
     pair_ref, valid_ref, gain_ref, bias_ref, w_ref, sems,
 ):
     row_count, col_count, chan_count = pair_ref.shape
-    quarter = chan_count // 4
+    half_rows = chan_count // 2
     pairs = [(pair_hbm.at[r], pair_ref.at[r]) for r in range(row_count)]
-    for i in range(0, chan_count, quarter):
-        rows = pl.ds(i, quarter)
-        pairs.append((w_hbm.at[rows, : 4 * chan_count], w_ref.at[rows]))
+    for i in range(0, chan_count, half_rows):
+        rows = pl.ds(i, half_rows)
+        pairs.append((w_hbm.at[rows], w_ref.at[rows]))
     pairs += [(gain_hbm, gain_ref), (bias_hbm, bias_ref), (valid_hbm, valid_ref)]
     needed = len(pairs)
     pairs += [
-        (w_hbm.at[:, 4 * chan_count :], w_gate_ref), (out_gain_hbm, out_gain_ref),
-        (out_bias_hbm, out_bias_ref), (w_out_hbm, w_out_ref),
+        (out_gain_hbm, out_gain_ref), (out_bias_hbm, out_bias_ref), (w_out_hbm, w_out_ref),
     ]
     fetches = [
         pltpu.make_async_copy(source, held, sems.at[i]) for i, (source, held) in enumerate(pairs)
@@ -60,8 +59,9 @@
     tokens = pair_ref[...].reshape(row_count * col_count, chan_count).astype(jnp.float32)
     normed = layer_norm(tokens, gain_ref[...], bias_ref[...], 1).astype(jnp.bfloat16)
     normed_ref[...] = normed
+    w_gate_ref[...] = w_ref[:, 4 * chan_count :]
     projected = lax.dot_general(
-        w_ref[...], normed, (((0,), (1,)), ((), ())),
+        w_ref[:, : 4 * chan_count], normed, (((0,), (1,)), ((), ())),
         preferred_element_type=jnp.float32,
     )
     col_flags = valid_ref[...].astype(jnp.float32)
@@ -172,8 +172,8 @@
             pltpu.VMEM((1, col_count), jnp.int32),
             pltpu.VMEM((1, chan_count), jnp.float32),
             pltpu.VMEM((1, chan_count), jnp.float32),
-            pltpu.VMEM((chan_count, 4 * chan_count), jnp.bfloat16),
-            pltpu.SemaphoreType.DMA((row_count + 11,)),
+            pltpu.VMEM(w_proj.shape, jnp.bfloat16),
+            pltpu.SemaphoreType.DMA((row_count + 8,)),
         ],
         compiler_params=limit,
         name="project",

time: 30.9 us -> 30.9 us (level)
  no operation moved by 1% of the time
where the time goes in v27:
time: 30.9 us; the launch traced here: 30.8 us
  blocking collectives  27.8 us (90%)
  Pallas kernels  2.91 us (9%)
    all_to_all x2, blocking collectives, exchange(): lax.all_to_all(blocks, axes, split_axis=0, concat_axis=0, axis_index_grou...  27.8 us
    pallas_call x1, Pallas kernels, local_blocks(): pl.pallas_call(project_kernel, out_shape=(shaped(shards, 8 * row_count, c...  1.66 us
    pallas_call x1, Pallas kernels, local_blocks(): pl.pallas_call(finish_kernel, out_shape=shaped(row_count, col_count, chan...  0.98 us

profile of v27, /device:TPU:0, one launch (start us, length us, event | category | flops | bytes accessed | tf_op | source)
XLA Modules:
  0.0 30.8 jit_solution(16311480662911412964)
XLA Ops:
  0.0 1.7 %project.1 = (bf16[32,32,128]{2,1,0:T(8,128)(2,1)S(1)}, bf16[512,128]{1,0:T(8,128)(2,1)S(1)}, bf16[128,128]{1,0:T(8,128)(2,1)S(1)}, f32[1,128]{1,0:T(1,128)S(1)}...) custom-call(bf16[4,128,128]{2,1,0:T(8,128)(2,1)} %pair_hbm.1, s32[1,128]{1,0:T(1,128)} %bitcast.5, f32[1,128]{1,0:T(1,128)} %bitcast.6, ...), custom_call_target="tpu_custom_call" | custom-call | tf_op jit(solution)/shard_map/project/pallas_call | solution.py:162
  1.7 17.0 %all_to_all.10.blocks_ref = bf16[32,32,128]{2,1,0:T(8,128)(2,1)S(1)} all-to-all(bf16[32,32,128]{2,1,0:T(8,128)(2,1)S(1)} %get-tuple-element.14), channel_id=1, replica_groups={{31,30,29,28,27,26,25,24,23,22,21,20,19,18,17,16,15,14,13,12,11,10,9,8,..., dimensions={0} | all-to-all | bytes 524288 | tf_op jit(solution)/shard_map/all_to_all | solution.py:98
  18.7 0.3 contract.1
  19.0 10.8 %all_to_all.11.blocks_ref = bf16[32,16,128]{2,1,0:T(8,128)(2,1)S(1)} all-to-all(bf16[32,16,128]{2,1,0:T(8,128)(2,1)S(1)} %get-tuple-element.19), channel_id=1, replica_groups={{31,30,29,28,27,26,25,24,23,22,21,20,19,18,17,16,15,14,13,12,11,10,9,8,..., dimensions={0} | all-to-all | bytes 262144 | tf_op jit(solution)/shard_map/all_to_all | solution.py:98
  29.8 1.0 %finish.1 = bf16[4,128,128]{2,1,0:T(8,128)(2,1)} custom-call(bf16[32,16,128]{2,1,0:T(8,128)(2,1)S(1)} %all_to_all.11.blocks_ref, bf16[512,128]{1,0:T(8,128)(2,1)S(1)} %get-tuple-element.20.gate_ref, f32[2,128,128]{2,1,0:T(8,128)S(1)} %get-tuple-element.21.scales_ref, bf16[128,128]{1,0:T(8,128)(2,1)S(1)} %get-tuple-element.22.w_ref), custom_call_target="tpu_custom_call" | custom-call | tf_op jit(solution)/shard_map/finish/pallas_call | solution.py:199
